TPU v7x, 32 devices: a whole 2x2x4 slice. The times are simulated.
32 devices in a mesh: dp: 2 (over x), expert: 16 (over z, y, core).
Axes of the slice: x: 2, y: 2, z: 4, core: 2. Of those that a mesh axis runs over, the one named last changes fastest.
Arguments:
- tokens: bfloat16 [4096, 3584], P(('dp', 'expert')), may hold values from -6 to 6
- out_grad: bfloat16 [4096, 3584], P(('dp', 'expert')), may hold values from -1.1953125 to 1.1953125
- gate_weight: bfloat16 [3584, 8192], P('dp', 'expert'), may hold values from -0.09375 to 0.09375
- up_weight: bfloat16 [3584, 8192], P('dp', 'expert'), may hold values from -0.09375 to 0.09375
- route_ids: int32 [4096, 8], P(('dp', 'expert')), may hold values from 0 to 255, all different within a row; in each aligned block of 128 rows (0 to 127, 128 to 255, ...) at most 6 rows name the same one
- route_weights: float32 [4096, 8], P(('dp', 'expert')), may hold values from 0.02 to 0.5
Outputs:
- grad_down: bfloat16 [8192, 3584], P(('expert', 'dp'))
Inputs may be any that keep to these rules, and one draw needn't show every extreme that they name: `route_ids`: each row names 8 different experts. At most 6 of the rows of one device name any one expert, a bound that some block reaches.
All inputs are finite; a program needn't handle non-finite values.
Results may differ from a plain program's by a relative error of at most 0.015.
Values may be sent and summed in bfloat16 or wider, within the bound.
No kernel may reach another device: no remote copies, remote signals or barrier semaphores. Data moves between devices by JAX's collectives and lax.ppermute only.
A program may use at most 128 MiB of HBM per device.

v0:
```python
import jax
import jax.numpy as jnp
from jax import lax
from jax.sharding import PartitionSpec as P

N_ROUTED = 256
LOG_SPLIT = 2


def pack_rows(tokens, out_grad, route_ids, route_weights, experts, row_cap):
    expert_ids = jnp.arange(experts, dtype=jnp.int32)
    matches = route_ids[:, :, None] == expert_ids[None, None, :]
    chosen = jnp.any(matches, axis=1)
    scales = jnp.sum(jnp.where(matches, route_weights[:, :, None], 0.0), axis=1)
    order_rank = jnp.cumsum(chosen.astype(jnp.int32), axis=0) - 1
    slot_ids = jnp.arange(row_cap, dtype=jnp.int32)
    pick_table = chosen.T[:, None, :] & (order_rank.T[:, None, :] == slot_ids[None, :, None])
    pick_flat = pick_table.reshape(experts * row_cap, tokens.shape[0])
    pick_values = pick_flat.astype(jnp.bfloat16)
    sent_rows = jnp.dot(pick_values, tokens, preferred_element_type=jnp.float32).astype(
        jnp.bfloat16
    )
    picked_grads = jnp.dot(pick_values, out_grad, preferred_element_type=jnp.float32)
    slot_scales = jnp.sum(jnp.where(pick_table, scales.T[:, None, :], 0.0), axis=2).reshape(
        experts * row_cap, 1
    )
    scaled = (picked_grads * slot_scales).astype(jnp.bfloat16)
    counts = jnp.sum(chosen.astype(jnp.int32), axis=0)
    return (jnp.stack([sent_rows, scaled]), counts)


def per_device(tokens, out_grad, gate_weight, up_weight, route_ids, route_weights):
    split_count = 2**LOG_SPLIT
    experts = lax.axis_size("expert") // split_count
    feature_count = tokens.shape[1]
    row_cap = max(2, tokens.shape[0] * route_ids.shape[1] * 3 // (2 * N_ROUTED))
    paired, counts = pack_rows(tokens, out_grad, route_ids, route_weights, experts, row_cap)
    spread = jnp.broadcast_to(
        paired.reshape(2, experts, 1, row_cap, feature_count),
        (2, experts, split_count, row_cap, feature_count),
    )
    spread = spread.reshape(2, experts * split_count * row_cap, feature_count)
    received = lax.all_to_all(spread, "expert", split_axis=1, concat_axis=1, tiled=True)
    rows_x = received[0]
    rows_dy = received[1]
    columns = rows_x
    gate_pre = jnp.dot(
        columns,
        lax.all_gather(gate_weight, "dp", axis=0, tiled=True),
        preferred_element_type=jnp.float32,
    )
    up_pre = jnp.dot(
        columns,
        lax.all_gather(up_weight, "dp", axis=0, tiled=True),
        preferred_element_type=jnp.float32,
    )
    hidden = (jax.nn.silu(gate_pre) * up_pre).astype(jnp.bfloat16)
    columns = hidden
    return lax.psum_scatter(
        lax.dot_general(
            columns, rows_dy, (((0,), (0,)), ((), ())), preferred_element_type=jnp.float32
        ).astype(jnp.bfloat16),
        "dp",
        scatter_dimension=0,
        tiled=True,
    )


def solution(mesh):
    return jax.shard_map(
        per_device,
        mesh=mesh,
        in_specs=(
            P(("dp", "expert"), None),
            P(("dp", "expert"), None),
            P("dp", "expert"),
            P("dp", "expert"),
            P(("dp", "expert"), None),
            P(("dp", "expert"), None),
        ),
        out_specs=P(("expert", "dp"), None),
        check_vma=False,
    )
```

profile of v0, /device:TPU:0, one launch (start us, length us, event | category | flops | bytes accessed | tf_op | source)
XLA Modules:
  0.0 176.8 jit_solution(13550303568389695714)
XLA Ops:
  6.5 0.0 copy-start
  6.5 0.0 all-gather.3.cloned.1.call-start
  6.5 0.0 copy-start.2
  6.6 0.7 all-gather.3.cloned.1.call-update
  7.3 0.0 copy-done.3
  7.3 0.1 copy.21
  7.5 0.2 reduce_window_sum.11
  7.6 0.1 copy.22
  7.8 0.1 eq.43
  7.9 0.1 select_reduce_fusion
  8.0 0.1 mul.17
  8.0 0.1 compare_and_fusion
  8.1 0.2 fusion
  8.4 0.1 stack.10
  8.4 0.0 copy-done.2
  8.4 0.2 convolution_convert_fusion.1
  8.7 0.1 stack.9
  8.7 0.1 maximum_bitcast_fusion
  8.9 0.4 copy.23
  9.2 1.8 %broadcast_in_dim.43 = bf16[2,4,4,6,3584]{4,0,3,2,1:T(2,128)(2,1)} broadcast(bf16[2,4,6,3584]{3,0,2,1:T(2,128)(2,1)S(1)} %copy.23), dimensions={0,1,3,4} | broadcast | bytes 1720320 | tf_op jit(solution)/shard_map/broadcast_in_dim | solution.py:38
  11.0 7.4 %all-to-all-start = ((bf16[2,96,3584]{2,0,1:T(2,128)(2,1)}), bf16[2,96,3584]{2,0,1:T(2,128)(2,1)S(1)}, u32[]{:S(2)}, u32[]{:S(2)}) async-start(bf16[2,96,3584]{2,0,1:T(2,128)(2,1)} %bitcast.22), calls=%async_computation | async-start | bytes 2752512 | tf_op jit(solution)/shard_map/all_to_all | solution.py:43
  18.4 0.0 all-gather.5.cloned.1.call-start
  18.5 0.7 all-gather.5.cloned.1.call-update
  19.2 0.0 reduce-scatter.2.cloned.1.call-start
  19.2 27.8 %all-to-all-done = bf16[2,96,3584]{2,0,1:T(2,128)(2,1)S(1)} async-done(((bf16[2,96,3584]{2,0,1:T(2,128)(2,1)}), bf16[2,96,3584]{2,0,1:T(2,128)(2,1)S(1)}, u32[]{:S(2)}, u32[]{:S(2)}) %all-to-all-start) | async-done | bytes 1376288 | tf_op jit(solution)/shard_map/all_to_all | solution.py:43
  47.0 3.5 %fusion.20 = (bf16[1,96,3584]{2,0,1:T(2,128)(2,1)}, bf16[1,96,3584]{2,0,1:T(2,128)(2,1)}) fusion(bf16[2,96,3584]{2,0,1:T(2,128)(2,1)S(1)} %all-to-all-done), kind=kLoop, calls=%fused_computation.29 | loop fusion | bytes 2752512 | tf_op jit(solution)/shard_map/slice | solution.py:44
  50.5 12.0 %all-gather.3.cloned.1.call-done = bf16[3584,512]{1,0:T(8,128)(2,1)} async-done(((bf16[1792,512]{1,0:T(8,128)(2,1)}), bf16[3584,512]{1,0:T(8,128)(2,1)}) %all-gather.3.cloned.1.call-update) | async-done | bytes 3670032 | tf_op jit(solution)/shard_map/all_gather | solution.py:49
  62.5 3.3 %fusion.6 = f32[96,512]{1,0:T(8,128)S(1)} fusion(bf16[3584,512]{1,0:T(8,128)(2,1)} %all-gather.3.cloned.1.call-done, bf16[1,96,3584]{2,0,1:T(2,128)(2,1)} %get-tuple-element.5), kind=kOutput, calls=%fused_computation.9 | convolution fusion | flops 352321536 | bytes 4554752 | tf_op jit(solution)/shard_map/dot_general | solution.py:47
  65.8 49.1 %all-gather.5.cloned.1.call-done = bf16[3584,512]{1,0:T(8,128)(2,1)} async-done(((bf16[1792,512]{1,0:T(8,128)(2,1)}), bf16[3584,512]{1,0:T(8,128)(2,1)}) %all-gather.5.cloned.1.call-update) | async-done | bytes 3670032 | tf_op jit(solution)/shard_map/all_gather | solution.py:54
  114.9 6.1 %convolution_convert_fusion = bf16[512,3584]{1,0:T(8,128)(2,1)} fusion(bf16[3584,512]{1,0:T(8,128)(2,1)} %all-gather.5.cloned.1.call-done, bf16[1,96,3584]{2,0,1:T(2,128)(2,1)} %get-tuple-element.6, bf16[1,96,3584]{2,0,1:T(2,128)(2,1)S(1)} %copy-done.1, f32[96,512]{1,0:T(8,128)S(1)} %fusion.6), kind=kOutput, calls=%fused_computation | convolution fusion | flops 706772992 | bytes 8912896 | tf_op jit(solution)/shard_map/dot_general | solution.py:60
  121.0 0.0 reduce-scatter.2.cloned.1.call-update
  121.1 49.3 %reduce-scatter.2.cloned.1.call-done = bf16[256,3584]{1,0:T(8,128)(2,1)} async-done(((bf16[512,3584]{1,0:T(8,128)(2,1)}), bf16[256,3584]{1,0:T(8,128)(2,1)}) %reduce-scatter.2.cloned.1.call-update) | async-done | bytes 1835024 | tf_op jit(solution)/shard_map/reduce_scatter | solution.py:59
  (15 shorter events, 0.1 us)
Async XLA Ops:
  6.5 1.6 copy-start
  6.5 0.8 copy-start.3
  6.5 1.3 copy-start.4
  6.5 55.9 %all-gather.3.cloned.1.call-start = ((), (), s32[]{:S(2)}) async-start(), calls=%async_computation.2 | async-start | bytes 5505024 | tf_op jit(solution)/shard_map/all_gather | solution.py:49
  6.5 1.9 %copy-start.2 = (bf16[128,3584]{1,0:T(8,128)(2,1)S(1)}, bf16[128,3584]{1,0:T(8,128)(2,1)}, u32[]{:S(2)}) copy-start(bf16[128,3584]{1,0:T(8,128)(2,1)} %param.6) | copy-start | bytes 2752516
  11.0 35.9 %all-to-all-start = ((bf16[2,96,3584]{2,0,1:T(2,128)(2,1)}), bf16[2,96,3584]{2,0,1:T(2,128)(2,1)S(1)}, u32[]{:S(2)}, u32[]{:S(2)}) async-start(bf16[2,96,3584]{2,0,1:T(2,128)(2,1)} %bitcast.22), calls=%async_computation | async-start | bytes 2752512 | tf_op jit(solution)/shard_map/all_to_all | solution.py:43
  18.4 96.5 %all-gather.5.cloned.1.call-start = ((), (), s32[]{:S(2)}) async-start(), calls=%async_computation.3 | async-start | bytes 5505024 | tf_op jit(solution)/shard_map/all_gather | solution.py:54
  19.2 151.2 %reduce-scatter.2.cloned.1.call-start = ((), (), s32[]{:S(2)}) async-start(), calls=%async_computation.4 | async-start | bytes 5505024 | tf_op jit(solution)/shard_map/reduce_scatter | solution.py:59
  62.5 52.4 %copy-start.1 = (bf16[1,96,3584]{2,0,1:T(2,128)(2,1)S(1)}, bf16[1,96,3584]{2,0,1:T(2,128)(2,1)}, u32[]{:S(2)}) copy-start(bf16[1,96,3584]{2,0,1:T(2,128)(2,1)} %get-tuple-element.5) | copy-start | bytes 2064388
Sparse Core Ops, SparseCore 0:
  8.9 53.5 all-gather.2
  64.0 50.8 all-gather.4
  121.2 49.0 reduce-scatter.1
where the time goes:
time: 177 us
  waiting for transfers between devices  140 us (79%)
  between operations  13.2 us (7%)
  matrix products  9.85 us (6%)
  starting transfers between devices  7.47 us (4%)
  local copies, waits for them, and re-layouts  6.23 us (4%)
    reduce_scatter x1, waiting for transfers between devices, per_device(): lax.psum_scatter(lax.dot_general(columns, rows_dy, (((0,), (0,)), ((), ()...  49.3 us
    all_gather x1, waiting for transfers between devices, per_device(): lax.all_gather(up_weight, 'dp', axis=0, tiled=True)  49.1 us
    all_to_all x1, waiting for transfers between devices, per_device(): lax.all_to_all(spread, 'expert', split_axis=1, concat_axis=1, tiled=True)  27.8 us
    all_gather x1, waiting for transfers between devices, per_device(): lax.all_gather(gate_weight, 'dp', axis=0, tiled=True)  12 us
    all_to_all x1, starting transfers between devices, per_device(): lax.all_to_all(spread, 'expert', split_axis=1, concat_axis=1, tiled=True)  7.39 us
    dot_general x1, matrix products, per_device(): lax.dot_general(columns, rows_dy, (((0,), (0,)), ((), ())), preferred_ele...  6.13 us
  transfers between devices with their start and end apart: 4, of which 4 were waited for; matrix products, arithmetic and copies ran while one was open for 6% of the time, Pallas kernels for 0%

commit v1 on v0

v1 whole, which is shorter than its diff:
```python
import jax
import jax.numpy as jnp
from jax import lax
from jax.sharding import PartitionSpec as P

N_ROUTED = 256
SPLIT = 4
AXES = ("dp", "expert")


def pack_rows(tokens, out_grad, route_ids, route_weights, experts, row_cap):
    expert_ids = jnp.arange(experts, dtype=jnp.int32)
    matches = route_ids[:, :, None] == expert_ids[None, None, :]
    chosen = jnp.any(matches, axis=1)
    scales = jnp.sum(jnp.where(matches, route_weights[:, :, None], 0.0), axis=1)
    rank = jnp.cumsum(chosen.astype(jnp.int32), axis=0) - 1
    slots = jnp.arange(row_cap, dtype=jnp.int32)
    pick = chosen.T[:, None, :] & (rank.T[:, None, :] == slots[None, :, None])
    flat = pick.reshape(experts * row_cap, tokens.shape[0]).astype(jnp.bfloat16)
    rows = jnp.dot(flat, tokens, preferred_element_type=jnp.float32).astype(jnp.bfloat16)
    grads = jnp.dot(flat, out_grad, preferred_element_type=jnp.float32)
    slot_scales = jnp.sum(jnp.where(pick, scales.T[:, None, :], 0.0), axis=2)
    scaled = (grads * slot_scales.reshape(experts * row_cap, 1)).astype(jnp.bfloat16)
    return rows, scaled


def per_device(tokens, out_grad, gate_weight, up_weight, route_ids, route_weights):
    n_dp, n_expert = lax.axis_size("dp"), lax.axis_size("expert")
    experts = n_expert // SPLIT
    features = tokens.shape[1]
    depth = gate_weight.shape[0]
    units = gate_weight.shape[1]
    own_units = units // n_dp
    cap = max(2, tokens.shape[0] * route_ids.shape[1] * 3 // (2 * N_ROUTED))
    me_d, me_s = lax.axis_index("dp"), lax.axis_index("expert")
    me_e = me_s // SPLIT

    def send(value, by_d, by_e, by_q):
        pairs = []
        for d in range(n_dp):
            for s in range(n_expert):
                e, q = s // SPLIT, s % SPLIT
                to = ((e + by_e) % experts) * SPLIT + (q ^ by_q)
                pairs.append((d * n_expert + s, (d + by_d) % n_dp * n_expert + to))
        return lax.ppermute(value, AXES, pairs)

    rows, scaled = pack_rows(tokens, out_grad, route_ids, route_weights, experts, cap)
    both = jnp.concatenate(
        [rows.reshape(experts, cap, features), scaled.reshape(experts, cap, features)], axis=2
    )

    def block_for(by_e):
        to = (me_e + by_e) % experts
        return lax.dynamic_index_in_dim(both, to, 0, keepdims=False)

    parts = [block_for(0)] + [send(block_for(k), 0, k, 0) for k in range(1, experts)]
    held = jnp.concatenate(parts, axis=0)
    held_x, held_dy = held[:, :features], held[:, features:]

    def x_for(by_d):
        return lax.dynamic_slice_in_dim(held_x, (me_d + by_d) % n_dp * depth, depth, 1)

    x_blocks, dy_blocks = [], []
    for by_d in range(n_dp):
        x_part = x_for(by_d)
        for by_q in range(0, SPLIT, 2):
            x_got = x_part if by_d == by_q == 0 else send(x_part, by_d, 0, by_q)
            x_blocks += [x_got, send(x_got, 0, 0, 1)]
    for by_d in range(n_dp):
        for by_q in range(0, SPLIT, 2):
            dy_got = held_dy if by_d == by_q == 0 else send(held_dy, by_d, 0, by_q)
            dy_blocks += [dy_got, send(dy_got, 0, 0, 1)]
    x_all = jnp.concatenate(x_blocks, axis=0)
    dy_all = jnp.concatenate(dy_blocks, axis=0)

    group_rows = SPLIT * held.shape[0]

    def partial_pre(by_d):
        at = (me_d + by_d) % n_dp * own_units
        gate = lax.dynamic_slice_in_dim(gate_weight, at, own_units, 1)
        up = lax.dynamic_slice_in_dim(up_weight, at, own_units, 1)
        weight = jnp.concatenate([gate, up], axis=1)
        return jnp.dot(x_all, weight, preferred_element_type=jnp.float32)

    arrived = []
    for by_d in range(1, n_dp):
        ready = jnp.roll(partial_pre(by_d), by_d * group_rows, axis=0).astype(jnp.bfloat16)
        arrived.append(send(ready, by_d, 0, 0))
    total = partial_pre(0)
    for other in arrived:
        total = total + other.astype(jnp.float32)
    gate_pre, up_pre = total[:, :own_units], total[:, own_units:]
    hidden = (jax.nn.silu(gate_pre) * up_pre).astype(jnp.bfloat16)
    return lax.dot_general(
        hidden, dy_all, (((0,), (0,)), ((), ())), preferred_element_type=jnp.float32
    ).astype(jnp.bfloat16)


def solution(mesh):
    return jax.shard_map(
        per_device,
        mesh=mesh,
        in_specs=(
            P(("dp", "expert"), None),
            P(("dp", "expert"), None),
            P("dp", "expert"),
            P("dp", "expert"),
            P(("dp", "expert"), None),
            P(("dp", "expert"), None),
        ),
        out_specs=P(("expert", "dp"), None),
        check_vma=False,
    )
```

time: 177 us -> 52.2 us (0.29)
  waiting for transfers between devices: 140 us -> 25.2 us
  between operations: 13.2 us -> 0.26 us
  starting transfers between devices: 7.47 us -> 17.7 us
  matrix products: 9.85 us -> 3.45 us
  local copies, waits for them, and re-layouts: 6.23 us -> 3.23 us
    all_gather x2 -> x0, waiting for transfers between devices: 61.2 us -> none  [the longest x1 49.1 us: per_device(): lax.all_gather(up_weight, 'dp', axis=0, tiled=True)]
    reduce_scatter x1 -> x0, waiting for transfers between devices: 49.3 us -> none  [per_device(): lax.psum_scatter(lax.dot_general(columns, rows_dy, (((0,), (0,)), ((), ()...]
    all_to_all x1 -> x0, waiting for transfers between devices: 27.8 us -> none  [per_device(): lax.all_to_all(spread, 'expert', split_axis=1, concat_axis=1, tiled=True)]
    ppermute x0 -> x18, waiting for transfers between devices: none -> 25.2 us  [send(): return lax.ppermute(value, AXES, pairs)]
    ppermute x0 -> x18, starting transfers between devices: none -> 17.7 us  [send(): return lax.ppermute(value, AXES, pairs)]
    all_to_all x1 -> x0, starting transfers between devices: 7.39 us -> none  [per_device(): lax.all_to_all(spread, 'expert', split_axis=1, concat_axis=1, tiled=True)]
    dot_general x4 -> x5, matrix products: 9.85 us -> 3.45 us  [the longest x1 1.93 us: per_device(): lax.dot_general(hidden, dy_all, (((0,), (0,)), ((), ())), preferred_eleme...]
    slice x1 -> x2, local copies, waits for them, and re-layouts: 3.5 us -> 0.05 us  [the longest x1 0.04 us: per_device(): held_x, held_dy = (held[:, :features], held[:, features:])]
  transfers between devices with their start and end apart: 4 -> 18, of which waited for: 4 -> 7; matrix products, arithmetic and copies ran while one was open for 6% -> 5% of each run, Pallas kernels for 0% -> 0%
where the time goes in v1:
time: 52.2 us; the launch traced here: 51.9 us
  waiting for transfers between devices  25.2 us (48%)
  starting transfers between devices  17.7 us (34%)
  matrix products  3.45 us (7%)
  local copies, waits for them, and re-layouts  3.23 us (6%)
  other arithmetic  2.12 us (4%)
    ppermute x18, waiting for transfers between devices, send(): return lax.ppermute(value, AXES, pairs)  25.2 us
    ppermute x18, starting transfers between devices, send(): return lax.ppermute(value, AXES, pairs)  17.7 us
    dot_general x1, matrix products, per_device(): lax.dot_general(hidden, dy_all, (((0,), (0,)), ((), ())), preferred_eleme...  1.93 us
    dynamic_slice x1, local copies, waits for them, and re-layouts, partial_pre(): up = lax.dynamic_slice_in_dim(up_weight, at, own_units, 1)  1.75 us
    dot_general x2, matrix products, partial_pre(): return jnp.dot(x_all, weight, preferred_element_type=jnp.float32)  1.06 us
  transfers between devices with their start and end apart: 18, of which 7 were waited for; matrix products, arithmetic and copies ran while one was open for 5% of the time, Pallas kernels for 0%

profile of v1, /device:TPU:0, one launch (start us, length us, event | category | flops | bytes accessed | tf_op | source)
XLA Modules:
  0.0 51.9 jit_solution(4888549997327117624)
XLA Ops:
  0.0 0.8 %fusion.18 = pred[128,4]{0,1:T(4,128)(4,1)S(1)} fusion(s32[128,8]{0,1:T(8,128)} %param.10), kind=kLoop, calls=%fused_computation.46 | loop fusion | flops 7680 | bytes 4608 | tf_op jit(solution)/shard_map/reduce_or | solution.py:14
  0.9 0.7 %select_reduce_fusion.1 = f32[128,4]{0,1:T(4,128)S(1)} fusion(f32[128,8]{0,1:T(8,128)} %param.11, s32[128,8]{0,1:T(8,128)} %param.10), kind=kLoop, calls=%fused_computation.43 | loop fusion | flops 11776 | bytes 10240 | tf_op jit(solution)/shard_map/reduce_sum | solution.py:15
  1.6 0.1 eq.52
  1.7 0.1 copy.15
  1.8 0.2 reduce_window_sum.11
  2.0 0.1 select_reduce_fusion
  2.3 0.2 fusion
  2.6 0.2 convolution_convert_fusion.1
  3.0 0.7 %dynamic-slice_bitcast_fusion.3 = (bf16[6,7168]{1,0:T(8,128)(2,1)S(1)}, bf16[6,7168]{1,0:T(8,128)(2,1)}, bf16[6,7168]{1,0:T(8,128)(2,1)S(1)}, bf16[6,7168]{1,0:T(8,128)(2,1)S(1)}) fusion(bf16[4,6,7168]{2,1,0:T(8,128)(2,1)S(1)} %constant_dynamic-update-slice_fusion, s32[]{:T(128)S(6)} %select_n.74, s32[]{:T(128)S(6)} %select_n.80, s32[]{:T(128)S(6)} %select_n.78, ...), kind=kLoop, calls=%fused_computation.21 | loop fusion | bytes 688144 | tf_op jit(solution)/shard_map/jit(dynamic_index_in_dim)/squeeze | solution.py:54
  3.7 5.0 %collective-permute-start.2 = (bf16[6,7168]{1,0:T(8,128)(2,1)}, bf16[6,7168]{1,0:T(8,128)(2,1)S(1)}, u32[]{:S(2)}, u32[]{:S(2)}) collective-permute-start(bf16[6,7168]{1,0:T(8,128)(2,1)} %get-tuple-element.12), channel_id=1, source_target_pairs={{0,12},{1,13},{2,14},{3,15},{4,0},{5,1},{6,2},{7,3},{8,4},{9,5},{1... | collective-permute-start | bytes 258056 | tf_op jit(solution)/shard_map/ppermute | solution.py:45
  8.8 1.0 %collective-permute-start = (bf16[6,7168]{1,0:T(8,128)(2,1)S(1)}, bf16[6,7168]{1,0:T(8,128)(2,1)S(1)}, u32[]{:S(2)}, u32[]{:S(2)}) collective-permute-start(bf16[6,7168]{1,0:T(8,128)(2,1)S(1)} %get-tuple-element.14), channel_id=1, source_target_pairs={{0,4},{1,5},{2,6},{3,7},{4,8},{5,9},{6,10},{7,11},{8,12},{9,13},{1... | collective-permute-start | bytes 258056 | tf_op jit(solution)/shard_map/ppermute | solution.py:45
  9.8 2.9 %collective-permute-done.2 = bf16[6,7168]{1,0:T(8,128)(2,1)S(1)} collective-permute-done((bf16[6,7168]{1,0:T(8,128)(2,1)}, bf16[6,7168]{1,0:T(8,128)(2,1)S(1)}, u32[]{:S(2)}, u32[]{:S(2)}) %collective-permute-start.2) | collective-permute-done | bytes 86048 | tf_op jit(solution)/shard_map/ppermute | solution.py:45
  12.7 6.2 %collective-permute-done.1 = bf16[6,7168]{1,0:T(8,128)(2,1)S(1)} collective-permute-done((bf16[6,7168]{1,0:T(8,128)(2,1)S(1)}, bf16[6,7168]{1,0:T(8,128)(2,1)S(1)}, u32[]{:S(2)}, u32[]{:S(2)}) %collective-permute-start.1) | collective-permute-done | bytes 86048 | tf_op jit(solution)/shard_map/ppermute | solution.py:45
  18.9 0.2 pad_maximum_fusion
  19.1 1.6 %collective-permute-start.4 = (bf16[24,1792]{1,0:T(8,128)(2,1)S(1)}, bf16[24,1792]{1,0:T(8,128)(2,1)S(1)}, u32[]{:S(2)}, u32[]{:S(2)}) collective-permute-start(bf16[24,1792]{1,0:T(8,128)(2,1)S(1)} %get-tuple-element.6), channel_id=1, source_target_pairs={{0,2},{1,3},{2,0},{3,1},{4,6},{5,7},{6,4},{7,5},{8,10},{9,11},{10,... | collective-permute-start | bytes 258056 | tf_op jit(solution)/shard_map/ppermute | solution.py:45
  20.7 1.8 %constant_dynamic-slice_fusion = (bf16[1792,256]{1,0:T(8,128)(2,1)S(1)}, bf16[1792,256]{1,0:T(8,128)(2,1)S(1)}, bf16[1792,256]{1,0:T(8,128)(2,1)S(1)}, bf16[1792,256]{1,0:T(8,128)(2,1)S(1)}) fusion(bf16[1792,512]{1,0:T(8,128)(2,1)S(1)} %copy-done.1, s32[]{:T(128)S(6)} %select_n.86, s32[]{:T(128)S(6)} %select_n.85, bf16[1792,512]{1,0:T(8,128)(2,1)} %param.8), kind=kLoop, calls=%fused_computation.49 | loop fusion | bytes 7340040 | tf_op jit(solution)/shard_map/dynamic_slice | solution.py:81
  22.5 1.5 %collective-permute-start.16 = (bf16[24,3584]{1,0:T(8,128)(2,1)S(1)}, bf16[24,3584]{1,0:T(8,128)(2,1)S(1)}, u32[]{:S(2)}, u32[]{:S(2)}) collective-permute-start(bf16[24,3584]{1,0:T(8,128)(2,1)S(1)} %get-tuple-element.17), channel_id=1, source_target_pairs={{0,18},{1,19},{2,16},{3,17},{4,22},{5,23},{6,20},{7,21},{8,26},{9,... | collective-permute-start | bytes 516104 | tf_op jit(solution)/shard_map/ppermute | solution.py:45
  23.9 0.6 %collective-permute-start.14 = (bf16[24,3584]{1,0:T(8,128)(2,1)S(1)}, bf16[24,3584]{1,0:T(8,128)(2,1)S(1)}, u32[]{:S(2)}, u32[]{:S(2)}) collective-permute-start(bf16[24,3584]{1,0:T(8,128)(2,1)S(1)} %get-tuple-element.17), channel_id=1, source_target_pairs={{0,16},{1,17},{2,18},{3,19},{4,20},{5,21},{6,22},{7,23},{8,24},{9,... | collective-permute-start | bytes 516104 | tf_op jit(solution)/shard_map/ppermute | solution.py:45
  24.5 1.5 %collective-permute-start.12 = (bf16[24,3584]{1,0:T(8,128)(2,1)S(1)}, bf16[24,3584]{1,0:T(8,128)(2,1)S(1)}, u32[]{:S(2)}, u32[]{:S(2)}) collective-permute-start(bf16[24,3584]{1,0:T(8,128)(2,1)S(1)} %get-tuple-element.17), channel_id=1, source_target_pairs={{0,2},{1,3},{2,0},{3,1},{4,6},{5,7},{6,4},{7,5},{8,10},{9,11},{10,... | collective-permute-start | bytes 516104 | tf_op jit(solution)/shard_map/ppermute | solution.py:45
  26.0 1.4 %collective-permute-start.6 = (bf16[24,1792]{1,0:T(8,128)(2,1)S(1)}, bf16[24,1792]{1,0:T(8,128)(2,1)S(1)}, u32[]{:S(2)}, u32[]{:S(2)}) collective-permute-start(bf16[24,1792]{1,0:T(8,128)(2,1)S(1)} %get-tuple-element.20), channel_id=1, source_target_pairs={{0,16},{1,17},{2,18},{3,19},{4,20},{5,21},{6,22},{7,23},{8,24},{9,... | collective-permute-start | bytes 258056 | tf_op jit(solution)/shard_map/ppermute | solution.py:45
  27.5 7.3 %collective-permute-done.6 = bf16[24,1792]{1,0:T(8,128)(2,1)S(1)} collective-permute-done((bf16[24,1792]{1,0:T(8,128)(2,1)S(1)}, bf16[24,1792]{1,0:T(8,128)(2,1)S(1)}, u32[]{:S(2)}, u32[]{:S(2)}) %collective-permute-start.6) | collective-permute-done | bytes 86048 | tf_op jit(solution)/shard_map/ppermute | solution.py:45
  34.8 2.4 %collective-permute-start.8 = (bf16[24,1792]{1,0:T(8,128)(2,1)S(1)}, bf16[24,1792]{1,0:T(8,128)(2,1)S(1)}, u32[]{:S(2)}, u32[]{:S(2)}) collective-permute-start(bf16[24,1792]{1,0:T(8,128)(2,1)S(1)} %get-tuple-element.20), channel_id=1, source_target_pairs={{0,18},{1,19},{2,16},{3,17},{4,22},{5,23},{6,20},{7,21},{8,26},{9,... | collective-permute-start | bytes 258056 | tf_op jit(solution)/shard_map/ppermute | solution.py:45
  37.3 2.9 %collective-permute-done.8 = bf16[24,1792]{1,0:T(8,128)(2,1)S(1)} collective-permute-done((bf16[24,1792]{1,0:T(8,128)(2,1)S(1)}, bf16[24,1792]{1,0:T(8,128)(2,1)S(1)}, u32[]{:S(2)}, u32[]{:S(2)}) %collective-permute-start.8) | collective-permute-done | bytes 86048 | tf_op jit(solution)/shard_map/ppermute | solution.py:45
  40.2 0.5 collective-permute-start.9
  40.7 1.0 %collective-permute-done.9 = bf16[24,1792]{1,0:T(8,128)(2,1)S(1)} collective-permute-done((bf16[24,1792]{1,0:T(8,128)(2,1)S(1)}, bf16[24,1792]{1,0:T(8,128)(2,1)S(1)}, u32[]{:S(2)}, u32[]{:S(2)}) %collective-permute-start.9) | collective-permute-done | bytes 86048 | tf_op jit(solution)/shard_map/ppermute | solution.py:45
  41.7 0.5 %fusion.12 = bf16[192,512]{1,0:T(8,128)(2,1)S(1)} fusion(bf16[192,1792]{1,0:T(8,128)(2,1)S(1)} %constant_dynamic-update-slice_fusion.2, bf16[1792,256]{1,0:T(8,128)(2,1)S(1)} %get-tuple-element.9, bf16[1792,256]{1,0:T(8,128)(2,1)S(1)} %get-tuple-element.22), kind=kOutput, calls=%fused_computation.13 | convolution fusion | flops 356089856 | bytes 2719744 | tf_op jit(solution)/shard_map/dot_general | solution.py:83
  42.3 1.5 %collective-permute-start.10 = (bf16[192,512]{1,0:T(8,128)(2,1)S(1)}, bf16[192,512]{1,0:T(8,128)(2,1)S(1)}, u32[]{:S(2)}, u32[]{:S(2)}) collective-permute-start(bf16[192,512]{1,0:T(8,128)(2,1)S(1)} %pad_maximum_fusion.1), channel_id=1, source_target_pairs={{0,16},{1,17},{2,18},{3,19},{4,20},{5,21},{6,22},{7,23},{8,24},{9,... | collective-permute-start | bytes 589832 | tf_op jit(solution)/shard_map/ppermute | solution.py:45
  43.9 0.5 collective-permute-start.15
  44.5 1.3 %collective-permute-done.13 = bf16[24,3584]{1,0:T(8,128)(2,1)S(1)} collective-permute-done((bf16[24,3584]{1,0:T(8,128)(2,1)S(1)}, bf16[24,3584]{1,0:T(8,128)(2,1)S(1)}, u32[]{:S(2)}, u32[]{:S(2)}) %collective-permute-start.13) | collective-permute-done | bytes 172064 | tf_op jit(solution)/shard_map/ppermute | solution.py:45
  45.9 3.6 %collective-permute-done.10 = bf16[192,512]{1,0:T(8,128)(2,1)S(1)} collective-permute-done((bf16[192,512]{1,0:T(8,128)(2,1)S(1)}, bf16[192,512]{1,0:T(8,128)(2,1)S(1)}, u32[]{:S(2)}, u32[]{:S(2)}) %collective-permute-start.10) | collective-permute-done | bytes 196640 | tf_op jit(solution)/shard_map/ppermute | solution.py:45
  49.5 0.5 %fusion.9 = f32[192,512]{1,0:T(8,128)S(1)} fusion(bf16[192,1792]{1,0:T(8,128)(2,1)S(1)} %constant_dynamic-update-slice_fusion.2, bf16[1792,256]{1,0:T(8,128)(2,1)S(1)} %get-tuple-element.10, bf16[1792,256]{1,0:T(8,128)(2,1)S(1)} %get-tuple-element.21, bf16[192,512]{1,0:T(8,128)(2,1)S(1)} %collective-permute-done.10), kind=kOutput, calls=%fused_computation.12 | convolution fusion | flops 356188160 | bytes 3112960 | tf_op jit(solution)/shard_map/dot_general | solution.py:83
  50.0 1.9 %convolution_convert_fusion = bf16[256,3584]{1,0:T(8,128)(2,1)} fusion(bf16[192,3584]{1,0:T(8,128)(2,1)S(1)} %constant_dynamic-update-slice_fusion.10, f32[192,512]{1,0:T(8,128)S(1)} %fusion.9), kind=kOutput, calls=%fused_computation | convolution fusion | flops 353533952 | bytes 3604480 | tf_op jit(solution)/shard_map/dot_general | solution.py:94
  (56 shorter events, 0.8 us)
Async XLA Ops:
  0.0 2.3 %copy-start = (bf16[128,3584]{1,0:T(8,128)(2,1)S(1)}, bf16[128,3584]{1,0:T(8,128)(2,1)}, u32[]{:S(2)}) copy-start(bf16[128,3584]{1,0:T(8,128)(2,1)} %param.7) | copy-start | bytes 2752516
  0.0 2.6 %copy-start.2 = (bf16[128,3584]{1,0:T(8,128)(2,1)S(1)}, bf16[128,3584]{1,0:T(8,128)(2,1)}, u32[]{:S(2)}) copy-start(bf16[128,3584]{1,0:T(8,128)(2,1)} %param.6) | copy-start | bytes 2752516
  3.0 17.7 %copy-start.1 = (bf16[1792,512]{1,0:T(8,128)(2,1)S(1)}, bf16[1792,512]{1,0:T(8,128)(2,1)}, u32[]{:S(2)}) copy-start(bf16[1792,512]{1,0:T(8,128)(2,1)} %param.9) | copy-start | bytes 5505028
  3.7 8.9 %collective-permute-start.2 = (bf16[6,7168]{1,0:T(8,128)(2,1)}, bf16[6,7168]{1,0:T(8,128)(2,1)S(1)}, u32[]{:S(2)}, u32[]{:S(2)}) collective-permute-start(bf16[6,7168]{1,0:T(8,128)(2,1)} %get-tuple-element.12), channel_id=1, source_target_pairs={{0,12},{1,13},{2,14},{3,15},{4,0},{5,1},{6,2},{7,3},{8,4},{9,5},{1... | collective-permute-start | bytes 258056 | tf_op jit(solution)/shard_map/ppermute | solution.py:45
  8.8 10.1 %collective-permute-start.1 = (bf16[6,7168]{1,0:T(8,128)(2,1)S(1)}, bf16[6,7168]{1,0:T(8,128)(2,1)S(1)}, u32[]{:S(2)}, u32[]{:S(2)}) collective-permute-start(bf16[6,7168]{1,0:T(8,128)(2,1)S(1)} %get-tuple-element.13), channel_id=1, source_target_pairs={{0,8},{1,9},{2,10},{3,11},{4,12},{5,13},{6,14},{7,15},{8,0},{9,1},... | collective-permute-start | bytes 258056 | tf_op jit(solution)/shard_map/ppermute | solution.py:45
  8.8 10.1 %collective-permute-start = (bf16[6,7168]{1,0:T(8,128)(2,1)S(1)}, bf16[6,7168]{1,0:T(8,128)(2,1)S(1)}, u32[]{:S(2)}, u32[]{:S(2)}) collective-permute-start(bf16[6,7168]{1,0:T(8,128)(2,1)S(1)} %get-tuple-element.14), channel_id=1, source_target_pairs={{0,4},{1,5},{2,6},{3,7},{4,8},{5,9},{6,10},{7,11},{8,12},{9,13},{1... | collective-permute-start | bytes 258056 | tf_op jit(solution)/shard_map/ppermute | solution.py:45
  19.1 6.9 %collective-permute-start.4 = (bf16[24,1792]{1,0:T(8,128)(2,1)S(1)}, bf16[24,1792]{1,0:T(8,128)(2,1)S(1)}, u32[]{:S(2)}, u32[]{:S(2)}) collective-permute-start(bf16[24,1792]{1,0:T(8,128)(2,1)S(1)} %get-tuple-element.6), channel_id=1, source_target_pairs={{0,2},{1,3},{2,0},{3,1},{4,6},{5,7},{6,4},{7,5},{8,10},{9,11},{10,... | collective-permute-start | bytes 258056 | tf_op jit(solution)/shard_map/ppermute | solution.py:45
  20.7 6.8 %collective-permute-start.3 = (bf16[24,1792]{1,0:T(8,128)(2,1)S(1)}, bf16[24,1792]{1,0:T(8,128)(2,1)S(1)}, u32[]{:S(2)}, u32[]{:S(2)}) collective-permute-start(bf16[24,1792]{1,0:T(8,128)(2,1)S(1)} %get-tuple-element.6), channel_id=1, source_target_pairs={{0,1},{1,0},{2,3},{3,2},{4,5},{5,4},{6,7},{7,6},{8,9},{9,8},{10,11... | collective-permute-start | bytes 258056 | tf_op jit(solution)/shard_map/ppermute | solution.py:45
  22.5 21.4 %collective-permute-start.16 = (bf16[24,3584]{1,0:T(8,128)(2,1)S(1)}, bf16[24,3584]{1,0:T(8,128)(2,1)S(1)}, u32[]{:S(2)}, u32[]{:S(2)}) collective-permute-start(bf16[24,3584]{1,0:T(8,128)(2,1)S(1)} %get-tuple-element.17), channel_id=1, source_target_pairs={{0,18},{1,19},{2,16},{3,17},{4,22},{5,23},{6,20},{7,21},{8,26},{9,... | collective-permute-start | bytes 516104 | tf_op jit(solution)/shard_map/ppermute | solution.py:45
  23.9 19.9 %collective-permute-start.14 = (bf16[24,3584]{1,0:T(8,128)(2,1)S(1)}, bf16[24,3584]{1,0:T(8,128)(2,1)S(1)}, u32[]{:S(2)}, u32[]{:S(2)}) collective-permute-start(bf16[24,3584]{1,0:T(8,128)(2,1)S(1)} %get-tuple-element.17), channel_id=1, source_target_pairs={{0,16},{1,17},{2,18},{3,19},{4,20},{5,21},{6,22},{7,23},{8,24},{9,... | collective-permute-start | bytes 516104 | tf_op jit(solution)/shard_map/ppermute | solution.py:45
  24.5 19.9 %collective-permute-start.12 = (bf16[24,3584]{1,0:T(8,128)(2,1)S(1)}, bf16[24,3584]{1,0:T(8,128)(2,1)S(1)}, u32[]{:S(2)}, u32[]{:S(2)}) collective-permute-start(bf16[24,3584]{1,0:T(8,128)(2,1)S(1)} %get-tuple-element.17), channel_id=1, source_target_pairs={{0,2},{1,3},{2,0},{3,1},{4,6},{5,7},{6,4},{7,5},{8,10},{9,11},{10,... | collective-permute-start | bytes 516104 | tf_op jit(solution)/shard_map/ppermute | solution.py:45
  26.0 8.8 %collective-permute-start.6 = (bf16[24,1792]{1,0:T(8,128)(2,1)S(1)}, bf16[24,1792]{1,0:T(8,128)(2,1)S(1)}, u32[]{:S(2)}, u32[]{:S(2)}) collective-permute-start(bf16[24,1792]{1,0:T(8,128)(2,1)S(1)} %get-tuple-element.20), channel_id=1, source_target_pairs={{0,16},{1,17},{2,18},{3,19},{4,20},{5,21},{6,22},{7,23},{8,24},{9,... | collective-permute-start | bytes 258056 | tf_op jit(solution)/shard_map/ppermute | solution.py:45
  27.5 9.8 %collective-permute-start.5 = (bf16[24,1792]{1,0:T(8,128)(2,1)S(1)}, bf16[24,1792]{1,0:T(8,128)(2,1)S(1)}, u32[]{:S(2)}, u32[]{:S(2)}) collective-permute-start(bf16[24,1792]{1,0:T(8,128)(2,1)S(1)} %collective-permute-done.4), channel_id=1, source_target_pairs={{0,1},{1,0},{2,3},{3,2},{4,5},{5,4},{6,7},{7,6},{8,9},{9,8},{10,11... | collective-permute-start | bytes 258056 | tf_op jit(solution)/shard_map/ppermute | solution.py:45
  34.8 5.4 %collective-permute-start.8 = (bf16[24,1792]{1,0:T(8,128)(2,1)S(1)}, bf16[24,1792]{1,0:T(8,128)(2,1)S(1)}, u32[]{:S(2)}, u32[]{:S(2)}) collective-permute-start(bf16[24,1792]{1,0:T(8,128)(2,1)S(1)} %get-tuple-element.20), channel_id=1, source_target_pairs={{0,18},{1,19},{2,16},{3,17},{4,22},{5,23},{6,20},{7,21},{8,26},{9,... | collective-permute-start | bytes 258056 | tf_op jit(solution)/shard_map/ppermute | solution.py:45
  37.2 3.0 %collective-permute-start.7 = (bf16[24,1792]{1,0:T(8,128)(2,1)S(1)}, bf16[24,1792]{1,0:T(8,128)(2,1)S(1)}, u32[]{:S(2)}, u32[]{:S(2)}) collective-permute-start(bf16[24,1792]{1,0:T(8,128)(2,1)S(1)} %collective-permute-done.6), channel_id=1, source_target_pairs={{0,1},{1,0},{2,3},{3,2},{4,5},{5,4},{6,7},{7,6},{8,9},{9,8},{10,11... | collective-permute-start | bytes 258056 | tf_op jit(solution)/shard_map/ppermute | solution.py:45
  40.2 4.2 %collective-permute-start.11 = (bf16[24,3584]{1,0:T(8,128)(2,1)S(1)}, bf16[24,3584]{1,0:T(8,128)(2,1)S(1)}, u32[]{:S(2)}, u32[]{:S(2)}) collective-permute-start(bf16[24,3584]{1,0:T(8,128)(2,1)S(1)} %get-tuple-element.17), channel_id=1, source_target_pairs={{0,1},{1,0},{2,3},{3,2},{4,5},{5,4},{6,7},{7,6},{8,9},{9,8},{10,11... | collective-permute-start | bytes 516104 | tf_op jit(solution)/shard_map/ppermute | solution.py:45
  40.2 1.5 %collective-permute-start.9 = (bf16[24,1792]{1,0:T(8,128)(2,1)S(1)}, bf16[24,1792]{1,0:T(8,128)(2,1)S(1)}, u32[]{:S(2)}, u32[]{:S(2)}) collective-permute-start(bf16[24,1792]{1,0:T(8,128)(2,1)S(1)} %collective-permute-done.8), channel_id=1, source_target_pairs={{0,1},{1,0},{2,3},{3,2},{4,5},{5,4},{6,7},{7,6},{8,9},{9,8},{10,11... | collective-permute-start | bytes 258056 | tf_op jit(solution)/shard_map/ppermute | solution.py:45
  42.3 7.1 %collective-permute-start.10 = (bf16[192,512]{1,0:T(8,128)(2,1)S(1)}, bf16[192,512]{1,0:T(8,128)(2,1)S(1)}, u32[]{:S(2)}, u32[]{:S(2)}) collective-permute-start(bf16[192,512]{1,0:T(8,128)(2,1)S(1)} %pad_maximum_fusion.1), channel_id=1, source_target_pairs={{0,16},{1,17},{2,18},{3,19},{4,20},{5,21},{6,22},{7,23},{8,24},{9,... | collective-permute-start | bytes 589832 | tf_op jit(solution)/shard_map/ppermute | solution.py:45
  43.8 2.0 %collective-permute-start.17 = (bf16[24,3584]{1,0:T(8,128)(2,1)S(1)}, bf16[24,3584]{1,0:T(8,128)(2,1)S(1)}, u32[]{:S(2)}, u32[]{:S(2)}) collective-permute-start(bf16[24,3584]{1,0:T(8,128)(2,1)S(1)} %collective-permute-done.16), channel_id=1, source_target_pairs={{0,1},{1,0},{2,3},{3,2},{4,5},{5,4},{6,7},{7,6},{8,9},{9,8},{10,11... | collective-permute-start | bytes 516104 | tf_op jit(solution)/shard_map/ppermute | solution.py:45
  43.9 2.0 %collective-permute-start.15 = (bf16[24,3584]{1,0:T(8,128)(2,1)S(1)}, bf16[24,3584]{1,0:T(8,128)(2,1)S(1)}, u32[]{:S(2)}, u32[]{:S(2)}) collective-permute-start(bf16[24,3584]{1,0:T(8,128)(2,1)S(1)} %collective-permute-done.14), channel_id=1, source_target_pairs={{0,1},{1,0},{2,3},{3,2},{4,5},{5,4},{6,7},{7,6},{8,9},{9,8},{10,11... | collective-permute-start | bytes 516104 | tf_op jit(solution)/shard_map/ppermute | solution.py:45
  44.4 1.4 %collective-permute-start.13 = (bf16[24,3584]{1,0:T(8,128)(2,1)S(1)}, bf16[24,3584]{1,0:T(8,128)(2,1)S(1)}, u32[]{:S(2)}, u32[]{:S(2)}) collective-permute-start(bf16[24,3584]{1,0:T(8,128)(2,1)S(1)} %collective-permute-done.12), channel_id=1, source_target_pairs={{0,1},{1,0},{2,3},{3,2},{4,5},{5,4},{6,7},{7,6},{8,9},{9,8},{10,11... | collective-permute-start | bytes 516104 | tf_op jit(solution)/shard_map/ppermute | solution.py:45

commit v2 on v1

v2 whole, which is shorter than its diff:
```python
import functools

import jax
import jax.numpy as jnp
from jax import lax
from jax.experimental import pallas as pl
from jax.experimental.pallas import tpu as pltpu
from jax.sharding import PartitionSpec as P

N_ROUTED = 256
SPLIT = 4
PIECES = 4
AXES = ("dp", "expert")
MIB = 1024 * 1024


def pack_kernel(cap, experts, me_ref, *refs):
    sources, out_refs = refs[:4], refs[4 : 4 + experts]
    held_refs, sems = refs[4 + experts : 8 + experts], refs[8 + experts]
    copies = [
        pltpu.make_async_copy(source, held, sems.at[i])
        for i, (source, held) in enumerate(zip(sources, held_refs))
    ]
    for copy in copies:
        copy.start()
    ids_ref, weights_ref, tokens_ref, grads_ref = held_refs
    rows, width = tokens_ref.shape[0], tokens_ref.shape[1] // PIECES
    copies[0].wait()
    copies[1].wait()
    ids, weights = ids_ref[...], weights_ref[...]
    chosen, scales = [], []
    for k in range(experts):
        match = ids == (me_ref[0] ^ k)
        chosen.append(jnp.max(jnp.where(match, 1.0, 0.0), axis=0, keepdims=True))
        scales.append(jnp.sum(jnp.where(match, weights, 0.0), axis=0, keepdims=True))
    flags = jnp.concatenate(chosen, axis=0)
    before = lax.broadcasted_iota(jnp.int32, (rows, rows), 0)
    after = lax.broadcasted_iota(jnp.int32, (rows, rows), 1)
    upper = jnp.where(before <= after, 1.0, 0.0).astype(jnp.bfloat16)
    rank = jnp.dot(flags.astype(jnp.bfloat16), upper, preferred_element_type=jnp.float32)
    height = PIECES * cap
    row = lax.broadcasted_iota(jnp.int32, (height, rows), 0)
    piece, slot = row // cap, row % cap
    picks, slot_scales = [], []
    for k in range(experts):
        place = jnp.where(chosen[k] > 0.0, rank[k : k + 1], 0.0).astype(jnp.int32)
        pick = place == slot + 1
        picks.append(jnp.where(pick, 1.0, 0.0))
        slot_scales.append(jnp.sum(jnp.where(pick, scales[k], 0.0), axis=1, keepdims=True))
    pick_all = jnp.concatenate(picks, axis=0)
    piece_all = jnp.concatenate([piece] * experts, axis=0)
    select = jnp.concatenate(
        [jnp.where(piece_all == j, pick_all, 0.0) for j in range(PIECES)], axis=1
    ).astype(jnp.bfloat16)

    def pieces(ref):
        return jnp.concatenate([ref[:, j * width : (j + 1) * width] for j in range(PIECES)], axis=0)

    copies[2].wait()
    rows_x = jnp.dot(select, pieces(tokens_ref), preferred_element_type=jnp.float32)
    copies[3].wait()
    rows_dy = jnp.dot(select, pieces(grads_ref), preferred_element_type=jnp.float32)
    for k in range(experts):
        at = slice(k * height, (k + 1) * height)
        both = jnp.concatenate([rows_x[at], rows_dy[at] * slot_scales[k]], axis=0)
        out_refs[k][...] = both.astype(jnp.bfloat16)


def pack(tokens, out_grad, route_ids, route_weights, me_e, experts, cap):
    features = tokens.shape[1]
    message = jax.ShapeDtypeStruct((2 * PIECES * cap, features // PIECES), jnp.bfloat16)
    sources = (route_ids.T, route_weights.T, tokens, out_grad)
    return pl.pallas_call(
        functools.partial(pack_kernel, cap, experts),
        out_shape=[message] * experts,
        in_specs=[pl.BlockSpec(memory_space=pltpu.SMEM)] + [pl.BlockSpec(memory_space=pl.ANY)] * 4,
        out_specs=[pl.BlockSpec(memory_space=pltpu.VMEM)] * experts,
        scratch_shapes=[pltpu.VMEM(source.shape, source.dtype) for source in sources]
        + [pltpu.SemaphoreType.DMA((4,))],
        compiler_params=pltpu.CompilerParams(vmem_limit_bytes=60 * MIB),
    )(me_e.reshape(1), *sources)


def project_kernel(units, at_ref, gate_ref, up_ref, *refs):
    x_refs, out_ref = refs[:-1], refs[-1]
    at = at_ref[0] if gate_ref.shape[1] == units else pl.multiple_of(at_ref[0] * units, units)
    x = jnp.concatenate([ref[...] for ref in x_refs], axis=0)
    for i, ref in enumerate((gate_ref, up_ref)):
        weight = ref[...] if ref.shape[1] == units else ref[:, pl.ds(at, units)]
        out_ref[:, i * units : (i + 1) * units] = jnp.dot(
            x, weight, preferred_element_type=jnp.float32
        ).astype(out_ref.dtype)


def project(x_blocks, gate_weight, up_weight, part, n_parts, dtype):
    units = gate_weight.shape[1] // n_parts
    rows, depth = sum(x.shape[0] for x in x_blocks), x_blocks[0].shape[1]
    if units % 128:
        gate_weight = lax.dynamic_slice_in_dim(gate_weight, part * units, units, 1)
        up_weight = lax.dynamic_slice_in_dim(up_weight, part * units, units, 1)
    vmem = pl.BlockSpec(memory_space=pltpu.VMEM)
    return pl.pallas_call(
        functools.partial(project_kernel, units),
        out_shape=jax.ShapeDtypeStruct((rows, 2 * units), dtype),
        in_specs=[pl.BlockSpec(memory_space=pltpu.SMEM)] + [vmem] * (2 + len(x_blocks)),
        out_specs=vmem,
        compiler_params=pltpu.CompilerParams(vmem_limit_bytes=32 * MIB),
        cost_estimate=pl.CostEstimate(
            flops=4 * rows * depth * units,
            bytes_accessed=2 * rows * depth + 4 * depth * units,
            transcendentals=0,
        ),
    )(part.reshape(1), gate_weight, up_weight, *x_blocks)


def finish_kernel(n_got, n_blocks, keep_ref, *refs):
    got_refs, dy_refs = refs[:n_got], refs[n_got : n_got + n_blocks]
    out_ref, stage_ref, sems = refs[n_got + n_blocks :]
    total = keep_ref[...]
    for got in got_refs:
        total = total + got[...].astype(jnp.float32)
    units = total.shape[1] // 2
    gate, up = total[:, :units], total[:, units:]
    hidden = gate / (1.0 + jnp.exp(-gate)) * up
    hidden = hidden.T.astype(jnp.bfloat16)
    chunks, _, width = stage_ref.shape
    copies = []
    for c in range(chunks):
        columns = slice(c * width, (c + 1) * width)
        dy = jnp.concatenate([ref[:, columns] for ref in dy_refs], axis=0)
        stage_ref[c] = jnp.dot(hidden, dy, preferred_element_type=jnp.float32).astype(jnp.bfloat16)
        copies.append(pltpu.make_async_copy(stage_ref.at[c], out_ref.at[:, columns], sems.at[c]))
        copies[-1].start()
    for copy in copies:
        copy.wait()


def finish(keep, arrived, dy_blocks):
    units, features = keep.shape[1] // 2, dy_blocks[0].shape[1]
    vmem = pl.BlockSpec(memory_space=pltpu.VMEM)
    width = 512
    chunks = features // width
    return pl.pallas_call(
        functools.partial(finish_kernel, len(arrived), len(dy_blocks)),
        out_shape=jax.ShapeDtypeStruct((units, features), jnp.bfloat16),
        in_specs=[vmem] * (1 + len(arrived) + len(dy_blocks)),
        out_specs=pl.BlockSpec(memory_space=pl.ANY),
        scratch_shapes=[
            pltpu.VMEM((chunks, units, width), jnp.bfloat16),
            pltpu.SemaphoreType.DMA((chunks,)),
        ],
        compiler_params=pltpu.CompilerParams(vmem_limit_bytes=48 * MIB),
    )(keep, *arrived, *dy_blocks)


def per_device(tokens, out_grad, gate_weight, up_weight, route_ids, route_weights):
    n_dp, n_expert = lax.axis_size("dp"), lax.axis_size("expert")
    experts = n_expert // SPLIT
    depth = gate_weight.shape[0]
    cap = max(2, tokens.shape[0] * route_ids.shape[1] * 3 // (2 * N_ROUTED))
    me_d, me_s = lax.axis_index("dp"), lax.axis_index("expert")
    me_e = me_s // SPLIT

    def send(value, by_d, by_e, by_q):
        pairs = []
        for d in range(n_dp):
            for s in range(n_expert):
                e, q = s // SPLIT, s % SPLIT
                to = (e ^ by_e) * SPLIT + (q ^ by_q)
                pairs.append((d * n_expert + s, (d + by_d) % n_dp * n_expert + to))
        return lax.ppermute(value, AXES, pairs)

    messages = pack(tokens, out_grad, route_ids, route_weights, me_e, experts, cap)
    parts = [messages[0]] + [send(messages[k], 0, k, 0) for k in range(1, experts)]

    def unfold(part, first):
        return jnp.concatenate(
            [part[(first + j) * cap : (first + j + 1) * cap] for j in range(PIECES)], axis=1
        )

    held_x = jnp.concatenate([unfold(part, 0) for part in parts], axis=0)
    held_dy = jnp.concatenate([unfold(part, PIECES) for part in parts], axis=0)

    def x_for(by_d):
        return lax.dynamic_slice_in_dim(held_x, (me_d + by_d) % n_dp * depth, depth, 1)

    x_blocks, dy_blocks = {}, {}
    for by_d in reversed(range(n_dp)):
        x_part = x_for(by_d)
        x_blocks[by_d, 2] = send(x_part, by_d, 0, 2)
        x_blocks[by_d, 0] = send(x_part, by_d, 0, 0) if by_d else x_part
    for by_d in reversed(range(n_dp)):
        dy_blocks[by_d, 0] = send(held_dy, by_d, 0, 0) if by_d else held_dy
        dy_blocks[by_d, 2] = send(dy_blocks[by_d, 0], 0, 0, 2)

    def both_cores(blocks):
        other = {key: send(block, 0, 0, 1) for key, block in blocks.items()}
        keys = [(by_d, by_q) for by_d in range(n_dp) for by_q in (0, 2)]
        return [blocks[key] for key in keys], [other[key] for key in keys]

    x_own, x_other = both_cores(x_blocks)
    dy_own, dy_other = both_cores(dy_blocks)

    def x_rows(by_d):
        rows = []
        for blocks in (x_own, x_other):
            step = len(blocks) // n_dp
            rows += [blocks[(i - by_d * step) % len(blocks)] for i in range(len(blocks))]
        return rows

    arrived = []
    for by_d in range(1, n_dp):
        to = (me_d + by_d) % n_dp
        ready = project(x_rows(by_d), gate_weight, up_weight, to, n_dp, jnp.bfloat16)
        arrived.append(send(ready, by_d, 0, 0))
    keep = project(x_rows(0), gate_weight, up_weight, me_d, n_dp, jnp.float32)
    return finish(keep, arrived, dy_own + dy_other)


def solution(mesh):
    return jax.shard_map(
        per_device,
        mesh=mesh,
        in_specs=(
            P(("dp", "expert"), None),
            P(("dp", "expert"), None),
            P("dp", "expert"),
            P("dp", "expert"),
            P(("dp", "expert"), None),
            P(("dp", "expert"), None),
        ),
        out_specs=P(("expert", "dp"), None),
        check_vma=False,
    )
```

time: 52.2 us -> 36.8 us (0.70)
  waiting for transfers between devices: 25.2 us -> 14.2 us
  Pallas kernels: 0 us -> 5.34 us
  matrix products: 3.45 us -> 0 us
  local copies, waits for them, and re-layouts: 3.23 us -> 1 us
  starting transfers between devices: 17.7 us -> 15.6 us
  other arithmetic: 2.12 us -> 0.18 us
    ppermute x18, waiting for transfers between devices: 25.2 us -> 14.2 us  [send(): return lax.ppermute(value, AXES, pairs)]
    pallas_call x0 -> x4, Pallas kernels: none -> 5.34 us  [the longest x1 2.68 us: pack(): pl.pallas_call(functools.partial(pack_kernel, cap, experts), out_shape=[m...]
    dot_general x5 -> x0, matrix products: 3.45 us -> none  [the longest x1 1.93 us: per_device(): lax.dot_general(hidden, dy_all, (((0,), (0,)), ((), ())), preferred_eleme...]
    ppermute x18, starting transfers between devices: 17.7 us -> 15.6 us  [send(): return lax.ppermute(value, AXES, pairs)]
    dynamic_slice x1, local copies, waits for them, and re-layouts: 1.75 us -> 0.02 us  [x_for(): lax.dynamic_slice_in_dim(held_x, (me_d + by_d) % n_dp * depth, depth, 1)]
    slice x2 -> x4, local copies, waits for them, and re-layouts: 0.05 us -> 0.96 us  [unfold(): part[(first + j) * cap:(first + j + 1) * cap]]
    reduce_or x1 -> x0, other arithmetic: 0.84 us -> none  [pack_rows(): chosen = jnp.any(matches, axis=1)]
    reduce_sum x2 -> x0, other arithmetic: 0.83 us -> none  [the longest x1 0.72 us: pack_rows(): scales = jnp.sum(jnp.where(matches, route_weights[:, :, None], 0.0), axis=1)]
  transfers between devices with their start and end apart: 18 -> 18, of which waited for: 7 -> 8; matrix products, arithmetic and copies ran while one was open for 5% -> 3% of each run, Pallas kernels for 0% -> 3%
where the time goes in v2:
time: 36.8 us; the launch traced here: 36.5 us
  starting transfers between devices  15.6 us (42%)
  waiting for transfers between devices  14.2 us (39%)
  Pallas kernels  5.34 us (15%)
  local copies, waits for them, and re-layouts  1 us (3%)
    ppermute x18, starting transfers between devices, send(): return lax.ppermute(value, AXES, pairs)  15.6 us
    ppermute x18, waiting for transfers between devices, send(): return lax.ppermute(value, AXES, pairs)  14.2 us
    pallas_call x1, Pallas kernels, pack(): pl.pallas_call(functools.partial(pack_kernel, cap, experts), out_shape=[m...  2.68 us
    pallas_call x1, Pallas kernels, finish(): pl.pallas_call(functools.partial(finish_kernel, len(arrived), len(dy_bloc...  1.6 us
    pallas_call x2, Pallas kernels, project(): pl.pallas_call(functools.partial(project_kernel, units), out_shape=jax.Sh...  1.06 us
    slice x4, local copies, waits for them, and re-layouts, unfold(): part[(first + j) * cap:(first + j + 1) * cap]  0.96 us
  transfers between devices with their start and end apart: 18, of which 8 were waited for; matrix products, arithmetic and copies ran while one was open for 3% of the time, Pallas kernels for 3%

profile of v2, /device:TPU:0, one launch (start us, length us, event | category | flops | bytes accessed | tf_op | source)
XLA Modules:
  0.0 36.5 jit_solution(7847417098900746470)
XLA Ops:
  0.0 2.7 %shard_map.64 = (bf16[48,896]{1,0:T(8,128)(2,1)}, bf16[48,896]{1,0:T(8,128)(2,1)}, bf16[48,896]{1,0:T(8,128)(2,1)}, bf16[48,896]{1,0:T(8,128)(2,1)}) custom-call(s32[1]{0:T(128)} %bitcast.1.me_ref, s32[8,128]{1,0:T(8,128)} %bitcast.5, f32[8,128]{1,0:T(8,128)} %bitcast.6, bf16[128,3584]{1,0:T(8,128)(2,1)} %refs_2_.1, bf16[128,3584]{1,0:T(8,128)(2,1)} %refs_3_.1), custom_call_target="tpu_custom_call" | custom-call | tf_op jit(solution)/shard_map/pallas_call | solution.py:73
  2.7 3.1 %collective-permute-start = (bf16[48,896]{1,0:T(8,128)(2,1)}, bf16[48,896]{1,0:T(8,128)(2,1)S(1)}, u32[]{:S(2)}, u32[]{:S(2)}) collective-permute-start(bf16[48,896]{1,0:T(8,128)(2,1)} %get-tuple-element.10), channel_id=1, source_target_pairs={{0,4},{1,5},{2,6},{3,7},{4,0},{5,1},{6,2},{7,3},{8,12},{9,13},{10,... | collective-permute-start | bytes 258056 | tf_op jit(solution)/shard_map/ppermute | solution.py:171
  5.8 2.6 %collective-permute-start.1 = (bf16[48,896]{1,0:T(8,128)(2,1)}, bf16[48,896]{1,0:T(8,128)(2,1)S(1)}, u32[]{:S(2)}, u32[]{:S(2)}) collective-permute-start(bf16[48,896]{1,0:T(8,128)(2,1)} %get-tuple-element.11), channel_id=1, source_target_pairs={{0,8},{1,9},{2,10},{3,11},{4,12},{5,13},{6,14},{7,15},{8,0},{9,1},... | collective-permute-start | bytes 258056 | tf_op jit(solution)/shard_map/ppermute | solution.py:171
  8.4 0.0 collective-permute-start.2
  8.4 0.9 %fusion = (bf16[6,896]{1,0:T(8,128)(2,1)S(1)}, bf16[6,896]{1,0:T(8,128)(2,1)S(1)}, bf16[6,896]{1,0:T(8,128)(2,1)S(1)}, bf16[6,896]{1,0:T(8,128)(2,1)S(1)}, bf16[...) fusion(bf16[48,896]{1,0:T(8,128)(2,1)} %get-tuple-element.9), kind=kLoop, calls=%fused_computation.4 | loop fusion | bytes 172032 | tf_op jit(solution)/shard_map/slice | solution.py:178
  9.3 0.0 copy-start.1
  9.3 0.0 collective-permute-done
  9.4 6.1 %collective-permute-done.1 = bf16[48,896]{1,0:T(8,128)(2,1)S(1)} collective-permute-done((bf16[48,896]{1,0:T(8,128)(2,1)}, bf16[48,896]{1,0:T(8,128)(2,1)S(1)}, u32[]{:S(2)}, u32[]{:S(2)}) %collective-permute-start.1) | collective-permute-done | bytes 86048 | tf_op jit(solution)/shard_map/ppermute | solution.py:171
  15.5 0.0 collective-permute-done.2
  15.6 0.1 maximum_maximum_fusion.1.refs_1_
  15.7 1.6 %collective-permute-start.12 = (bf16[24,3584]{1,0:T(8,128)(2,1)S(1)}, bf16[24,3584]{1,0:T(8,128)(2,1)S(1)}, u32[]{:S(2)}, u32[]{:S(2)}) collective-permute-start(bf16[24,3584]{1,0:T(8,128)(2,1)S(1)} %maximum_maximum_fusion.1.refs_1_), channel_id=1, source_target_pairs={{0,16},{1,17},{2,18},{3,19},{4,20},{5,21},{6,22},{7,23},{8,24},{9,... | collective-permute-start | bytes 516104 | tf_op jit(solution)/shard_map/ppermute | solution.py:171
  17.2 0.1 maximum_maximum_fusion
  17.4 1.5 %collective-permute-start.5 = (bf16[24,1792]{1,0:T(8,128)(2,1)S(1)}, bf16[24,1792]{1,0:T(8,128)(2,1)S(1)}, u32[]{:S(2)}, u32[]{:S(2)}) collective-permute-start(bf16[24,1792]{1,0:T(8,128)(2,1)S(1)} %get-tuple-element.13), channel_id=1, source_target_pairs={{0,18},{1,19},{2,16},{3,17},{4,22},{5,23},{6,20},{7,21},{8,26},{9,... | collective-permute-start | bytes 258056 | tf_op jit(solution)/shard_map/ppermute | solution.py:171
  18.9 1.5 %collective-permute-start.4 = (bf16[24,1792]{1,0:T(8,128)(2,1)S(1)}, bf16[24,1792]{1,0:T(8,128)(2,1)S(1)}, u32[]{:S(2)}, u32[]{:S(2)}) collective-permute-start(bf16[24,1792]{1,0:T(8,128)(2,1)S(1)} %get-tuple-element.13), channel_id=1, source_target_pairs={{0,16},{1,17},{2,18},{3,19},{4,20},{5,21},{6,22},{7,23},{8,24},{9,... | collective-permute-start | bytes 258056 | tf_op jit(solution)/shard_map/ppermute | solution.py:171
  20.4 0.5 %collective-permute-start.3 = (bf16[24,1792]{1,0:T(8,128)(2,1)S(1)}, bf16[24,1792]{1,0:T(8,128)(2,1)S(1)}, u32[]{:S(2)}, u32[]{:S(2)}) collective-permute-start(bf16[24,1792]{1,0:T(8,128)(2,1)S(1)} %get-tuple-element.14.refs_0_.refs_2_), channel_id=1, source_target_pairs={{0,2},{1,3},{2,0},{3,1},{4,6},{5,7},{6,4},{7,5},{8,10},{9,11},{10,... | collective-permute-start | bytes 258056 | tf_op jit(solution)/shard_map/ppermute | solution.py:171
  20.9 2.6 %collective-permute-done.5.refs_3_.refs_1_ = bf16[24,1792]{1,0:T(8,128)(2,1)S(1)} collective-permute-done((bf16[24,1792]{1,0:T(8,128)(2,1)S(1)}, bf16[24,1792]{1,0:T(8,128)(2,1)S(1)}, u32[]{:S(2)}, u32[]{:S(2)}) %collective-permute-start.5) | collective-permute-done | bytes 86048 | tf_op jit(solution)/shard_map/ppermute | solution.py:171
  23.5 1.1 %collective-permute-start.11 = (bf16[24,3584]{1,0:T(8,128)(2,1)S(1)}, bf16[24,3584]{1,0:T(8,128)(2,1)S(1)}, u32[]{:S(2)}, u32[]{:S(2)}) collective-permute-start(bf16[24,3584]{1,0:T(8,128)(2,1)S(1)} %maximum_maximum_fusion.1.refs_1_), channel_id=1, source_target_pairs={{0,2},{1,3},{2,0},{3,1},{4,6},{5,7},{6,4},{7,5},{8,10},{9,11},{10,... | collective-permute-start | bytes 516104 | tf_op jit(solution)/shard_map/ppermute | solution.py:171
  24.6 1.0 %collective-permute-start.13 = (bf16[24,3584]{1,0:T(8,128)(2,1)S(1)}, bf16[24,3584]{1,0:T(8,128)(2,1)S(1)}, u32[]{:S(2)}, u32[]{:S(2)}) collective-permute-start(bf16[24,3584]{1,0:T(8,128)(2,1)S(1)} %collective-permute-done.12.refs_3_), channel_id=1, source_target_pairs={{0,2},{1,3},{2,0},{3,1},{4,6},{5,7},{6,4},{7,5},{8,10},{9,11},{10,... | collective-permute-start | bytes 516104 | tf_op jit(solution)/shard_map/ppermute | solution.py:171
  25.5 0.0 collective-permute-done.4.refs_2_.refs_0_
  25.5 0.5 %collective-permute-start.8 = (bf16[24,1792]{1,0:T(8,128)(2,1)S(1)}, bf16[24,1792]{1,0:T(8,128)(2,1)S(1)}, u32[]{:S(2)}, u32[]{:S(2)}) collective-permute-start(bf16[24,1792]{1,0:T(8,128)(2,1)S(1)} %collective-permute-done.4.refs_2_.refs_0_), channel_id=1, source_target_pairs={{0,1},{1,0},{2,3},{3,2},{4,5},{5,4},{6,7},{7,6},{8,9},{9,8},{10,11... | collective-permute-start | bytes 258056 | tf_op jit(solution)/shard_map/ppermute | solution.py:171
  26.0 0.1 collective-permute-start.7
  26.1 0.7 %collective-permute-done.9.refs_7_.refs_5_ = bf16[24,1792]{1,0:T(8,128)(2,1)S(1)} collective-permute-done((bf16[24,1792]{1,0:T(8,128)(2,1)S(1)}, bf16[24,1792]{1,0:T(8,128)(2,1)S(1)}, u32[]{:S(2)}, u32[]{:S(2)}) %collective-permute-start.9) | collective-permute-done | bytes 86048 | tf_op jit(solution)/shard_map/ppermute | solution.py:171
  26.8 0.2 collective-permute-done.8.refs_6_.refs_4_
  27.0 0.4 collective-permute-done.7.refs_5_.refs_7_
  27.3 0.5 %shard_map.66 = bf16[192,512]{1,0:T(8,128)(2,1)S(1)} custom-call(s32[1]{0:T(128)} %bitcast.4.at_ref, bf16[1792,512]{1,0:T(8,128)(2,1)S(1)} %copy-done, bf16[1792,512]{1,0:T(8,128)(2,1)S(1)} %copy-done.1, bf16[24,1792]{1,0:T(8,128)(2,1)S(1)} %collective-permute-done.4.refs_2_.refs_0_, bf16[24,1792]{1,0:T(8,128)(2,1)S(1)} %collective-permute-done.5.refs_3_.refs_1_, ...), custom_call_target="tpu_custom_call" | custom-call | flops 352321536 | bytes 2523136 | tf_op jit(solution)/shard_map/pallas_call | solution.py:102
  27.9 1.7 %collective-permute-start.10 = (bf16[192,512]{1,0:T(8,128)(2,1)S(1)}, bf16[192,512]{1,0:T(8,128)(2,1)S(1)}, u32[]{:S(2)}, u32[]{:S(2)}) collective-permute-start(bf16[192,512]{1,0:T(8,128)(2,1)S(1)} %shard_map.66), channel_id=1, source_target_pairs={{0,16},{1,17},{2,18},{3,19},{4,20},{5,21},{6,22},{7,23},{8,24},{9,... | collective-permute-start | bytes 589832 | tf_op jit(solution)/shard_map/ppermute | solution.py:171
  29.5 0.5 %collective-permute-start.16 = (bf16[24,3584]{1,0:T(8,128)(2,1)S(1)}, bf16[24,3584]{1,0:T(8,128)(2,1)S(1)}, u32[]{:S(2)}, u32[]{:S(2)}) collective-permute-start(bf16[24,3584]{1,0:T(8,128)(2,1)S(1)} %collective-permute-done.12.refs_3_), channel_id=1, source_target_pairs={{0,1},{1,0},{2,3},{3,2},{4,5},{5,4},{6,7},{7,6},{8,9},{9,8},{10,11... | collective-permute-start | bytes 516104 | tf_op jit(solution)/shard_map/ppermute | solution.py:171
  30.0 0.8 %collective-permute-done.11.refs_2_ = bf16[24,3584]{1,0:T(8,128)(2,1)S(1)} collective-permute-done((bf16[24,3584]{1,0:T(8,128)(2,1)S(1)}, bf16[24,3584]{1,0:T(8,128)(2,1)S(1)}, u32[]{:S(2)}, u32[]{:S(2)}) %collective-permute-start.11) | collective-permute-done | bytes 172064 | tf_op jit(solution)/shard_map/ppermute | solution.py:171
  30.8 1.9 %collective-permute-done.13.refs_4_ = bf16[24,3584]{1,0:T(8,128)(2,1)S(1)} collective-permute-done((bf16[24,3584]{1,0:T(8,128)(2,1)S(1)}, bf16[24,3584]{1,0:T(8,128)(2,1)S(1)}, u32[]{:S(2)}, u32[]{:S(2)}) %collective-permute-start.13) | collective-permute-done | bytes 172064 | tf_op jit(solution)/shard_map/ppermute | solution.py:171
  32.7 0.5 %shard_map.65.keep_ref = f32[192,512]{1,0:T(8,128)S(1)} custom-call(s32[1]{0:T(128)} %bitcast.at_ref, bf16[1792,512]{1,0:T(8,128)(2,1)S(1)} %copy-done, bf16[1792,512]{1,0:T(8,128)(2,1)S(1)} %copy-done.1, bf16[24,1792]{1,0:T(8,128)(2,1)S(1)} %get-tuple-element.14.refs_0_.refs_2_, bf16[24,1792]{1,0:T(8,128)(2,1)S(1)} %collective-permute-done.3.refs_1_.refs_3_, ...), custom_call_target="tpu_custom_call" | custom-call | flops 352321536 | bytes 2523136 | tf_op jit(solution)/shard_map/pallas_call | solution.py:102
  33.3 1.6 %collective-permute-done.10.refs_0_ = bf16[192,512]{1,0:T(8,128)(2,1)S(1)} collective-permute-done((bf16[192,512]{1,0:T(8,128)(2,1)S(1)}, bf16[192,512]{1,0:T(8,128)(2,1)S(1)}, u32[]{:S(2)}, u32[]{:S(2)}) %collective-permute-start.10) | collective-permute-done | bytes 196640 | tf_op jit(solution)/shard_map/ppermute | solution.py:171
  34.9 1.6 %shard_map.67 = bf16[256,3584]{1,0:T(8,128)(2,1)} custom-call(f32[192,512]{1,0:T(8,128)S(1)} %shard_map.65.keep_ref, bf16[192,512]{1,0:T(8,128)(2,1)S(1)} %collective-permute-done.10.refs_0_, bf16[24,3584]{1,0:T(8,128)(2,1)S(1)} %maximum_maximum_fusion.1.refs_1_, bf16[24,3584]{1,0:T(8,128)(2,1)S(1)} %collective-permute-done.11.refs_2_, ...), custom_call_target="tpu_custom_call" | custom-call | tf_op jit(solution)/shard_map/pallas_call | solution.py:143
  (19 shorter events, 0.1 us)
Async XLA Ops:
  0.0 27.3 %copy-start = (bf16[1792,512]{1,0:T(8,128)(2,1)S(1)}, bf16[1792,512]{1,0:T(8,128)(2,1)}, u32[]{:S(2)}) copy-start(bf16[1792,512]{1,0:T(8,128)(2,1)} %gate_ref.3) | copy-start | bytes 5505028
  2.7 6.6 %collective-permute-start = (bf16[48,896]{1,0:T(8,128)(2,1)}, bf16[48,896]{1,0:T(8,128)(2,1)S(1)}, u32[]{:S(2)}, u32[]{:S(2)}) collective-permute-start(bf16[48,896]{1,0:T(8,128)(2,1)} %get-tuple-element.10), channel_id=1, source_target_pairs={{0,4},{1,5},{2,6},{3,7},{4,0},{5,1},{6,2},{7,3},{8,12},{9,13},{10,... | collective-permute-start | bytes 258056 | tf_op jit(solution)/shard_map/ppermute | solution.py:171
  5.8 9.7 %collective-permute-start.1 = (bf16[48,896]{1,0:T(8,128)(2,1)}, bf16[48,896]{1,0:T(8,128)(2,1)S(1)}, u32[]{:S(2)}, u32[]{:S(2)}) collective-permute-start(bf16[48,896]{1,0:T(8,128)(2,1)} %get-tuple-element.11), channel_id=1, source_target_pairs={{0,8},{1,9},{2,10},{3,11},{4,12},{5,13},{6,14},{7,15},{8,0},{9,1},... | collective-permute-start | bytes 258056 | tf_op jit(solution)/shard_map/ppermute | solution.py:171
  8.4 7.1 %collective-permute-start.2 = (bf16[48,896]{1,0:T(8,128)(2,1)}, bf16[48,896]{1,0:T(8,128)(2,1)S(1)}, u32[]{:S(2)}, u32[]{:S(2)}) collective-permute-start(bf16[48,896]{1,0:T(8,128)(2,1)} %get-tuple-element.12), channel_id=1, source_target_pairs={{0,12},{1,13},{2,14},{3,15},{4,8},{5,9},{6,10},{7,11},{8,4},{9,5},... | collective-permute-start | bytes 258056 | tf_op jit(solution)/shard_map/ppermute | solution.py:171
  9.3 18.0 %copy-start.1 = (bf16[1792,512]{1,0:T(8,128)(2,1)S(1)}, bf16[1792,512]{1,0:T(8,128)(2,1)}, u32[]{:S(2)}) copy-start(bf16[1792,512]{1,0:T(8,128)(2,1)} %up_ref.3) | copy-start | bytes 5505028
  15.7 8.9 %collective-permute-start.12 = (bf16[24,3584]{1,0:T(8,128)(2,1)S(1)}, bf16[24,3584]{1,0:T(8,128)(2,1)S(1)}, u32[]{:S(2)}, u32[]{:S(2)}) collective-permute-start(bf16[24,3584]{1,0:T(8,128)(2,1)S(1)} %maximum_maximum_fusion.1.refs_1_), channel_id=1, source_target_pairs={{0,16},{1,17},{2,18},{3,19},{4,20},{5,21},{6,22},{7,23},{8,24},{9,... | collective-permute-start | bytes 516104 | tf_op jit(solution)/shard_map/ppermute | solution.py:171
  17.4 6.1 %collective-permute-start.5 = (bf16[24,1792]{1,0:T(8,128)(2,1)S(1)}, bf16[24,1792]{1,0:T(8,128)(2,1)S(1)}, u32[]{:S(2)}, u32[]{:S(2)}) collective-permute-start(bf16[24,1792]{1,0:T(8,128)(2,1)S(1)} %get-tuple-element.13), channel_id=1, source_target_pairs={{0,18},{1,19},{2,16},{3,17},{4,22},{5,23},{6,20},{7,21},{8,26},{9,... | collective-permute-start | bytes 258056 | tf_op jit(solution)/shard_map/ppermute | solution.py:171
  18.9 6.6 %collective-permute-start.4 = (bf16[24,1792]{1,0:T(8,128)(2,1)S(1)}, bf16[24,1792]{1,0:T(8,128)(2,1)S(1)}, u32[]{:S(2)}, u32[]{:S(2)}) collective-permute-start(bf16[24,1792]{1,0:T(8,128)(2,1)S(1)} %get-tuple-element.13), channel_id=1, source_target_pairs={{0,16},{1,17},{2,18},{3,19},{4,20},{5,21},{6,22},{7,23},{8,24},{9,... | collective-permute-start | bytes 258056 | tf_op jit(solution)/shard_map/ppermute | solution.py:171
  20.4 5.1 %collective-permute-start.6 = (bf16[24,1792]{1,0:T(8,128)(2,1)S(1)}, bf16[24,1792]{1,0:T(8,128)(2,1)S(1)}, u32[]{:S(2)}, u32[]{:S(2)}) collective-permute-start(bf16[24,1792]{1,0:T(8,128)(2,1)S(1)} %get-tuple-element.14.refs_0_.refs_2_), channel_id=1, source_target_pairs={{0,1},{1,0},{2,3},{3,2},{4,5},{5,4},{6,7},{7,6},{8,9},{9,8},{10,11... | collective-permute-start | bytes 258056 | tf_op jit(solution)/shard_map/ppermute | solution.py:171
  20.4 5.7 %collective-permute-start.3 = (bf16[24,1792]{1,0:T(8,128)(2,1)S(1)}, bf16[24,1792]{1,0:T(8,128)(2,1)S(1)}, u32[]{:S(2)}, u32[]{:S(2)}) collective-permute-start(bf16[24,1792]{1,0:T(8,128)(2,1)S(1)} %get-tuple-element.14.refs_0_.refs_2_), channel_id=1, source_target_pairs={{0,2},{1,3},{2,0},{3,1},{4,6},{5,7},{6,4},{7,5},{8,10},{9,11},{10,... | collective-permute-start | bytes 258056 | tf_op jit(solution)/shard_map/ppermute | solution.py:171
  23.5 7.3 %collective-permute-start.11 = (bf16[24,3584]{1,0:T(8,128)(2,1)S(1)}, bf16[24,3584]{1,0:T(8,128)(2,1)S(1)}, u32[]{:S(2)}, u32[]{:S(2)}) collective-permute-start(bf16[24,3584]{1,0:T(8,128)(2,1)S(1)} %maximum_maximum_fusion.1.refs_1_), channel_id=1, source_target_pairs={{0,2},{1,3},{2,0},{3,1},{4,6},{5,7},{6,4},{7,5},{8,10},{9,11},{10,... | collective-permute-start | bytes 516104 | tf_op jit(solution)/shard_map/ppermute | solution.py:171
  24.6 8.2 %collective-permute-start.13 = (bf16[24,3584]{1,0:T(8,128)(2,1)S(1)}, bf16[24,3584]{1,0:T(8,128)(2,1)S(1)}, u32[]{:S(2)}, u32[]{:S(2)}) collective-permute-start(bf16[24,3584]{1,0:T(8,128)(2,1)S(1)} %collective-permute-done.12.refs_3_), channel_id=1, source_target_pairs={{0,2},{1,3},{2,0},{3,1},{4,6},{5,7},{6,4},{7,5},{8,10},{9,11},{10,... | collective-permute-start | bytes 516104 | tf_op jit(solution)/shard_map/ppermute | solution.py:171
  25.5 1.3 %collective-permute-start.9 = (bf16[24,1792]{1,0:T(8,128)(2,1)S(1)}, bf16[24,1792]{1,0:T(8,128)(2,1)S(1)}, u32[]{:S(2)}, u32[]{:S(2)}) collective-permute-start(bf16[24,1792]{1,0:T(8,128)(2,1)S(1)} %collective-permute-done.5.refs_3_.refs_1_), channel_id=1, source_target_pairs={{0,1},{1,0},{2,3},{3,2},{4,5},{5,4},{6,7},{7,6},{8,9},{9,8},{10,11... | collective-permute-start | bytes 258056 | tf_op jit(solution)/shard_map/ppermute | solution.py:171
  25.5 1.4 %collective-permute-start.8 = (bf16[24,1792]{1,0:T(8,128)(2,1)S(1)}, bf16[24,1792]{1,0:T(8,128)(2,1)S(1)}, u32[]{:S(2)}, u32[]{:S(2)}) collective-permute-start(bf16[24,1792]{1,0:T(8,128)(2,1)S(1)} %collective-permute-done.4.refs_2_.refs_0_), channel_id=1, source_target_pairs={{0,1},{1,0},{2,3},{3,2},{4,5},{5,4},{6,7},{7,6},{8,9},{9,8},{10,11... | collective-permute-start | bytes 258056 | tf_op jit(solution)/shard_map/ppermute | solution.py:171
  26.0 1.3 %collective-permute-start.7 = (bf16[24,1792]{1,0:T(8,128)(2,1)S(1)}, bf16[24,1792]{1,0:T(8,128)(2,1)S(1)}, u32[]{:S(2)}, u32[]{:S(2)}) collective-permute-start(bf16[24,1792]{1,0:T(8,128)(2,1)S(1)} %collective-permute-done.3.refs_1_.refs_3_), channel_id=1, source_target_pairs={{0,1},{1,0},{2,3},{3,2},{4,5},{5,4},{6,7},{7,6},{8,9},{9,8},{10,11... | collective-permute-start | bytes 258056 | tf_op jit(solution)/shard_map/ppermute | solution.py:171
  27.9 7.0 %collective-permute-start.10 = (bf16[192,512]{1,0:T(8,128)(2,1)S(1)}, bf16[192,512]{1,0:T(8,128)(2,1)S(1)}, u32[]{:S(2)}, u32[]{:S(2)}) collective-permute-start(bf16[192,512]{1,0:T(8,128)(2,1)S(1)} %shard_map.66), channel_id=1, source_target_pairs={{0,16},{1,17},{2,18},{3,19},{4,20},{5,21},{6,22},{7,23},{8,24},{9,... | collective-permute-start | bytes 589832 | tf_op jit(solution)/shard_map/ppermute | solution.py:171
  29.5 3.7 %collective-permute-start.14 = (bf16[24,3584]{1,0:T(8,128)(2,1)S(1)}, bf16[24,3584]{1,0:T(8,128)(2,1)S(1)}, u32[]{:S(2)}, u32[]{:S(2)}) collective-permute-start(bf16[24,3584]{1,0:T(8,128)(2,1)S(1)} %maximum_maximum_fusion.1.refs_1_), channel_id=1, source_target_pairs={{0,1},{1,0},{2,3},{3,2},{4,5},{5,4},{6,7},{7,6},{8,9},{9,8},{10,11... | collective-permute-start | bytes 516104 | tf_op jit(solution)/shard_map/ppermute | solution.py:171
  29.5 3.7 %collective-permute-start.16 = (bf16[24,3584]{1,0:T(8,128)(2,1)S(1)}, bf16[24,3584]{1,0:T(8,128)(2,1)S(1)}, u32[]{:S(2)}, u32[]{:S(2)}) collective-permute-start(bf16[24,3584]{1,0:T(8,128)(2,1)S(1)} %collective-permute-done.12.refs_3_), channel_id=1, source_target_pairs={{0,1},{1,0},{2,3},{3,2},{4,5},{5,4},{6,7},{7,6},{8,9},{9,8},{10,11... | collective-permute-start | bytes 516104 | tf_op jit(solution)/shard_map/ppermute | solution.py:171
  30.8 2.5 %collective-permute-start.15 = (bf16[24,3584]{1,0:T(8,128)(2,1)S(1)}, bf16[24,3584]{1,0:T(8,128)(2,1)S(1)}, u32[]{:S(2)}, u32[]{:S(2)}) collective-permute-start(bf16[24,3584]{1,0:T(8,128)(2,1)S(1)} %collective-permute-done.11.refs_2_), channel_id=1, source_target_pairs={{0,1},{1,0},{2,3},{3,2},{4,5},{5,4},{6,7},{7,6},{8,9},{9,8},{10,11... | collective-permute-start | bytes 516104 | tf_op jit(solution)/shard_map/ppermute | solution.py:171
  32.7 2.2 %collective-permute-start.17 = (bf16[24,3584]{1,0:T(8,128)(2,1)S(1)}, bf16[24,3584]{1,0:T(8,128)(2,1)S(1)}, u32[]{:S(2)}, u32[]{:S(2)}) collective-permute-start(bf16[24,3584]{1,0:T(8,128)(2,1)S(1)} %collective-permute-done.13.refs_4_), channel_id=1, source_target_pairs={{0,1},{1,0},{2,3},{3,2},{4,5},{5,4},{6,7},{7,6},{8,9},{9,8},{10,11... | collective-permute-start | bytes 516104 | tf_op jit(solution)/shard_map/ppermute | solution.py:171

commit v3 on v2

--- a/solution.py
+++ b/solution.py
@@ -70,47 +70,49 @@
     features = tokens.shape[1]
     message = jax.ShapeDtypeStruct((2 * PIECES * cap, features // PIECES), jnp.bfloat16)
     sources = (route_ids.T, route_weights.T, tokens, out_grad)
+    held = [pltpu.VMEM(source.shape, source.dtype) for source in sources]
+    sources = [pltpu.with_memory_space_constraint(source, pltpu.HBM) for source in sources]
     return pl.pallas_call(
         functools.partial(pack_kernel, cap, experts),
         out_shape=[message] * experts,
         in_specs=[pl.BlockSpec(memory_space=pltpu.SMEM)] + [pl.BlockSpec(memory_space=pl.ANY)] * 4,
         out_specs=[pl.BlockSpec(memory_space=pltpu.VMEM)] * experts,
-        scratch_shapes=[pltpu.VMEM(source.shape, source.dtype) for source in sources]
-        + [pltpu.SemaphoreType.DMA((4,))],
-        compiler_params=pltpu.CompilerParams(vmem_limit_bytes=60 * MIB),
+        scratch_shapes=held + [pltpu.SemaphoreType.DMA((4,))],
+        compiler_params=pltpu.CompilerParams(vmem_limit_bytes=16 * MIB),
     )(me_e.reshape(1), *sources)
 
 
-def project_kernel(units, at_ref, gate_ref, up_ref, *refs):
-    x_refs, out_ref = refs[:-1], refs[-1]
-    at = at_ref[0] if gate_ref.shape[1] == units else pl.multiple_of(at_ref[0] * units, units)
+def project_kernel(n_weights, at_ref, *refs):
+    weight_refs, x_refs, out_ref = refs[:n_weights], refs[n_weights:-1], refs[-1]
     x = jnp.concatenate([ref[...] for ref in x_refs], axis=0)
-    for i, ref in enumerate((gate_ref, up_ref)):
-        weight = ref[...] if ref.shape[1] == units else ref[:, pl.ds(at, units)]
-        out_ref[:, i * units : (i + 1) * units] = jnp.dot(
+    width = out_ref.shape[1] // n_weights
+    for i, ref in enumerate(weight_refs):
+        if ref.shape[1] == width:
+            weight = ref[...]
+        else:
+            weight = ref[:, pl.ds(pl.multiple_of(at_ref[0] * width, width), width)]
+        out_ref[:, i * width : (i + 1) * width] = jnp.dot(
             x, weight, preferred_element_type=jnp.float32
         ).astype(out_ref.dtype)
 
 
-def project(x_blocks, gate_weight, up_weight, part, n_parts, dtype):
-    units = gate_weight.shape[1] // n_parts
-    rows, depth = sum(x.shape[0] for x in x_blocks), x_blocks[0].shape[1]
-    if units % 128:
-        gate_weight = lax.dynamic_slice_in_dim(gate_weight, part * units, units, 1)
-        up_weight = lax.dynamic_slice_in_dim(up_weight, part * units, units, 1)
+def project(x_blocks, weights, part, units, dtype):
+    rows, depth = sum(x.shape[0] for x in x_blocks), weights[0].shape[0]
+    if units % 128 and len(weights) == 2:
+        weights = [lax.dynamic_slice_in_dim(weight, part * units, units, 1) for weight in weights]
     vmem = pl.BlockSpec(memory_space=pltpu.VMEM)
     return pl.pallas_call(
-        functools.partial(project_kernel, units),
+        functools.partial(project_kernel, len(weights)),
         out_shape=jax.ShapeDtypeStruct((rows, 2 * units), dtype),
-        in_specs=[pl.BlockSpec(memory_space=pltpu.SMEM)] + [vmem] * (2 + len(x_blocks)),
+        in_specs=[pl.BlockSpec(memory_space=pltpu.SMEM)] + [vmem] * (len(weights) + len(x_blocks)),
         out_specs=vmem,
-        compiler_params=pltpu.CompilerParams(vmem_limit_bytes=32 * MIB),
+        compiler_params=pltpu.CompilerParams(vmem_limit_bytes=16 * MIB + 8 * rows * depth),
         cost_estimate=pl.CostEstimate(
             flops=4 * rows * depth * units,
             bytes_accessed=2 * rows * depth + 4 * depth * units,
             transcendentals=0,
         ),
-    )(part.reshape(1), gate_weight, up_weight, *x_blocks)
+    )(part.reshape(1), *weights, *x_blocks)
 
 
 def finish_kernel(n_got, n_blocks, keep_ref, *refs):
@@ -149,14 +151,16 @@
             pltpu.VMEM((chunks, units, width), jnp.bfloat16),
             pltpu.SemaphoreType.DMA((chunks,)),
         ],
-        compiler_params=pltpu.CompilerParams(vmem_limit_bytes=48 * MIB),
+        compiler_params=pltpu.CompilerParams(
+            vmem_limit_bytes=8 * MIB + 4 * features * (keep.shape[0] + units)
+        ),
     )(keep, *arrived, *dy_blocks)
 
 
 def per_device(tokens, out_grad, gate_weight, up_weight, route_ids, route_weights):
     n_dp, n_expert = lax.axis_size("dp"), lax.axis_size("expert")
     experts = n_expert // SPLIT
-    depth = gate_weight.shape[0]
+    depth, units = gate_weight.shape[0], gate_weight.shape[1] // n_dp
     cap = max(2, tokens.shape[0] * route_ids.shape[1] * 3 // (2 * N_ROUTED))
     me_d, me_s = lax.axis_index("dp"), lax.axis_index("expert")
     me_e = me_s // SPLIT
@@ -170,51 +174,72 @@
                 pairs.append((d * n_expert + s, (d + by_d) % n_dp * n_expert + to))
         return lax.ppermute(value, AXES, pairs)
 
+    def after(value, *others):
+        return lax.optimization_barrier((value, *others))[0]
+
     messages = pack(tokens, out_grad, route_ids, route_weights, me_e, experts, cap)
-    parts = [messages[0]] + [send(messages[k], 0, k, 0) for k in range(1, experts)]
+    parts = {0: messages[0]}
+    for k in range(1, experts):
+        parts[k] = send(messages[k], 0, k, 0)
+
+    gate_from, up_from, _ = lax.optimization_barrier((gate_weight, up_weight, parts[1]))
+
+    def columns_for(by_d):
+        at = (me_d + by_d) % n_dp * units
+        return jnp.concatenate(
+            [lax.dynamic_slice_in_dim(weight, at, units, 1) for weight in (gate_from, up_from)], axis=1
+        )
 
     def unfold(part, first):
         return jnp.concatenate(
             [part[(first + j) * cap : (first + j + 1) * cap] for j in range(PIECES)], axis=1
         )
 
-    held_x = jnp.concatenate([unfold(part, 0) for part in parts], axis=0)
-    held_dy = jnp.concatenate([unfold(part, PIECES) for part in parts], axis=0)
-
-    def x_for(by_d):
-        return lax.dynamic_slice_in_dim(held_x, (me_d + by_d) % n_dp * depth, depth, 1)
-
-    x_blocks, dy_blocks = {}, {}
-    for by_d in reversed(range(n_dp)):
-        x_part = x_for(by_d)
-        x_blocks[by_d, 2] = send(x_part, by_d, 0, 2)
-        x_blocks[by_d, 0] = send(x_part, by_d, 0, 0) if by_d else x_part
-    for by_d in reversed(range(n_dp)):
-        dy_blocks[by_d, 0] = send(held_dy, by_d, 0, 0) if by_d else held_dy
+    def held(ks, first):
+        return jnp.concatenate([unfold(parts[k], first) for k in ks], axis=0)
+
+    def half(rows, by_d):
+        return lax.dynamic_slice_in_dim(rows, (me_d + by_d) % n_dp * depth, depth, 1)
+
+    next_chips = [(by_d, 0) for by_d in range(1, n_dp)] + [(0, 2)]
+    soon, late = range(experts // 2), range(experts // 2, experts)
+    soon_x, soon_dy = held(soon, 0), held(soon, PIECES)
+    early = {(by_d, by_q): send(soon_dy, by_d, 0, by_q) for by_d, by_q in next_chips}
+    late_x = after(held(late, 0), *early.values())
+    late_dy = after(held(late, PIECES), *early.values())
+    held_x = jnp.concatenate([soon_x, late_x], axis=0)
+    held_dy = jnp.concatenate([soon_dy, late_dy], axis=0)
+
+    x_blocks, dy_blocks = {(0, 0): half(held_x, 0)}, {(0, 0): held_dy}
+    for by_d in reversed(range(1, n_dp)):
+        x_blocks[by_d, 2] = send(half(held_x, by_d), by_d, 0, 2)
+    for by_d, by_q in next_chips:
+        x_blocks[by_d, by_q] = send(half(held_x, by_d), by_d, 0, by_q)
+    for by_d, by_q in next_chips:
+        rows = send(late_dy, by_d, 0, by_q)
+        dy_blocks[by_d, by_q] = jnp.concatenate([early[by_d, by_q], rows], axis=0)
+    for by_d in range(1, n_dp):
         dy_blocks[by_d, 2] = send(dy_blocks[by_d, 0], 0, 0, 2)
 
     def both_cores(blocks):
-        other = {key: send(block, 0, 0, 1) for key, block in blocks.items()}
-        keys = [(by_d, by_q) for by_d in range(n_dp) for by_q in (0, 2)]
-        return [blocks[key] for key in keys], [other[key] for key in keys]
-
-    x_own, x_other = both_cores(x_blocks)
-    dy_own, dy_other = both_cores(dy_blocks)
+        own = [blocks[by_d, by_q] for by_d in range(n_dp) for by_q in (0, 2)]
+        return [own, [send(block, 0, 0, 1) for block in own]]
+
+    x_lists, dy_lists = both_cores(x_blocks), both_cores(dy_blocks)
 
     def x_rows(by_d):
         rows = []
-        for blocks in (x_own, x_other):
+        for blocks in x_lists:
             step = len(blocks) // n_dp
             rows += [blocks[(i - by_d * step) % len(blocks)] for i in range(len(blocks))]
         return rows
 
     arrived = []
     for by_d in range(1, n_dp):
-        to = (me_d + by_d) % n_dp
-        ready = project(x_rows(by_d), gate_weight, up_weight, to, n_dp, jnp.bfloat16)
+        ready = project(x_rows(by_d), [columns_for(by_d)], me_d, units, jnp.bfloat16)
         arrived.append(send(ready, by_d, 0, 0))
-    keep = project(x_rows(0), gate_weight, up_weight, me_d, n_dp, jnp.float32)
-    return finish(keep, arrived, dy_own + dy_other)
+    keep = project(x_rows(0), [gate_weight, up_weight], me_d, units, jnp.float32)
+    return finish(keep, arrived, [block for blocks in dy_lists for block in blocks])
 
 
 def solution(mesh):

time: 36.8 us -> 34.5 us (0.938)
  waiting for transfers between devices: 14.2 us -> 7.85 us
  starting transfers between devices: 15.6 us -> 19.7 us
  Pallas kernels: 5.34 us -> 4.63 us
  local copies, waits for them, and re-layouts: 1 us -> 1.46 us
    ppermute x18 -> x20, waiting for transfers between devices: 14.2 us -> 7.85 us  [send(): return lax.ppermute(value, AXES, pairs)]
    ppermute x18 -> x20, starting transfers between devices: 15.6 us -> 19.7 us  [send(): return lax.ppermute(value, AXES, pairs)]
    dynamic_slice x1 -> x2, local copies, waits for them, and re-layouts: 0.02 us -> 1.35 us  [the longest x1 1.33 us: columns_for(): lax.dynamic_slice_in_dim(weight, at, units, 1)]
    slice x4, local copies, waits for them, and re-layouts: 0.96 us -> 0.1 us  [unfold(): part[(first + j) * cap:(first + j + 1) * cap]]
    pallas_call x1, Pallas kernels: 2.68 us -> 1.99 us  [pack(): pl.pallas_call(functools.partial(pack_kernel, cap, experts), out_shape=[m...]
  transfers between devices with their start and end apart: 18 -> 20, of which waited for: 8 -> 7; matrix products, arithmetic and copies ran while one was open for 3% -> 5% of each run, Pallas kernels for 3% -> 3%
where the time goes in v3:
time: 34.5 us; the launch traced here: 34.4 us
  starting transfers between devices  19.7 us (57%)
  waiting for transfers between devices  7.85 us (23%)
  Pallas kernels  4.63 us (13%)
  local copies, waits for them, and re-layouts  1.46 us (4%)
  other arithmetic  0.51 us (1%)
    ppermute x20, starting transfers between devices, send(): return lax.ppermute(value, AXES, pairs)  19.7 us
    ppermute x20, waiting for transfers between devices, send(): return lax.ppermute(value, AXES, pairs)  7.85 us
    pallas_call x1, Pallas kernels, pack(): pl.pallas_call(functools.partial(pack_kernel, cap, experts), out_shape=[m...  1.99 us
    pallas_call x1, Pallas kernels, finish(): pl.pallas_call(functools.partial(finish_kernel, len(arrived), len(dy_bloc...  1.6 us
    dynamic_slice x1, local copies, waits for them, and re-layouts, columns_for(): lax.dynamic_slice_in_dim(weight, at, units, 1)  1.33 us
    pallas_call x2, Pallas kernels, project(): pl.pallas_call(functools.partial(project_kernel, len(weights)), out_shape...  1.05 us
  transfers between devices with their start and end apart: 20, of which 7 were waited for; matrix products, arithmetic and copies ran while one was open for 5% of the time, Pallas kernels for 3%

profile of v3, /device:TPU:0, one launch (start us, length us, event | category | flops | bytes accessed | tf_op | source)
XLA Modules:
  0.0 34.4 jit_solution(5388877484434511063)
XLA Ops:
  0.0 2.0 %shard_map.64 = (bf16[48,896]{1,0:T(8,128)(2,1)S(1)}, bf16[48,896]{1,0:T(8,128)(2,1)S(1)}, bf16[48,896]{1,0:T(8,128)(2,1)S(1)}, bf16[48,896]{1,0:T(8,128)(2,1)S(1)}) custom-call(s32[1]{0:T(128)} %bitcast.1.me_ref, s32[8,128]{1,0:T(8,128)} %bitcast.4, f32[8,128]{1,0:T(8,128)} %bitcast.5, bf16[128,3584]{1,0:T(8,128)(2,1)} %refs_2_.1, bf16[128,3584]{1,0:T(8,128)(2,1)} %refs_3_.1), custom_call_target="tpu_custom_call" | custom-call | tf_op jit(solution)/shard_map/pallas_call | solution.py:75
  2.0 3.1 %collective-permute-start = (bf16[48,896]{1,0:T(8,128)(2,1)S(1)}, bf16[48,896]{1,0:T(8,128)(2,1)S(1)}, u32[]{:S(2)}, u32[]{:S(2)}) collective-permute-start(bf16[48,896]{1,0:T(8,128)(2,1)S(1)} %get-tuple-element.14), channel_id=1, source_target_pairs={{0,4},{1,5},{2,6},{3,7},{4,0},{5,1},{6,2},{7,3},{8,12},{9,13},{10,... | collective-permute-start | bytes 258056 | tf_op jit(solution)/shard_map/ppermute | solution.py:175
  5.1 2.6 %collective-permute-start.1 = (bf16[48,896]{1,0:T(8,128)(2,1)S(1)}, bf16[48,896]{1,0:T(8,128)(2,1)S(1)}, u32[]{:S(2)}, u32[]{:S(2)}) collective-permute-start(bf16[48,896]{1,0:T(8,128)(2,1)S(1)} %get-tuple-element.15), channel_id=1, source_target_pairs={{0,8},{1,9},{2,10},{3,11},{4,12},{5,13},{6,14},{7,15},{8,0},{9,1},... | collective-permute-start | bytes 258056 | tf_op jit(solution)/shard_map/ppermute | solution.py:175
  7.8 1.8 %collective-permute-start.3 = (bf16[12,3584]{1,0:T(8,128)(2,1)S(1)}, bf16[12,3584]{1,0:T(8,128)(2,1)S(1)}, u32[]{:S(2)}, u32[]{:S(2)}) collective-permute-start(bf16[12,3584]{1,0:T(8,128)(2,1)S(1)} %maximum_maximum_fusion.1), channel_id=1, source_target_pairs={{0,16},{1,17},{2,18},{3,19},{4,20},{5,21},{6,22},{7,23},{8,24},{9,... | collective-permute-start | bytes 258056 | tf_op jit(solution)/shard_map/ppermute | solution.py:175
  9.6 1.5 %collective-permute-start.4 = (bf16[12,3584]{1,0:T(8,128)(2,1)S(1)}, bf16[12,3584]{1,0:T(8,128)(2,1)S(1)}, u32[]{:S(2)}, u32[]{:S(2)}) collective-permute-start(bf16[12,3584]{1,0:T(8,128)(2,1)S(1)} %maximum_maximum_fusion.1), channel_id=1, source_target_pairs={{0,2},{1,3},{2,0},{3,1},{4,6},{5,7},{6,4},{7,5},{8,10},{9,11},{10,... | collective-permute-start | bytes 258056 | tf_op jit(solution)/shard_map/ppermute | solution.py:175
  11.2 1.3 %constant_dynamic-slice_fusion = (bf16[1792,256]{1,0:T(8,128)(2,1)S(1)}, bf16[1792,256]{1,0:T(8,128)(2,1)S(1)}) fusion(bf16[1792,512]{1,0:T(8,128)(2,1)} %refs_1_.1, s32[]{:T(128)S(6)} %select_n.38, bf16[1792,512]{1,0:T(8,128)(2,1)S(1)} %copy-done), kind=kLoop, calls=%fused_computation.8 | loop fusion | bytes 3670020 | tf_op jit(solution)/shard_map/dynamic_slice | solution.py:190
  12.5 2.1 %collective-permute-done.1 = bf16[48,896]{1,0:T(8,128)(2,1)S(1)} collective-permute-done((bf16[48,896]{1,0:T(8,128)(2,1)S(1)}, bf16[48,896]{1,0:T(8,128)(2,1)S(1)}, u32[]{:S(2)}, u32[]{:S(2)}) %collective-permute-start.1) | collective-permute-done | bytes 86048 | tf_op jit(solution)/shard_map/ppermute | solution.py:175
  14.7 0.1 maximum_maximum_fusion
  14.7 0.1 pad_maximum_fusion.refs_0_
  14.9 0.1 pad_maximum_fusion.1
  15.0 1.6 %collective-permute-start.6 = (bf16[24,1792]{1,0:T(8,128)(2,1)S(1)}, bf16[24,1792]{1,0:T(8,128)(2,1)S(1)}, u32[]{:S(2)}, u32[]{:S(2)}) collective-permute-start(bf16[24,1792]{1,0:T(8,128)(2,1)S(1)} %get-tuple-element.21), channel_id=1, source_target_pairs={{0,16},{1,17},{2,18},{3,19},{4,20},{5,21},{6,22},{7,23},{8,24},{9,... | collective-permute-start | bytes 258056 | tf_op jit(solution)/shard_map/ppermute | solution.py:175
  16.6 1.5 %collective-permute-start.7 = (bf16[24,1792]{1,0:T(8,128)(2,1)S(1)}, bf16[24,1792]{1,0:T(8,128)(2,1)S(1)}, u32[]{:S(2)}, u32[]{:S(2)}) collective-permute-start(bf16[24,1792]{1,0:T(8,128)(2,1)S(1)} %get-tuple-element.21), channel_id=1, source_target_pairs={{0,18},{1,19},{2,16},{3,17},{4,22},{5,23},{6,20},{7,21},{8,26},{9,... | collective-permute-start | bytes 258056 | tf_op jit(solution)/shard_map/ppermute | solution.py:175
  18.1 0.5 %collective-permute-start.5 = (bf16[24,1792]{1,0:T(8,128)(2,1)S(1)}, bf16[24,1792]{1,0:T(8,128)(2,1)S(1)}, u32[]{:S(2)}, u32[]{:S(2)}) collective-permute-start(bf16[24,1792]{1,0:T(8,128)(2,1)S(1)} %get-tuple-element.22.refs_2_.refs_3_), channel_id=1, source_target_pairs={{0,2},{1,3},{2,0},{3,1},{4,6},{5,7},{6,4},{7,5},{8,10},{9,11},{10,... | collective-permute-start | bytes 258056 | tf_op jit(solution)/shard_map/ppermute | solution.py:175
  18.6 1.5 %collective-permute-start.14 = (bf16[12,3584]{1,0:T(8,128)(2,1)S(1)}, bf16[12,3584]{1,0:T(8,128)(2,1)S(1)}, u32[]{:S(2)}, u32[]{:S(2)}) collective-permute-start(bf16[12,3584]{1,0:T(8,128)(2,1)S(1)} %get-tuple-element.20), channel_id=1, source_target_pairs={{0,16},{1,17},{2,18},{3,19},{4,20},{5,21},{6,22},{7,23},{8,24},{9,... | collective-permute-start | bytes 258056 | tf_op jit(solution)/shard_map/ppermute | solution.py:175
  20.1 0.1 pad_maximum_fusion.2.refs_1_
  20.2 0.1 collective-permute-start.8
  20.2 0.3 collective-permute-done.6.refs_4_.refs_1_
  20.5 1.3 %collective-permute-start.13 = (bf16[12,3584]{1,0:T(8,128)(2,1)S(1)}, bf16[12,3584]{1,0:T(8,128)(2,1)S(1)}, u32[]{:S(2)}, u32[]{:S(2)}) collective-permute-start(bf16[12,3584]{1,0:T(8,128)(2,1)S(1)} %get-tuple-element.20), channel_id=1, source_target_pairs={{0,2},{1,3},{2,0},{3,1},{4,6},{5,7},{6,4},{7,5},{8,10},{9,11},{10,... | collective-permute-start | bytes 258056 | tf_op jit(solution)/shard_map/ppermute | solution.py:175
  21.8 0.4 %collective-permute-done.7.refs_5_.refs_2_ = bf16[24,1792]{1,0:T(8,128)(2,1)S(1)} collective-permute-done((bf16[24,1792]{1,0:T(8,128)(2,1)S(1)}, bf16[24,1792]{1,0:T(8,128)(2,1)S(1)}, u32[]{:S(2)}, u32[]{:S(2)}) %collective-permute-start.7) | collective-permute-done | bytes 86048 | tf_op jit(solution)/shard_map/ppermute | solution.py:175
  22.2 0.9 %collective-permute-done.5.refs_3_.refs_4_ = bf16[24,1792]{1,0:T(8,128)(2,1)S(1)} collective-permute-done((bf16[24,1792]{1,0:T(8,128)(2,1)S(1)}, bf16[24,1792]{1,0:T(8,128)(2,1)S(1)}, u32[]{:S(2)}, u32[]{:S(2)}) %collective-permute-start.5) | collective-permute-done | bytes 86048 | tf_op jit(solution)/shard_map/ppermute | solution.py:175
  23.1 0.3 collective-permute-done.14
  23.4 0.2 collective-permute-start.9
  23.6 0.4 %collective-permute-start.16 = (bf16[24,3584]{1,0:T(8,128)(2,1)S(1)}, bf16[24,3584]{1,0:T(8,128)(2,1)S(1)}, u32[]{:S(2)}, u32[]{:S(2)}) collective-permute-start(bf16[24,3584]{1,0:T(8,128)(2,1)S(1)} %pad_maximum_fusion.2.refs_1_), channel_id=1, source_target_pairs={{0,1},{1,0},{2,3},{3,2},{4,5},{5,4},{6,7},{7,6},{8,9},{9,8},{10,11... | collective-permute-start | bytes 516104 | tf_op jit(solution)/shard_map/ppermute | solution.py:175
  24.0 1.5 %collective-permute-start.15 = (bf16[24,3584]{1,0:T(8,128)(2,1)S(1)}, bf16[24,3584]{1,0:T(8,128)(2,1)S(1)}, u32[]{:S(2)}, u32[]{:S(2)}) collective-permute-start(bf16[24,3584]{1,0:T(8,128)(2,1)S(1)} %pad_maximum_fusion.4.refs_3_), channel_id=1, source_target_pairs={{0,2},{1,3},{2,0},{3,1},{4,6},{5,7},{6,4},{7,5},{8,10},{9,11},{10,... | collective-permute-start | bytes 516104 | tf_op jit(solution)/shard_map/ppermute | solution.py:175
  25.5 0.5 %shard_map.66 = bf16[192,512]{1,0:T(8,128)(2,1)S(1)} custom-call(s32[1]{0:T(128)} %bitcast.at_ref, bf16[1792,512]{1,0:T(8,128)(2,1)S(1)} %pad_maximum_fusion.refs_0_, bf16[24,1792]{1,0:T(8,128)(2,1)S(1)} %collective-permute-done.6.refs_4_.refs_1_, bf16[24,1792]{1,0:T(8,128)(2,1)S(1)} %collective-permute-done.7.refs_5_.refs_2_, ...), custom_call_target="tpu_custom_call" | custom-call | flops 352321536 | bytes 2523136 | tf_op jit(solution)/shard_map/pallas_call | solution.py:104
  26.1 1.6 %collective-permute-start.12 = (bf16[192,512]{1,0:T(8,128)(2,1)S(1)}, bf16[192,512]{1,0:T(8,128)(2,1)S(1)}, u32[]{:S(2)}, u32[]{:S(2)}) collective-permute-start(bf16[192,512]{1,0:T(8,128)(2,1)S(1)} %shard_map.66), channel_id=1, source_target_pairs={{0,16},{1,17},{2,18},{3,19},{4,20},{5,21},{6,22},{7,23},{8,24},{9,... | collective-permute-start | bytes 589832 | tf_op jit(solution)/shard_map/ppermute | solution.py:175
  27.7 0.1 collective-permute-start.17
  27.8 0.5 %collective-permute-start.18 = (bf16[24,3584]{1,0:T(8,128)(2,1)S(1)}, bf16[24,3584]{1,0:T(8,128)(2,1)S(1)}, u32[]{:S(2)}, u32[]{:S(2)}) collective-permute-start(bf16[24,3584]{1,0:T(8,128)(2,1)S(1)} %pad_maximum_fusion.4.refs_3_), channel_id=1, source_target_pairs={{0,1},{1,0},{2,3},{3,2},{4,5},{5,4},{6,7},{7,6},{8,9},{9,8},{10,11... | collective-permute-start | bytes 516104 | tf_op jit(solution)/shard_map/ppermute | solution.py:175
  28.3 2.2 %collective-permute-done.15.refs_4_ = bf16[24,3584]{1,0:T(8,128)(2,1)S(1)} collective-permute-done((bf16[24,3584]{1,0:T(8,128)(2,1)S(1)}, bf16[24,3584]{1,0:T(8,128)(2,1)S(1)}, u32[]{:S(2)}, u32[]{:S(2)}) %collective-permute-start.15) | collective-permute-done | bytes 172064 | tf_op jit(solution)/shard_map/ppermute | solution.py:175
  30.5 0.5 %shard_map.65.keep_ref = f32[192,512]{1,0:T(8,128)S(1)} custom-call(s32[1]{0:T(128)} %bitcast.at_ref, bf16[1792,512]{1,0:T(8,128)(2,1)S(1)} %copy-done, bf16[1792,512]{1,0:T(8,128)(2,1)S(1)} %copy-done.1, bf16[24,1792]{1,0:T(8,128)(2,1)S(1)} %get-tuple-element.22.refs_2_.refs_3_, bf16[24,1792]{1,0:T(8,128)(2,1)S(1)} %collective-permute-done.5.refs_3_.refs_4_, ...), custom_call_target="tpu_custom_call" | custom-call | flops 352321536 | bytes 2523136 | tf_op jit(solution)/shard_map/pallas_call | solution.py:104
  31.1 1.7 %collective-permute-done.12.refs_0_ = bf16[192,512]{1,0:T(8,128)(2,1)S(1)} collective-permute-done((bf16[192,512]{1,0:T(8,128)(2,1)S(1)}, bf16[192,512]{1,0:T(8,128)(2,1)S(1)}, u32[]{:S(2)}, u32[]{:S(2)}) %collective-permute-start.12) | collective-permute-done | bytes 196640 | tf_op jit(solution)/shard_map/ppermute | solution.py:175
  32.8 1.6 %shard_map.67 = bf16[256,3584]{1,0:T(8,128)(2,1)} custom-call(f32[192,512]{1,0:T(8,128)S(1)} %shard_map.65.keep_ref, bf16[192,512]{1,0:T(8,128)(2,1)S(1)} %collective-permute-done.12.refs_0_, bf16[24,3584]{1,0:T(8,128)(2,1)S(1)} %pad_maximum_fusion.2.refs_1_, bf16[24,3584]{1,0:T(8,128)(2,1)S(1)} %pad_maximum_fusion.3.refs_2_, ...), custom_call_target="tpu_custom_call" | custom-call | tf_op jit(solution)/shard_map/pallas_call | solution.py:145
  (29 shorter events, 0.3 us)
Async XLA Ops:
  0.0 11.2 %copy-start = (bf16[1792,512]{1,0:T(8,128)(2,1)S(1)}, bf16[1792,512]{1,0:T(8,128)(2,1)}, u32[]{:S(2)}) copy-start(bf16[1792,512]{1,0:T(8,128)(2,1)} %refs_0_.1) | copy-start | bytes 5505028
  2.0 5.8 %collective-permute-start = (bf16[48,896]{1,0:T(8,128)(2,1)S(1)}, bf16[48,896]{1,0:T(8,128)(2,1)S(1)}, u32[]{:S(2)}, u32[]{:S(2)}) collective-permute-start(bf16[48,896]{1,0:T(8,128)(2,1)S(1)} %get-tuple-element.14), channel_id=1, source_target_pairs={{0,4},{1,5},{2,6},{3,7},{4,0},{5,1},{6,2},{7,3},{8,12},{9,13},{10,... | collective-permute-start | bytes 258056 | tf_op jit(solution)/shard_map/ppermute | solution.py:175
  5.1 9.5 %collective-permute-start.1 = (bf16[48,896]{1,0:T(8,128)(2,1)S(1)}, bf16[48,896]{1,0:T(8,128)(2,1)S(1)}, u32[]{:S(2)}, u32[]{:S(2)}) collective-permute-start(bf16[48,896]{1,0:T(8,128)(2,1)S(1)} %get-tuple-element.15), channel_id=1, source_target_pairs={{0,8},{1,9},{2,10},{3,11},{4,12},{5,13},{6,14},{7,15},{8,0},{9,1},... | collective-permute-start | bytes 258056 | tf_op jit(solution)/shard_map/ppermute | solution.py:175
  7.7 6.9 %collective-permute-start.2 = (bf16[48,896]{1,0:T(8,128)(2,1)S(1)}, bf16[48,896]{1,0:T(8,128)(2,1)S(1)}, u32[]{:S(2)}, u32[]{:S(2)}) collective-permute-start(bf16[48,896]{1,0:T(8,128)(2,1)S(1)} %get-tuple-element.16), channel_id=1, source_target_pairs={{0,12},{1,13},{2,14},{3,15},{4,8},{5,9},{6,10},{7,11},{8,4},{9,5},... | collective-permute-start | bytes 258056 | tf_op jit(solution)/shard_map/ppermute | solution.py:175
  7.8 7.1 %collective-permute-start.3 = (bf16[12,3584]{1,0:T(8,128)(2,1)S(1)}, bf16[12,3584]{1,0:T(8,128)(2,1)S(1)}, u32[]{:S(2)}, u32[]{:S(2)}) collective-permute-start(bf16[12,3584]{1,0:T(8,128)(2,1)S(1)} %maximum_maximum_fusion.1), channel_id=1, source_target_pairs={{0,16},{1,17},{2,18},{3,19},{4,20},{5,21},{6,22},{7,23},{8,24},{9,... | collective-permute-start | bytes 258056 | tf_op jit(solution)/shard_map/ppermute | solution.py:175
  9.6 5.3 %collective-permute-start.4 = (bf16[12,3584]{1,0:T(8,128)(2,1)S(1)}, bf16[12,3584]{1,0:T(8,128)(2,1)S(1)}, u32[]{:S(2)}, u32[]{:S(2)}) collective-permute-start(bf16[12,3584]{1,0:T(8,128)(2,1)S(1)} %maximum_maximum_fusion.1), channel_id=1, source_target_pairs={{0,2},{1,3},{2,0},{3,1},{4,6},{5,7},{6,4},{7,5},{8,10},{9,11},{10,... | collective-permute-start | bytes 258056 | tf_op jit(solution)/shard_map/ppermute | solution.py:175
  15.0 5.5 %collective-permute-start.6 = (bf16[24,1792]{1,0:T(8,128)(2,1)S(1)}, bf16[24,1792]{1,0:T(8,128)(2,1)S(1)}, u32[]{:S(2)}, u32[]{:S(2)}) collective-permute-start(bf16[24,1792]{1,0:T(8,128)(2,1)S(1)} %get-tuple-element.21), channel_id=1, source_target_pairs={{0,16},{1,17},{2,18},{3,19},{4,20},{5,21},{6,22},{7,23},{8,24},{9,... | collective-permute-start | bytes 258056 | tf_op jit(solution)/shard_map/ppermute | solution.py:175
  16.6 5.6 %collective-permute-start.7 = (bf16[24,1792]{1,0:T(8,128)(2,1)S(1)}, bf16[24,1792]{1,0:T(8,128)(2,1)S(1)}, u32[]{:S(2)}, u32[]{:S(2)}) collective-permute-start(bf16[24,1792]{1,0:T(8,128)(2,1)S(1)} %get-tuple-element.21), channel_id=1, source_target_pairs={{0,18},{1,19},{2,16},{3,17},{4,22},{5,23},{6,20},{7,21},{8,26},{9,... | collective-permute-start | bytes 258056 | tf_op jit(solution)/shard_map/ppermute | solution.py:175
  18.1 5.0 %collective-permute-start.5 = (bf16[24,1792]{1,0:T(8,128)(2,1)S(1)}, bf16[24,1792]{1,0:T(8,128)(2,1)S(1)}, u32[]{:S(2)}, u32[]{:S(2)}) collective-permute-start(bf16[24,1792]{1,0:T(8,128)(2,1)S(1)} %get-tuple-element.22.refs_2_.refs_3_), channel_id=1, source_target_pairs={{0,2},{1,3},{2,0},{3,1},{4,6},{5,7},{6,4},{7,5},{8,10},{9,11},{10,... | collective-permute-start | bytes 258056 | tf_op jit(solution)/shard_map/ppermute | solution.py:175
  18.6 4.8 %collective-permute-start.14 = (bf16[12,3584]{1,0:T(8,128)(2,1)S(1)}, bf16[12,3584]{1,0:T(8,128)(2,1)S(1)}, u32[]{:S(2)}, u32[]{:S(2)}) collective-permute-start(bf16[12,3584]{1,0:T(8,128)(2,1)S(1)} %get-tuple-element.20), channel_id=1, source_target_pairs={{0,16},{1,17},{2,18},{3,19},{4,20},{5,21},{6,22},{7,23},{8,24},{9,... | collective-permute-start | bytes 258056 | tf_op jit(solution)/shard_map/ppermute | solution.py:175
  20.2 10.4 %copy-start.1 = (bf16[1792,512]{1,0:T(8,128)(2,1)S(1)}, bf16[1792,512]{1,0:T(8,128)(2,1)}, u32[]{:S(2)}) copy-start(bf16[1792,512]{1,0:T(8,128)(2,1)} %refs_1_.1) | copy-start | bytes 5505028
  20.2 3.5 %collective-permute-start.8 = (bf16[24,1792]{1,0:T(8,128)(2,1)S(1)}, bf16[24,1792]{1,0:T(8,128)(2,1)S(1)}, u32[]{:S(2)}, u32[]{:S(2)}) collective-permute-start(bf16[24,1792]{1,0:T(8,128)(2,1)S(1)} %get-tuple-element.22.refs_2_.refs_3_), channel_id=1, source_target_pairs={{0,1},{1,0},{2,3},{3,2},{4,5},{5,4},{6,7},{7,6},{8,9},{9,8},{10,11... | collective-permute-start | bytes 258056 | tf_op jit(solution)/shard_map/ppermute | solution.py:175
  20.5 7.1 %collective-permute-start.13 = (bf16[12,3584]{1,0:T(8,128)(2,1)S(1)}, bf16[12,3584]{1,0:T(8,128)(2,1)S(1)}, u32[]{:S(2)}, u32[]{:S(2)}) collective-permute-start(bf16[12,3584]{1,0:T(8,128)(2,1)S(1)} %get-tuple-element.20), channel_id=1, source_target_pairs={{0,2},{1,3},{2,0},{3,1},{4,6},{5,7},{6,4},{7,5},{8,10},{9,11},{10,... | collective-permute-start | bytes 258056 | tf_op jit(solution)/shard_map/ppermute | solution.py:175
  22.2 1.8 %collective-permute-start.10 = (bf16[24,1792]{1,0:T(8,128)(2,1)S(1)}, bf16[24,1792]{1,0:T(8,128)(2,1)S(1)}, u32[]{:S(2)}, u32[]{:S(2)}) collective-permute-start(bf16[24,1792]{1,0:T(8,128)(2,1)S(1)} %collective-permute-done.6.refs_4_.refs_1_), channel_id=1, source_target_pairs={{0,1},{1,0},{2,3},{3,2},{4,5},{5,4},{6,7},{7,6},{8,9},{9,8},{10,11... | collective-permute-start | bytes 258056 | tf_op jit(solution)/shard_map/ppermute | solution.py:175
  23.1 2.5 %collective-permute-start.11 = (bf16[24,1792]{1,0:T(8,128)(2,1)S(1)}, bf16[24,1792]{1,0:T(8,128)(2,1)S(1)}, u32[]{:S(2)}, u32[]{:S(2)}) collective-permute-start(bf16[24,1792]{1,0:T(8,128)(2,1)S(1)} %collective-permute-done.7.refs_5_.refs_2_), channel_id=1, source_target_pairs={{0,1},{1,0},{2,3},{3,2},{4,5},{5,4},{6,7},{7,6},{8,9},{9,8},{10,11... | collective-permute-start | bytes 258056 | tf_op jit(solution)/shard_map/ppermute | solution.py:175
  23.4 2.2 %collective-permute-start.9 = (bf16[24,1792]{1,0:T(8,128)(2,1)S(1)}, bf16[24,1792]{1,0:T(8,128)(2,1)S(1)}, u32[]{:S(2)}, u32[]{:S(2)}) collective-permute-start(bf16[24,1792]{1,0:T(8,128)(2,1)S(1)} %collective-permute-done.5.refs_3_.refs_4_), channel_id=1, source_target_pairs={{0,1},{1,0},{2,3},{3,2},{4,5},{5,4},{6,7},{7,6},{8,9},{9,8},{10,11... | collective-permute-start | bytes 258056 | tf_op jit(solution)/shard_map/ppermute | solution.py:175
  23.6 7.4 %collective-permute-start.16 = (bf16[24,3584]{1,0:T(8,128)(2,1)S(1)}, bf16[24,3584]{1,0:T(8,128)(2,1)S(1)}, u32[]{:S(2)}, u32[]{:S(2)}) collective-permute-start(bf16[24,3584]{1,0:T(8,128)(2,1)S(1)} %pad_maximum_fusion.2.refs_1_), channel_id=1, source_target_pairs={{0,1},{1,0},{2,3},{3,2},{4,5},{5,4},{6,7},{7,6},{8,9},{9,8},{10,11... | collective-permute-start | bytes 516104 | tf_op jit(solution)/shard_map/ppermute | solution.py:175
  24.0 6.5 %collective-permute-start.15 = (bf16[24,3584]{1,0:T(8,128)(2,1)S(1)}, bf16[24,3584]{1,0:T(8,128)(2,1)S(1)}, u32[]{:S(2)}, u32[]{:S(2)}) collective-permute-start(bf16[24,3584]{1,0:T(8,128)(2,1)S(1)} %pad_maximum_fusion.4.refs_3_), channel_id=1, source_target_pairs={{0,2},{1,3},{2,0},{3,1},{4,6},{5,7},{6,4},{7,5},{8,10},{9,11},{10,... | collective-permute-start | bytes 516104 | tf_op jit(solution)/shard_map/ppermute | solution.py:175
  26.1 6.7 %collective-permute-start.12 = (bf16[192,512]{1,0:T(8,128)(2,1)S(1)}, bf16[192,512]{1,0:T(8,128)(2,1)S(1)}, u32[]{:S(2)}, u32[]{:S(2)}) collective-permute-start(bf16[192,512]{1,0:T(8,128)(2,1)S(1)} %shard_map.66), channel_id=1, source_target_pairs={{0,16},{1,17},{2,18},{3,19},{4,20},{5,21},{6,22},{7,23},{8,24},{9,... | collective-permute-start | bytes 589832 | tf_op jit(solution)/shard_map/ppermute | solution.py:175
  27.7 3.4 %collective-permute-start.17 = (bf16[24,3584]{1,0:T(8,128)(2,1)S(1)}, bf16[24,3584]{1,0:T(8,128)(2,1)S(1)}, u32[]{:S(2)}, u32[]{:S(2)}) collective-permute-start(bf16[24,3584]{1,0:T(8,128)(2,1)S(1)} %pad_maximum_fusion.3.refs_2_), channel_id=1, source_target_pairs={{0,1},{1,0},{2,3},{3,2},{4,5},{5,4},{6,7},{7,6},{8,9},{9,8},{10,11... | collective-permute-start | bytes 516104 | tf_op jit(solution)/shard_map/ppermute | solution.py:175
  27.8 3.3 %collective-permute-start.18 = (bf16[24,3584]{1,0:T(8,128)(2,1)S(1)}, bf16[24,3584]{1,0:T(8,128)(2,1)S(1)}, u32[]{:S(2)}, u32[]{:S(2)}) collective-permute-start(bf16[24,3584]{1,0:T(8,128)(2,1)S(1)} %pad_maximum_fusion.4.refs_3_), channel_id=1, source_target_pairs={{0,1},{1,0},{2,3},{3,2},{4,5},{5,4},{6,7},{7,6},{8,9},{9,8},{10,11... | collective-permute-start | bytes 516104 | tf_op jit(solution)/shard_map/ppermute | solution.py:175
  30.5 2.3 %collective-permute-start.19 = (bf16[24,3584]{1,0:T(8,128)(2,1)S(1)}, bf16[24,3584]{1,0:T(8,128)(2,1)S(1)}, u32[]{:S(2)}, u32[]{:S(2)}) collective-permute-start(bf16[24,3584]{1,0:T(8,128)(2,1)S(1)} %collective-permute-done.15.refs_4_), channel_id=1, source_target_pairs={{0,1},{1,0},{2,3},{3,2},{4,5},{5,4},{6,7},{7,6},{8,9},{9,8},{10,11... | collective-permute-start | bytes 516104 | tf_op jit(solution)/shard_map/ppermute | solution.py:175

commit v4 on v3

--- a/solution.py
+++ b/solution.py
@@ -15,8 +15,8 @@
 
 
 def pack_kernel(cap, experts, me_ref, *refs):
-    sources, out_refs = refs[:4], refs[4 : 4 + experts]
-    held_refs, sems = refs[4 + experts : 8 + experts], refs[8 + experts]
+    sources, x_out_refs, dy_out_refs = refs[:4], refs[4 : 4 + experts], refs[4 + experts : -5]
+    held_refs, sems = refs[-5:-1], refs[-1]
     copies = [
         pltpu.make_async_copy(source, held, sems.at[i])
         for i, (source, held) in enumerate(zip(sources, held_refs))
@@ -62,24 +62,25 @@
     rows_dy = jnp.dot(select, pieces(grads_ref), preferred_element_type=jnp.float32)
     for k in range(experts):
         at = slice(k * height, (k + 1) * height)
-        both = jnp.concatenate([rows_x[at], rows_dy[at] * slot_scales[k]], axis=0)
-        out_refs[k][...] = both.astype(jnp.bfloat16)
+        x_out_refs[k][...] = rows_x[at].astype(jnp.bfloat16)
+        dy_out_refs[k][...] = (rows_dy[at] * slot_scales[k]).astype(jnp.bfloat16)
 
 
 def pack(tokens, out_grad, route_ids, route_weights, me_e, experts, cap):
     features = tokens.shape[1]
-    message = jax.ShapeDtypeStruct((2 * PIECES * cap, features // PIECES), jnp.bfloat16)
+    message = jax.ShapeDtypeStruct((PIECES * cap, features // PIECES), jnp.bfloat16)
     sources = (route_ids.T, route_weights.T, tokens, out_grad)
     held = [pltpu.VMEM(source.shape, source.dtype) for source in sources]
     sources = [pltpu.with_memory_space_constraint(source, pltpu.HBM) for source in sources]
-    return pl.pallas_call(
+    packed = pl.pallas_call(
         functools.partial(pack_kernel, cap, experts),
-        out_shape=[message] * experts,
+        out_shape=[message] * 2 * experts,
         in_specs=[pl.BlockSpec(memory_space=pltpu.SMEM)] + [pl.BlockSpec(memory_space=pl.ANY)] * 4,
-        out_specs=[pl.BlockSpec(memory_space=pltpu.VMEM)] * experts,
+        out_specs=[pl.BlockSpec(memory_space=pltpu.VMEM)] * 2 * experts,
         scratch_shapes=held + [pltpu.SemaphoreType.DMA((4,))],
         compiler_params=pltpu.CompilerParams(vmem_limit_bytes=16 * MIB),
     )(me_e.reshape(1), *sources)
+    return packed[:experts], packed[experts:]
 
 
 def project_kernel(n_weights, at_ref, *refs):
@@ -177,12 +178,14 @@
     def after(value, *others):
         return lax.optimization_barrier((value, *others))[0]
 
-    messages = pack(tokens, out_grad, route_ids, route_weights, me_e, experts, cap)
-    parts = {0: messages[0]}
-    for k in range(1, experts):
-        parts[k] = send(messages[k], 0, k, 0)
-
-    gate_from, up_from, _ = lax.optimization_barrier((gate_weight, up_weight, parts[1]))
+    packed_x, packed_dy = pack(tokens, out_grad, route_ids, route_weights, me_e, experts, cap)
+
+    def across_planes(packed):
+        return [packed[0]] + [send(packed[k], 0, k, 0) for k in range(1, experts)]
+
+    x_parts, dy_parts = across_planes(packed_x), across_planes(packed_dy)
+
+    gate_from, up_from, _ = lax.optimization_barrier((gate_weight, up_weight, x_parts[1]))
 
     def columns_for(by_d):
         at = (me_d + by_d) % n_dp * units
@@ -190,34 +193,30 @@
             [lax.dynamic_slice_in_dim(weight, at, units, 1) for weight in (gate_from, up_from)], axis=1
         )
 
-    def unfold(part, first):
+    def unfold(parts):
         return jnp.concatenate(
-            [part[(first + j) * cap : (first + j + 1) * cap] for j in range(PIECES)], axis=1
+            [
+                jnp.concatenate([part[j * cap : (j + 1) * cap] for j in range(PIECES)], axis=1)
+                for part in parts
+            ],
+            axis=0,
         )
 
-    def held(ks, first):
-        return jnp.concatenate([unfold(parts[k], first) for k in ks], axis=0)
-
-    def half(rows, by_d):
-        return lax.dynamic_slice_in_dim(rows, (me_d + by_d) % n_dp * depth, depth, 1)
+    held_x, held_dy = unfold(x_parts), unfold(dy_parts)
+
+    def half(by_d):
+        return lax.dynamic_slice_in_dim(held_x, (me_d + by_d) % n_dp * depth, depth, 1)
 
     next_chips = [(by_d, 0) for by_d in range(1, n_dp)] + [(0, 2)]
-    soon, late = range(experts // 2), range(experts // 2, experts)
-    soon_x, soon_dy = held(soon, 0), held(soon, PIECES)
-    early = {(by_d, by_q): send(soon_dy, by_d, 0, by_q) for by_d, by_q in next_chips}
-    late_x = after(held(late, 0), *early.values())
-    late_dy = after(held(late, PIECES), *early.values())
-    held_x = jnp.concatenate([soon_x, late_x], axis=0)
-    held_dy = jnp.concatenate([soon_dy, late_dy], axis=0)
-
-    x_blocks, dy_blocks = {(0, 0): half(held_x, 0)}, {(0, 0): held_dy}
+    x_blocks = {(0, 0): half(0)}
     for by_d in reversed(range(1, n_dp)):
-        x_blocks[by_d, 2] = send(half(held_x, by_d), by_d, 0, 2)
+        x_blocks[by_d, 2] = send(half(by_d), by_d, 0, 2)
     for by_d, by_q in next_chips:
-        x_blocks[by_d, by_q] = send(half(held_x, by_d), by_d, 0, by_q)
+        x_blocks[by_d, by_q] = send(half(by_d), by_d, 0, by_q)
+    ready_dy = after(held_dy, x_blocks[1, 0])
+    dy_blocks = {(0, 0): held_dy}
     for by_d, by_q in next_chips:
-        rows = send(late_dy, by_d, 0, by_q)
-        dy_blocks[by_d, by_q] = jnp.concatenate([early[by_d, by_q], rows], axis=0)
+        dy_blocks[by_d, by_q] = send(ready_dy, by_d, 0, by_q)
     for by_d in range(1, n_dp):
         dy_blocks[by_d, 2] = send(dy_blocks[by_d, 0], 0, 0, 2)
 

time: 34.5 us -> 33.2 us (0.962)
  local copies, waits for them, and re-layouts: 1.46 us -> 0.27 us
  starting transfers between devices: 19.7 us -> 20.6 us
  waiting for transfers between devices: 7.85 us -> 6.96 us
    dynamic_slice x1, local copies, waits for them, and re-layouts: 1.33 us -> 0.12 us  [columns_for(): lax.dynamic_slice_in_dim(weight, at, units, 1)]
    ppermute x20 -> x21, starting transfers between devices: 19.7 us -> 20.6 us  [send(): return lax.ppermute(value, AXES, pairs)]
    ppermute x20 -> x21, waiting for transfers between devices: 7.85 us -> 6.96 us  [send(): return lax.ppermute(value, AXES, pairs)]
  transfers between devices with their start and end apart: 20 -> 21, of which waited for: 7 -> 7; matrix products, arithmetic and copies ran while one was open for 5% -> 2% of each run, Pallas kernels for 3% -> 3%
where the time goes in v4:
time: 33.2 us; the launch traced here: 33 us
  starting transfers between devices  20.6 us (62%)
  waiting for transfers between devices  6.96 us (21%)
  Pallas kernels  4.65 us (14%)
    ppermute x21, starting transfers between devices, send(): return lax.ppermute(value, AXES, pairs)  20.6 us
    ppermute x21, waiting for transfers between devices, send(): return lax.ppermute(value, AXES, pairs)  6.96 us
    pallas_call x1, Pallas kernels, pack(): pl.pallas_call(functools.partial(pack_kernel, cap, experts), out_shape=[m...  1.99 us
    pallas_call x1, Pallas kernels, finish(): pl.pallas_call(functools.partial(finish_kernel, len(arrived), len(dy_bloc...  1.6 us
    pallas_call x2, Pallas kernels, project(): pl.pallas_call(functools.partial(project_kernel, len(weights)), out_shape...  1.05 us
  transfers between devices with their start and end apart: 21, of which 7 were waited for; matrix products, arithmetic and copies ran while one was open for 2% of the time, Pallas kernels for 3%

profile of v4, /device:TPU:0, one launch (start us, length us, event | category | flops | bytes accessed | tf_op | source)
XLA Modules:
  0.0 33.0 jit_solution(15272018292663838900)
XLA Ops:
  0.0 2.0 %shard_map.64 = (bf16[24,896]{1,0:T(8,128)(2,1)S(1)}, bf16[24,896]{1,0:T(8,128)(2,1)S(1)}, bf16[24,896]{1,0:T(8,128)(2,1)S(1)}, bf16[24,896]{1,0:T(8,128)(2,1)S(...) custom-call(s32[1]{0:T(128)} %bitcast.1.me_ref, ...), custom_call_target="tpu_custom_call" | custom-call | tf_op jit(solution)/shard_map/pallas_call | solution.py:75
  2.0 5.1 %collective-permute-start.2 = (bf16[24,896]{1,0:T(8,128)(2,1)S(1)}, bf16[24,896]{1,0:T(8,128)(2,1)S(1)}, u32[]{:S(2)}, u32[]{:S(2)}) collective-permute-start(bf16[24,896]{1,0:T(8,128)(2,1)S(1)} %get-tuple-element.19), channel_id=1, source_target_pairs={{0,12},{1,13},{2,14},{3,15},{4,8},{5,9},{6,10},{7,11},{8,4},{9,5},... | collective-permute-start | bytes 129032 | tf_op jit(solution)/shard_map/ppermute | solution.py:176
  7.1 0.6 %collective-permute-start = (bf16[24,896]{1,0:T(8,128)(2,1)S(1)}, bf16[24,896]{1,0:T(8,128)(2,1)S(1)}, u32[]{:S(2)}, u32[]{:S(2)}) collective-permute-start(bf16[24,896]{1,0:T(8,128)(2,1)S(1)} %get-tuple-element.17), channel_id=1, source_target_pairs={{0,4},{1,5},{2,6},{3,7},{4,0},{5,1},{6,2},{7,3},{8,12},{9,13},{10,... | collective-permute-start | bytes 129032 | tf_op jit(solution)/shard_map/ppermute | solution.py:176
  7.8 3.7 %collective-permute-start.13 = (bf16[24,896]{1,0:T(8,128)(2,1)S(1)}, bf16[24,896]{1,0:T(8,128)(2,1)S(1)}, u32[]{:S(2)}, u32[]{:S(2)}) collective-permute-start(bf16[24,896]{1,0:T(8,128)(2,1)S(1)} %get-tuple-element.25), channel_id=1, source_target_pairs={{0,12},{1,13},{2,14},{3,15},{4,8},{5,9},{6,10},{7,11},{8,4},{9,5},... | collective-permute-start | bytes 129032 | tf_op jit(solution)/shard_map/ppermute | solution.py:176
  11.6 0.0 copy-start.1
  11.6 0.0 collective-permute-done.2
  11.6 0.7 %collective-permute-start.11 = (bf16[24,896]{1,0:T(8,128)(2,1)S(1)}, bf16[24,896]{1,0:T(8,128)(2,1)S(1)}, u32[]{:S(2)}, u32[]{:S(2)}) collective-permute-start(bf16[24,896]{1,0:T(8,128)(2,1)S(1)} %get-tuple-element.23), channel_id=1, source_target_pairs={{0,4},{1,5},{2,6},{3,7},{4,0},{5,1},{6,2},{7,3},{8,12},{9,13},{10,... | collective-permute-start | bytes 129032 | tf_op jit(solution)/shard_map/ppermute | solution.py:176
  12.3 0.2 collective-permute-done.1
  12.6 0.1 maximum_maximum_fusion
  12.7 1.6 %collective-permute-start.4 = (bf16[24,1792]{1,0:T(8,128)(2,1)S(1)}, bf16[24,1792]{1,0:T(8,128)(2,1)S(1)}, u32[]{:S(2)}, u32[]{:S(2)}) collective-permute-start(bf16[24,1792]{1,0:T(8,128)(2,1)S(1)} %get-tuple-element.27), channel_id=1, source_target_pairs={{0,16},{1,17},{2,18},{3,19},{4,20},{5,21},{6,22},{7,23},{8,24},{9,... | collective-permute-start | bytes 258056 | tf_op jit(solution)/shard_map/ppermute | solution.py:176
  14.2 1.5 %collective-permute-start.5 = (bf16[24,1792]{1,0:T(8,128)(2,1)S(1)}, bf16[24,1792]{1,0:T(8,128)(2,1)S(1)}, u32[]{:S(2)}, u32[]{:S(2)}) collective-permute-start(bf16[24,1792]{1,0:T(8,128)(2,1)S(1)} %get-tuple-element.27), channel_id=1, source_target_pairs={{0,18},{1,19},{2,16},{3,17},{4,22},{5,23},{6,20},{7,21},{8,26},{9,... | collective-permute-start | bytes 258056 | tf_op jit(solution)/shard_map/ppermute | solution.py:176
  15.7 0.5 %collective-permute-start.3 = (bf16[24,1792]{1,0:T(8,128)(2,1)S(1)}, bf16[24,1792]{1,0:T(8,128)(2,1)S(1)}, u32[]{:S(2)}, u32[]{:S(2)}) collective-permute-start(bf16[24,1792]{1,0:T(8,128)(2,1)S(1)} %get-tuple-element.28.refs_2_.refs_3_), channel_id=1, source_target_pairs={{0,2},{1,3},{2,0},{3,1},{4,6},{5,7},{6,4},{7,5},{8,10},{9,11},{10,... | collective-permute-start | bytes 258056 | tf_op jit(solution)/shard_map/ppermute | solution.py:176
  16.3 0.2 collective-permute-done.12
  16.5 0.1 maximum_maximum_fusion.1.refs_1_
  16.6 1.0 %collective-permute-done.4.refs_4_.refs_1_ = bf16[24,1792]{1,0:T(8,128)(2,1)S(1)} collective-permute-done((bf16[24,1792]{1,0:T(8,128)(2,1)S(1)}, bf16[24,1792]{1,0:T(8,128)(2,1)S(1)}, u32[]{:S(2)}, u32[]{:S(2)}) %collective-permute-start.4) | collective-permute-done | bytes 86048 | tf_op jit(solution)/shard_map/ppermute | solution.py:176
  17.6 1.1 %collective-permute-start.15 = (bf16[24,3584]{1,0:T(8,128)(2,1)S(1)}, bf16[24,3584]{1,0:T(8,128)(2,1)S(1)}, u32[]{:S(2)}, u32[]{:S(2)}) collective-permute-start(bf16[24,3584]{1,0:T(8,128)(2,1)S(1)} %maximum_maximum_fusion.1.refs_1_), channel_id=1, source_target_pairs={{0,16},{1,17},{2,18},{3,19},{4,20},{5,21},{6,22},{7,23},{8,24},{9,... | collective-permute-start | bytes 516104 | tf_op jit(solution)/shard_map/ppermute | solution.py:176
  18.7 0.1 constant_dynamic-slice_fusion
  18.8 1.6 %collective-permute-start.14 = (bf16[24,3584]{1,0:T(8,128)(2,1)S(1)}, bf16[24,3584]{1,0:T(8,128)(2,1)S(1)}, u32[]{:S(2)}, u32[]{:S(2)}) collective-permute-start(bf16[24,3584]{1,0:T(8,128)(2,1)S(1)} %maximum_maximum_fusion.1.refs_1_), channel_id=1, source_target_pairs={{0,2},{1,3},{2,0},{3,1},{4,6},{5,7},{6,4},{7,5},{8,10},{9,11},{10,... | collective-permute-start | bytes 516104 | tf_op jit(solution)/shard_map/ppermute | solution.py:176
  20.4 0.1 collective-permute-done.3.refs_3_.refs_4_
  20.5 0.5 %collective-permute-start.7 = (bf16[24,1792]{1,0:T(8,128)(2,1)S(1)}, bf16[24,1792]{1,0:T(8,128)(2,1)S(1)}, u32[]{:S(2)}, u32[]{:S(2)}) collective-permute-start(bf16[24,1792]{1,0:T(8,128)(2,1)S(1)} %collective-permute-done.3.refs_3_.refs_4_), channel_id=1, source_target_pairs={{0,1},{1,0},{2,3},{3,2},{4,5},{5,4},{6,7},{7,6},{8,9},{9,8},{10,11... | collective-permute-start | bytes 258056 | tf_op jit(solution)/shard_map/ppermute | solution.py:176
  21.1 0.1 collective-permute-start.9
  21.1 2.3 %collective-permute-done.15.refs_3_ = bf16[24,3584]{1,0:T(8,128)(2,1)S(1)} collective-permute-done((bf16[24,3584]{1,0:T(8,128)(2,1)S(1)}, bf16[24,3584]{1,0:T(8,128)(2,1)S(1)}, u32[]{:S(2)}, u32[]{:S(2)}) %collective-permute-start.15) | collective-permute-done | bytes 172064 | tf_op jit(solution)/shard_map/ppermute | solution.py:176
  23.4 1.5 %collective-permute-start.16 = (bf16[24,3584]{1,0:T(8,128)(2,1)S(1)}, bf16[24,3584]{1,0:T(8,128)(2,1)S(1)}, u32[]{:S(2)}, u32[]{:S(2)}) collective-permute-start(bf16[24,3584]{1,0:T(8,128)(2,1)S(1)} %collective-permute-done.15.refs_3_), channel_id=1, source_target_pairs={{0,2},{1,3},{2,0},{3,1},{4,6},{5,7},{6,4},{7,5},{8,10},{9,11},{10,... | collective-permute-start | bytes 516104 | tf_op jit(solution)/shard_map/ppermute | solution.py:176
  25.0 0.1 pad_maximum_fusion.refs_0_
  25.1 0.5 %shard_map.66 = bf16[192,512]{1,0:T(8,128)(2,1)S(1)} custom-call(s32[1]{0:T(128)} %bitcast.at_ref, bf16[1792,512]{1,0:T(8,128)(2,1)S(1)} %pad_maximum_fusion.refs_0_, bf16[24,1792]{1,0:T(8,128)(2,1)S(1)} %collective-permute-done.4.refs_4_.refs_1_, bf16[24,1792]{1,0:T(8,128)(2,1)S(1)} %collective-permute-done.5.refs_5_.refs_2_, ...), custom_call_target="tpu_custom_call" | custom-call | flops 352321536 | bytes 2523136 | tf_op jit(solution)/shard_map/pallas_call | solution.py:105
  25.7 1.6 %collective-permute-start.10 = (bf16[192,512]{1,0:T(8,128)(2,1)S(1)}, bf16[192,512]{1,0:T(8,128)(2,1)S(1)}, u32[]{:S(2)}, u32[]{:S(2)}) collective-permute-start(bf16[192,512]{1,0:T(8,128)(2,1)S(1)} %shard_map.66), channel_id=1, source_target_pairs={{0,16},{1,17},{2,18},{3,19},{4,20},{5,21},{6,22},{7,23},{8,24},{9,... | collective-permute-start | bytes 589832 | tf_op jit(solution)/shard_map/ppermute | solution.py:176
  27.2 0.5 %collective-permute-start.19 = (bf16[24,3584]{1,0:T(8,128)(2,1)S(1)}, bf16[24,3584]{1,0:T(8,128)(2,1)S(1)}, u32[]{:S(2)}, u32[]{:S(2)}) collective-permute-start(bf16[24,3584]{1,0:T(8,128)(2,1)S(1)} %collective-permute-done.15.refs_3_), channel_id=1, source_target_pairs={{0,1},{1,0},{2,3},{3,2},{4,5},{5,4},{6,7},{7,6},{8,9},{9,8},{10,11... | collective-permute-start | bytes 516104 | tf_op jit(solution)/shard_map/ppermute | solution.py:176
  27.7 0.0 collective-permute-start.18
  27.8 1.1 %collective-permute-done.16.refs_4_ = bf16[24,3584]{1,0:T(8,128)(2,1)S(1)} collective-permute-done((bf16[24,3584]{1,0:T(8,128)(2,1)S(1)}, bf16[24,3584]{1,0:T(8,128)(2,1)S(1)}, u32[]{:S(2)}, u32[]{:S(2)}) %collective-permute-start.16) | collective-permute-done | bytes 172064 | tf_op jit(solution)/shard_map/ppermute | solution.py:176
  28.9 0.5 %shard_map.65.keep_ref = f32[192,512]{1,0:T(8,128)S(1)} custom-call(s32[1]{0:T(128)} %bitcast.at_ref, bf16[1792,512]{1,0:T(8,128)(2,1)S(1)} %copy-done, bf16[1792,512]{1,0:T(8,128)(2,1)S(1)} %copy-done.1, bf16[24,1792]{1,0:T(8,128)(2,1)S(1)} %get-tuple-element.28.refs_2_.refs_3_, bf16[24,1792]{1,0:T(8,128)(2,1)S(1)} %collective-permute-done.3.refs_3_.refs_4_, ...), custom_call_target="tpu_custom_call" | custom-call | flops 352321536 | bytes 2523136 | tf_op jit(solution)/shard_map/pallas_call | solution.py:105
  29.4 2.0 %collective-permute-done.10.refs_0_ = bf16[192,512]{1,0:T(8,128)(2,1)S(1)} collective-permute-done((bf16[192,512]{1,0:T(8,128)(2,1)S(1)}, bf16[192,512]{1,0:T(8,128)(2,1)S(1)}, u32[]{:S(2)}, u32[]{:S(2)}) %collective-permute-start.10) | collective-permute-done | bytes 196640 | tf_op jit(solution)/shard_map/ppermute | solution.py:176
  31.4 1.6 %shard_map.67 = bf16[256,3584]{1,0:T(8,128)(2,1)} custom-call(f32[192,512]{1,0:T(8,128)S(1)} %shard_map.65.keep_ref, bf16[192,512]{1,0:T(8,128)(2,1)S(1)} %collective-permute-done.10.refs_0_, bf16[24,3584]{1,0:T(8,128)(2,1)S(1)} %maximum_maximum_fusion.1.refs_1_, bf16[24,3584]{1,0:T(8,128)(2,1)S(1)} %collective-permute-done.14.refs_2_, ...), custom_call_target="tpu_custom_call" | custom-call | tf_op jit(solution)/shard_map/pallas_call | solution.py:146
  (30 shorter events, 0.2 us)
Async XLA Ops:
  0.0 18.7 %copy-start = (bf16[1792,512]{1,0:T(8,128)(2,1)S(1)}, bf16[1792,512]{1,0:T(8,128)(2,1)}, u32[]{:S(2)}) copy-start(bf16[1792,512]{1,0:T(8,128)(2,1)} %refs_0_.1) | copy-start | bytes 5505028
  2.0 9.6 %collective-permute-start.2 = (bf16[24,896]{1,0:T(8,128)(2,1)S(1)}, bf16[24,896]{1,0:T(8,128)(2,1)S(1)}, u32[]{:S(2)}, u32[]{:S(2)}) collective-permute-start(bf16[24,896]{1,0:T(8,128)(2,1)S(1)} %get-tuple-element.19), channel_id=1, source_target_pairs={{0,12},{1,13},{2,14},{3,15},{4,8},{5,9},{6,10},{7,11},{8,4},{9,5},... | collective-permute-start | bytes 129032 | tf_op jit(solution)/shard_map/ppermute | solution.py:176
  7.1 5.4 %collective-permute-start.1 = (bf16[24,896]{1,0:T(8,128)(2,1)S(1)}, bf16[24,896]{1,0:T(8,128)(2,1)S(1)}, u32[]{:S(2)}, u32[]{:S(2)}) collective-permute-start(bf16[24,896]{1,0:T(8,128)(2,1)S(1)} %get-tuple-element.18), channel_id=1, source_target_pairs={{0,8},{1,9},{2,10},{3,11},{4,12},{5,13},{6,14},{7,15},{8,0},{9,1},... | collective-permute-start | bytes 129032 | tf_op jit(solution)/shard_map/ppermute | solution.py:176
  7.1 5.4 %collective-permute-start = (bf16[24,896]{1,0:T(8,128)(2,1)S(1)}, bf16[24,896]{1,0:T(8,128)(2,1)S(1)}, u32[]{:S(2)}, u32[]{:S(2)}) collective-permute-start(bf16[24,896]{1,0:T(8,128)(2,1)S(1)} %get-tuple-element.17), channel_id=1, source_target_pairs={{0,4},{1,5},{2,6},{3,7},{4,0},{5,1},{6,2},{7,3},{8,12},{9,13},{10,... | collective-permute-start | bytes 129032 | tf_op jit(solution)/shard_map/ppermute | solution.py:176
  7.8 8.0 %collective-permute-start.13 = (bf16[24,896]{1,0:T(8,128)(2,1)S(1)}, bf16[24,896]{1,0:T(8,128)(2,1)S(1)}, u32[]{:S(2)}, u32[]{:S(2)}) collective-permute-start(bf16[24,896]{1,0:T(8,128)(2,1)S(1)} %get-tuple-element.25), channel_id=1, source_target_pairs={{0,12},{1,13},{2,14},{3,15},{4,8},{5,9},{6,10},{7,11},{8,4},{9,5},... | collective-permute-start | bytes 129032 | tf_op jit(solution)/shard_map/ppermute | solution.py:176
  11.5 4.9 %collective-permute-start.12 = (bf16[24,896]{1,0:T(8,128)(2,1)S(1)}, bf16[24,896]{1,0:T(8,128)(2,1)S(1)}, u32[]{:S(2)}, u32[]{:S(2)}) collective-permute-start(bf16[24,896]{1,0:T(8,128)(2,1)S(1)} %get-tuple-element.24), channel_id=1, source_target_pairs={{0,8},{1,9},{2,10},{3,11},{4,12},{5,13},{6,14},{7,15},{8,0},{9,1},... | collective-permute-start | bytes 129032 | tf_op jit(solution)/shard_map/ppermute | solution.py:176
  11.6 7.2 %copy-start.1 = (bf16[1792,512]{1,0:T(8,128)(2,1)S(1)}, bf16[1792,512]{1,0:T(8,128)(2,1)}, u32[]{:S(2)}) copy-start(bf16[1792,512]{1,0:T(8,128)(2,1)} %refs_1_.1) | copy-start | bytes 5505028
  11.6 4.9 %collective-permute-start.11 = (bf16[24,896]{1,0:T(8,128)(2,1)S(1)}, bf16[24,896]{1,0:T(8,128)(2,1)S(1)}, u32[]{:S(2)}, u32[]{:S(2)}) collective-permute-start(bf16[24,896]{1,0:T(8,128)(2,1)S(1)} %get-tuple-element.23), channel_id=1, source_target_pairs={{0,4},{1,5},{2,6},{3,7},{4,0},{5,1},{6,2},{7,3},{8,12},{9,13},{10,... | collective-permute-start | bytes 129032 | tf_op jit(solution)/shard_map/ppermute | solution.py:176
  12.7 4.9 %collective-permute-start.4 = (bf16[24,1792]{1,0:T(8,128)(2,1)S(1)}, bf16[24,1792]{1,0:T(8,128)(2,1)S(1)}, u32[]{:S(2)}, u32[]{:S(2)}) collective-permute-start(bf16[24,1792]{1,0:T(8,128)(2,1)S(1)} %get-tuple-element.27), channel_id=1, source_target_pairs={{0,16},{1,17},{2,18},{3,19},{4,20},{5,21},{6,22},{7,23},{8,24},{9,... | collective-permute-start | bytes 258056 | tf_op jit(solution)/shard_map/ppermute | solution.py:176
  14.2 6.3 %collective-permute-start.5 = (bf16[24,1792]{1,0:T(8,128)(2,1)S(1)}, bf16[24,1792]{1,0:T(8,128)(2,1)S(1)}, u32[]{:S(2)}, u32[]{:S(2)}) collective-permute-start(bf16[24,1792]{1,0:T(8,128)(2,1)S(1)} %get-tuple-element.27), channel_id=1, source_target_pairs={{0,18},{1,19},{2,16},{3,17},{4,22},{5,23},{6,20},{7,21},{8,26},{9,... | collective-permute-start | bytes 258056 | tf_op jit(solution)/shard_map/ppermute | solution.py:176
  15.7 4.8 %collective-permute-start.3 = (bf16[24,1792]{1,0:T(8,128)(2,1)S(1)}, bf16[24,1792]{1,0:T(8,128)(2,1)S(1)}, u32[]{:S(2)}, u32[]{:S(2)}) collective-permute-start(bf16[24,1792]{1,0:T(8,128)(2,1)S(1)} %get-tuple-element.28.refs_2_.refs_3_), channel_id=1, source_target_pairs={{0,2},{1,3},{2,0},{3,1},{4,6},{5,7},{6,4},{7,5},{8,10},{9,11},{10,... | collective-permute-start | bytes 258056 | tf_op jit(solution)/shard_map/ppermute | solution.py:176
  16.4 4.6 %collective-permute-start.6 = (bf16[24,1792]{1,0:T(8,128)(2,1)S(1)}, bf16[24,1792]{1,0:T(8,128)(2,1)S(1)}, u32[]{:S(2)}, u32[]{:S(2)}) collective-permute-start(bf16[24,1792]{1,0:T(8,128)(2,1)S(1)} %get-tuple-element.28.refs_2_.refs_3_), channel_id=1, source_target_pairs={{0,1},{1,0},{2,3},{3,2},{4,5},{5,4},{6,7},{7,6},{8,9},{9,8},{10,11... | collective-permute-start | bytes 258056 | tf_op jit(solution)/shard_map/ppermute | solution.py:176
  17.6 5.8 %collective-permute-start.15 = (bf16[24,3584]{1,0:T(8,128)(2,1)S(1)}, bf16[24,3584]{1,0:T(8,128)(2,1)S(1)}, u32[]{:S(2)}, u32[]{:S(2)}) collective-permute-start(bf16[24,3584]{1,0:T(8,128)(2,1)S(1)} %maximum_maximum_fusion.1.refs_1_), channel_id=1, source_target_pairs={{0,16},{1,17},{2,18},{3,19},{4,20},{5,21},{6,22},{7,23},{8,24},{9,... | collective-permute-start | bytes 516104 | tf_op jit(solution)/shard_map/ppermute | solution.py:176
  18.8 8.9 %collective-permute-start.14 = (bf16[24,3584]{1,0:T(8,128)(2,1)S(1)}, bf16[24,3584]{1,0:T(8,128)(2,1)S(1)}, u32[]{:S(2)}, u32[]{:S(2)}) collective-permute-start(bf16[24,3584]{1,0:T(8,128)(2,1)S(1)} %maximum_maximum_fusion.1.refs_1_), channel_id=1, source_target_pairs={{0,2},{1,3},{2,0},{3,1},{4,6},{5,7},{6,4},{7,5},{8,10},{9,11},{10,... | collective-permute-start | bytes 516104 | tf_op jit(solution)/shard_map/ppermute | solution.py:176
  20.5 4.6 %collective-permute-start.8 = (bf16[24,1792]{1,0:T(8,128)(2,1)S(1)}, bf16[24,1792]{1,0:T(8,128)(2,1)S(1)}, u32[]{:S(2)}, u32[]{:S(2)}) collective-permute-start(bf16[24,1792]{1,0:T(8,128)(2,1)S(1)} %collective-permute-done.4.refs_4_.refs_1_), channel_id=1, source_target_pairs={{0,1},{1,0},{2,3},{3,2},{4,5},{5,4},{6,7},{7,6},{8,9},{9,8},{10,11... | collective-permute-start | bytes 258056 | tf_op jit(solution)/shard_map/ppermute | solution.py:176
  20.5 4.6 %collective-permute-start.7 = (bf16[24,1792]{1,0:T(8,128)(2,1)S(1)}, bf16[24,1792]{1,0:T(8,128)(2,1)S(1)}, u32[]{:S(2)}, u32[]{:S(2)}) collective-permute-start(bf16[24,1792]{1,0:T(8,128)(2,1)S(1)} %collective-permute-done.3.refs_3_.refs_4_), channel_id=1, source_target_pairs={{0,1},{1,0},{2,3},{3,2},{4,5},{5,4},{6,7},{7,6},{8,9},{9,8},{10,11... | collective-permute-start | bytes 258056 | tf_op jit(solution)/shard_map/ppermute | solution.py:176
  21.1 4.1 %collective-permute-start.9 = (bf16[24,1792]{1,0:T(8,128)(2,1)S(1)}, bf16[24,1792]{1,0:T(8,128)(2,1)S(1)}, u32[]{:S(2)}, u32[]{:S(2)}) collective-permute-start(bf16[24,1792]{1,0:T(8,128)(2,1)S(1)} %collective-permute-done.5.refs_5_.refs_2_), channel_id=1, source_target_pairs={{0,1},{1,0},{2,3},{3,2},{4,5},{5,4},{6,7},{7,6},{8,9},{9,8},{10,11... | collective-permute-start | bytes 258056 | tf_op jit(solution)/shard_map/ppermute | solution.py:176
  23.4 5.4 %collective-permute-start.16 = (bf16[24,3584]{1,0:T(8,128)(2,1)S(1)}, bf16[24,3584]{1,0:T(8,128)(2,1)S(1)}, u32[]{:S(2)}, u32[]{:S(2)}) collective-permute-start(bf16[24,3584]{1,0:T(8,128)(2,1)S(1)} %collective-permute-done.15.refs_3_), channel_id=1, source_target_pairs={{0,2},{1,3},{2,0},{3,1},{4,6},{5,7},{6,4},{7,5},{8,10},{9,11},{10,... | collective-permute-start | bytes 516104 | tf_op jit(solution)/shard_map/ppermute | solution.py:176
  25.7 5.7 %collective-permute-start.10 = (bf16[192,512]{1,0:T(8,128)(2,1)S(1)}, bf16[192,512]{1,0:T(8,128)(2,1)S(1)}, u32[]{:S(2)}, u32[]{:S(2)}) collective-permute-start(bf16[192,512]{1,0:T(8,128)(2,1)S(1)} %shard_map.66), channel_id=1, source_target_pairs={{0,16},{1,17},{2,18},{3,19},{4,20},{5,21},{6,22},{7,23},{8,24},{9,... | collective-permute-start | bytes 589832 | tf_op jit(solution)/shard_map/ppermute | solution.py:176
  27.2 2.2 %collective-permute-start.17 = (bf16[24,3584]{1,0:T(8,128)(2,1)S(1)}, bf16[24,3584]{1,0:T(8,128)(2,1)S(1)}, u32[]{:S(2)}, u32[]{:S(2)}) collective-permute-start(bf16[24,3584]{1,0:T(8,128)(2,1)S(1)} %maximum_maximum_fusion.1.refs_1_), channel_id=1, source_target_pairs={{0,1},{1,0},{2,3},{3,2},{4,5},{5,4},{6,7},{7,6},{8,9},{9,8},{10,11... | collective-permute-start | bytes 516104 | tf_op jit(solution)/shard_map/ppermute | solution.py:176
  27.2 4.2 %collective-permute-start.19 = (bf16[24,3584]{1,0:T(8,128)(2,1)S(1)}, bf16[24,3584]{1,0:T(8,128)(2,1)S(1)}, u32[]{:S(2)}, u32[]{:S(2)}) collective-permute-start(bf16[24,3584]{1,0:T(8,128)(2,1)S(1)} %collective-permute-done.15.refs_3_), channel_id=1, source_target_pairs={{0,1},{1,0},{2,3},{3,2},{4,5},{5,4},{6,7},{7,6},{8,9},{9,8},{10,11... | collective-permute-start | bytes 516104 | tf_op jit(solution)/shard_map/ppermute | solution.py:176
  27.7 3.7 %collective-permute-start.18 = (bf16[24,3584]{1,0:T(8,128)(2,1)S(1)}, bf16[24,3584]{1,0:T(8,128)(2,1)S(1)}, u32[]{:S(2)}, u32[]{:S(2)}) collective-permute-start(bf16[24,3584]{1,0:T(8,128)(2,1)S(1)} %collective-permute-done.14.refs_2_), channel_id=1, source_target_pairs={{0,1},{1,0},{2,3},{3,2},{4,5},{5,4},{6,7},{7,6},{8,9},{9,8},{10,11... | collective-permute-start | bytes 516104 | tf_op jit(solution)/shard_map/ppermute | solution.py:176
  28.9 2.6 %collective-permute-start.20 = (bf16[24,3584]{1,0:T(8,128)(2,1)S(1)}, bf16[24,3584]{1,0:T(8,128)(2,1)S(1)}, u32[]{:S(2)}, u32[]{:S(2)}) collective-permute-start(bf16[24,3584]{1,0:T(8,128)(2,1)S(1)} %collective-permute-done.16.refs_4_), channel_id=1, source_target_pairs={{0,1},{1,0},{2,3},{3,2},{4,5},{5,4},{6,7},{7,6},{8,9},{9,8},{10,11... | collective-permute-start | bytes 516104 | tf_op jit(solution)/shard_map/ppermute | solution.py:176

commit v5 on v4

--- a/solution.py
+++ b/solution.py
@@ -21,18 +21,16 @@
         pltpu.make_async_copy(source, held, sems.at[i])
         for i, (source, held) in enumerate(zip(sources, held_refs))
     ]
-    for copy in copies:
-        copy.start()
+    for i in (0, 2, 1, 3):
+        copies[i].start()
     ids_ref, weights_ref, tokens_ref, grads_ref = held_refs
     rows, width = tokens_ref.shape[0], tokens_ref.shape[1] // PIECES
     copies[0].wait()
-    copies[1].wait()
-    ids, weights = ids_ref[...], weights_ref[...]
-    chosen, scales = [], []
-    for k in range(experts):
-        match = ids == (me_ref[0] ^ k)
-        chosen.append(jnp.max(jnp.where(match, 1.0, 0.0), axis=0, keepdims=True))
-        scales.append(jnp.sum(jnp.where(match, weights, 0.0), axis=0, keepdims=True))
+    ids = ids_ref[...]
+    matches, chosen = [], []
+    for k in range(experts):
+        matches.append(ids == (me_ref[0] ^ k))
+        chosen.append(jnp.max(jnp.where(matches[k], 1.0, 0.0), axis=0, keepdims=True))
     flags = jnp.concatenate(chosen, axis=0)
     before = lax.broadcasted_iota(jnp.int32, (rows, rows), 0)
     after = lax.broadcasted_iota(jnp.int32, (rows, rows), 1)
@@ -41,12 +39,10 @@
     height = PIECES * cap
     row = lax.broadcasted_iota(jnp.int32, (height, rows), 0)
     piece, slot = row // cap, row % cap
-    picks, slot_scales = [], []
+    picks = []
     for k in range(experts):
         place = jnp.where(chosen[k] > 0.0, rank[k : k + 1], 0.0).astype(jnp.int32)
-        pick = place == slot + 1
-        picks.append(jnp.where(pick, 1.0, 0.0))
-        slot_scales.append(jnp.sum(jnp.where(pick, scales[k], 0.0), axis=1, keepdims=True))
+        picks.append(jnp.where(place == slot + 1, 1.0, 0.0))
     pick_all = jnp.concatenate(picks, axis=0)
     piece_all = jnp.concatenate([piece] * experts, axis=0)
     select = jnp.concatenate(
@@ -58,6 +54,12 @@
 
     copies[2].wait()
     rows_x = jnp.dot(select, pieces(tokens_ref), preferred_element_type=jnp.float32)
+    copies[1].wait()
+    weights = weights_ref[...]
+    slot_scales = []
+    for k in range(experts):
+        scale = jnp.sum(jnp.where(matches[k], weights, 0.0), axis=0, keepdims=True)
+        slot_scales.append(jnp.sum(jnp.where(picks[k] > 0.0, scale, 0.0), axis=1, keepdims=True))
     copies[3].wait()
     rows_dy = jnp.dot(select, pieces(grads_ref), preferred_element_type=jnp.float32)
     for k in range(experts):

time: 33.2 us -> 33.3 us (level)
  no operation moved by 1% of the time
where the time goes in v5:
time: 33.3 us; the launch traced here: 33.1 us
  starting transfers between devices  20.6 us (62%)
  waiting for transfers between devices  6.96 us (21%)
  Pallas kernels  4.73 us (14%)
    ppermute x21, starting transfers between devices, send(): return lax.ppermute(value, AXES, pairs)  20.6 us
    ppermute x21, waiting for transfers between devices, send(): return lax.ppermute(value, AXES, pairs)  6.96 us
    pallas_call x1, Pallas kernels, pack(): pl.pallas_call(functools.partial(pack_kernel, cap, experts), out_shape=[m...  2.07 us
    pallas_call x1, Pallas kernels, finish(): pl.pallas_call(functools.partial(finish_kernel, len(arrived), len(dy_bloc...  1.61 us
    pallas_call x2, Pallas kernels, project(): pl.pallas_call(functools.partial(project_kernel, len(weights)), out_shape...  1.05 us
  transfers between devices with their start and end apart: 21, of which 7 were waited for; matrix products, arithmetic and copies ran while one was open for 2% of the time, Pallas kernels for 3%

profile of v5, /device:TPU:0, one launch (start us, length us, event | category | flops | bytes accessed | tf_op | source)
XLA Modules:
  0.0 33.1 jit_solution(6162195783509169331)
XLA Ops:
  0.0 2.1 %shard_map.64 = (bf16[24,896]{1,0:T(8,128)(2,1)S(1)}, bf16[24,896]{1,0:T(8,128)(2,1)S(1)}, bf16[24,896]{1,0:T(8,128)(2,1)S(1)}, bf16[24,896]{1,0:T(8,128)(2,1)S(...) custom-call(s32[1]{0:T(128)} %bitcast.1.me_ref, ...), custom_call_target="tpu_custom_call" | custom-call | tf_op jit(solution)/shard_map/pallas_call | solution.py:77
  2.1 5.1 %collective-permute-start.2 = (bf16[24,896]{1,0:T(8,128)(2,1)S(1)}, bf16[24,896]{1,0:T(8,128)(2,1)S(1)}, u32[]{:S(2)}, u32[]{:S(2)}) collective-permute-start(bf16[24,896]{1,0:T(8,128)(2,1)S(1)} %get-tuple-element.19), channel_id=1, source_target_pairs={{0,12},{1,13},{2,14},{3,15},{4,8},{5,9},{6,10},{7,11},{8,4},{9,5},... | collective-permute-start | bytes 129032 | tf_op jit(solution)/shard_map/ppermute | solution.py:178
  7.2 0.6 %collective-permute-start = (bf16[24,896]{1,0:T(8,128)(2,1)S(1)}, bf16[24,896]{1,0:T(8,128)(2,1)S(1)}, u32[]{:S(2)}, u32[]{:S(2)}) collective-permute-start(bf16[24,896]{1,0:T(8,128)(2,1)S(1)} %get-tuple-element.17), channel_id=1, source_target_pairs={{0,4},{1,5},{2,6},{3,7},{4,0},{5,1},{6,2},{7,3},{8,12},{9,13},{10,... | collective-permute-start | bytes 129032 | tf_op jit(solution)/shard_map/ppermute | solution.py:178
  7.8 3.7 %collective-permute-start.13 = (bf16[24,896]{1,0:T(8,128)(2,1)S(1)}, bf16[24,896]{1,0:T(8,128)(2,1)S(1)}, u32[]{:S(2)}, u32[]{:S(2)}) collective-permute-start(bf16[24,896]{1,0:T(8,128)(2,1)S(1)} %get-tuple-element.25), channel_id=1, source_target_pairs={{0,12},{1,13},{2,14},{3,15},{4,8},{5,9},{6,10},{7,11},{8,4},{9,5},... | collective-permute-start | bytes 129032 | tf_op jit(solution)/shard_map/ppermute | solution.py:178
  11.7 0.0 copy-start.1
  11.7 0.0 collective-permute-done.2
  11.7 0.7 %collective-permute-start.11 = (bf16[24,896]{1,0:T(8,128)(2,1)S(1)}, bf16[24,896]{1,0:T(8,128)(2,1)S(1)}, u32[]{:S(2)}, u32[]{:S(2)}) collective-permute-start(bf16[24,896]{1,0:T(8,128)(2,1)S(1)} %get-tuple-element.23), channel_id=1, source_target_pairs={{0,4},{1,5},{2,6},{3,7},{4,0},{5,1},{6,2},{7,3},{8,12},{9,13},{10,... | collective-permute-start | bytes 129032 | tf_op jit(solution)/shard_map/ppermute | solution.py:178
  12.4 0.2 collective-permute-done.1
  12.6 0.1 maximum_maximum_fusion
  12.8 1.6 %collective-permute-start.4 = (bf16[24,1792]{1,0:T(8,128)(2,1)S(1)}, bf16[24,1792]{1,0:T(8,128)(2,1)S(1)}, u32[]{:S(2)}, u32[]{:S(2)}) collective-permute-start(bf16[24,1792]{1,0:T(8,128)(2,1)S(1)} %get-tuple-element.27), channel_id=1, source_target_pairs={{0,16},{1,17},{2,18},{3,19},{4,20},{5,21},{6,22},{7,23},{8,24},{9,... | collective-permute-start | bytes 258056 | tf_op jit(solution)/shard_map/ppermute | solution.py:178
  14.3 1.5 %collective-permute-start.5 = (bf16[24,1792]{1,0:T(8,128)(2,1)S(1)}, bf16[24,1792]{1,0:T(8,128)(2,1)S(1)}, u32[]{:S(2)}, u32[]{:S(2)}) collective-permute-start(bf16[24,1792]{1,0:T(8,128)(2,1)S(1)} %get-tuple-element.27), channel_id=1, source_target_pairs={{0,18},{1,19},{2,16},{3,17},{4,22},{5,23},{6,20},{7,21},{8,26},{9,... | collective-permute-start | bytes 258056 | tf_op jit(solution)/shard_map/ppermute | solution.py:178
  15.8 0.5 %collective-permute-start.3 = (bf16[24,1792]{1,0:T(8,128)(2,1)S(1)}, bf16[24,1792]{1,0:T(8,128)(2,1)S(1)}, u32[]{:S(2)}, u32[]{:S(2)}) collective-permute-start(bf16[24,1792]{1,0:T(8,128)(2,1)S(1)} %get-tuple-element.28.refs_2_.refs_3_), channel_id=1, source_target_pairs={{0,2},{1,3},{2,0},{3,1},{4,6},{5,7},{6,4},{7,5},{8,10},{9,11},{10,... | collective-permute-start | bytes 258056 | tf_op jit(solution)/shard_map/ppermute | solution.py:178
  16.3 0.2 collective-permute-done.12
  16.6 0.1 maximum_maximum_fusion.1.refs_1_
  16.7 1.0 %collective-permute-done.4.refs_4_.refs_1_ = bf16[24,1792]{1,0:T(8,128)(2,1)S(1)} collective-permute-done((bf16[24,1792]{1,0:T(8,128)(2,1)S(1)}, bf16[24,1792]{1,0:T(8,128)(2,1)S(1)}, u32[]{:S(2)}, u32[]{:S(2)}) %collective-permute-start.4) | collective-permute-done | bytes 86048 | tf_op jit(solution)/shard_map/ppermute | solution.py:178
  17.7 1.1 %collective-permute-start.15 = (bf16[24,3584]{1,0:T(8,128)(2,1)S(1)}, bf16[24,3584]{1,0:T(8,128)(2,1)S(1)}, u32[]{:S(2)}, u32[]{:S(2)}) collective-permute-start(bf16[24,3584]{1,0:T(8,128)(2,1)S(1)} %maximum_maximum_fusion.1.refs_1_), channel_id=1, source_target_pairs={{0,16},{1,17},{2,18},{3,19},{4,20},{5,21},{6,22},{7,23},{8,24},{9,... | collective-permute-start | bytes 516104 | tf_op jit(solution)/shard_map/ppermute | solution.py:178
  18.8 0.1 constant_dynamic-slice_fusion
  18.9 1.6 %collective-permute-start.14 = (bf16[24,3584]{1,0:T(8,128)(2,1)S(1)}, bf16[24,3584]{1,0:T(8,128)(2,1)S(1)}, u32[]{:S(2)}, u32[]{:S(2)}) collective-permute-start(bf16[24,3584]{1,0:T(8,128)(2,1)S(1)} %maximum_maximum_fusion.1.refs_1_), channel_id=1, source_target_pairs={{0,2},{1,3},{2,0},{3,1},{4,6},{5,7},{6,4},{7,5},{8,10},{9,11},{10,... | collective-permute-start | bytes 516104 | tf_op jit(solution)/shard_map/ppermute | solution.py:178
  20.5 0.1 collective-permute-done.3.refs_3_.refs_4_
  20.6 0.5 %collective-permute-start.7 = (bf16[24,1792]{1,0:T(8,128)(2,1)S(1)}, bf16[24,1792]{1,0:T(8,128)(2,1)S(1)}, u32[]{:S(2)}, u32[]{:S(2)}) collective-permute-start(bf16[24,1792]{1,0:T(8,128)(2,1)S(1)} %collective-permute-done.3.refs_3_.refs_4_), channel_id=1, source_target_pairs={{0,1},{1,0},{2,3},{3,2},{4,5},{5,4},{6,7},{7,6},{8,9},{9,8},{10,11... | collective-permute-start | bytes 258056 | tf_op jit(solution)/shard_map/ppermute | solution.py:178
  21.1 0.1 collective-permute-start.9
  21.2 2.3 %collective-permute-done.15.refs_3_ = bf16[24,3584]{1,0:T(8,128)(2,1)S(1)} collective-permute-done((bf16[24,3584]{1,0:T(8,128)(2,1)S(1)}, bf16[24,3584]{1,0:T(8,128)(2,1)S(1)}, u32[]{:S(2)}, u32[]{:S(2)}) %collective-permute-start.15) | collective-permute-done | bytes 172064 | tf_op jit(solution)/shard_map/ppermute | solution.py:178
  23.5 1.5 %collective-permute-start.16 = (bf16[24,3584]{1,0:T(8,128)(2,1)S(1)}, bf16[24,3584]{1,0:T(8,128)(2,1)S(1)}, u32[]{:S(2)}, u32[]{:S(2)}) collective-permute-start(bf16[24,3584]{1,0:T(8,128)(2,1)S(1)} %collective-permute-done.15.refs_3_), channel_id=1, source_target_pairs={{0,2},{1,3},{2,0},{3,1},{4,6},{5,7},{6,4},{7,5},{8,10},{9,11},{10,... | collective-permute-start | bytes 516104 | tf_op jit(solution)/shard_map/ppermute | solution.py:178
  25.0 0.1 pad_maximum_fusion.refs_0_
  25.2 0.5 %shard_map.66 = bf16[192,512]{1,0:T(8,128)(2,1)S(1)} custom-call(s32[1]{0:T(128)} %bitcast.at_ref, bf16[1792,512]{1,0:T(8,128)(2,1)S(1)} %pad_maximum_fusion.refs_0_, bf16[24,1792]{1,0:T(8,128)(2,1)S(1)} %collective-permute-done.4.refs_4_.refs_1_, bf16[24,1792]{1,0:T(8,128)(2,1)S(1)} %collective-permute-done.5.refs_5_.refs_2_, ...), custom_call_target="tpu_custom_call" | custom-call | flops 352321536 | bytes 2523136 | tf_op jit(solution)/shard_map/pallas_call | solution.py:107
  25.8 1.6 %collective-permute-start.10 = (bf16[192,512]{1,0:T(8,128)(2,1)S(1)}, bf16[192,512]{1,0:T(8,128)(2,1)S(1)}, u32[]{:S(2)}, u32[]{:S(2)}) collective-permute-start(bf16[192,512]{1,0:T(8,128)(2,1)S(1)} %shard_map.66), channel_id=1, source_target_pairs={{0,16},{1,17},{2,18},{3,19},{4,20},{5,21},{6,22},{7,23},{8,24},{9,... | collective-permute-start | bytes 589832 | tf_op jit(solution)/shard_map/ppermute | solution.py:178
  27.3 0.5 %collective-permute-start.19 = (bf16[24,3584]{1,0:T(8,128)(2,1)S(1)}, bf16[24,3584]{1,0:T(8,128)(2,1)S(1)}, u32[]{:S(2)}, u32[]{:S(2)}) collective-permute-start(bf16[24,3584]{1,0:T(8,128)(2,1)S(1)} %collective-permute-done.15.refs_3_), channel_id=1, source_target_pairs={{0,1},{1,0},{2,3},{3,2},{4,5},{5,4},{6,7},{7,6},{8,9},{9,8},{10,11... | collective-permute-start | bytes 516104 | tf_op jit(solution)/shard_map/ppermute | solution.py:178
  27.8 0.0 collective-permute-start.18
  27.8 1.1 %collective-permute-done.16.refs_4_ = bf16[24,3584]{1,0:T(8,128)(2,1)S(1)} collective-permute-done((bf16[24,3584]{1,0:T(8,128)(2,1)S(1)}, bf16[24,3584]{1,0:T(8,128)(2,1)S(1)}, u32[]{:S(2)}, u32[]{:S(2)}) %collective-permute-start.16) | collective-permute-done | bytes 172064 | tf_op jit(solution)/shard_map/ppermute | solution.py:178
  28.9 0.5 %shard_map.65.keep_ref = f32[192,512]{1,0:T(8,128)S(1)} custom-call(s32[1]{0:T(128)} %bitcast.at_ref, bf16[1792,512]{1,0:T(8,128)(2,1)S(1)} %copy-done, bf16[1792,512]{1,0:T(8,128)(2,1)S(1)} %copy-done.1, bf16[24,1792]{1,0:T(8,128)(2,1)S(1)} %get-tuple-element.28.refs_2_.refs_3_, bf16[24,1792]{1,0:T(8,128)(2,1)S(1)} %collective-permute-done.3.refs_3_.refs_4_, ...), custom_call_target="tpu_custom_call" | custom-call | flops 352321536 | bytes 2523136 | tf_op jit(solution)/shard_map/pallas_call | solution.py:107
  29.5 2.0 %collective-permute-done.10.refs_0_ = bf16[192,512]{1,0:T(8,128)(2,1)S(1)} collective-permute-done((bf16[192,512]{1,0:T(8,128)(2,1)S(1)}, bf16[192,512]{1,0:T(8,128)(2,1)S(1)}, u32[]{:S(2)}, u32[]{:S(2)}) %collective-permute-start.10) | collective-permute-done | bytes 196640 | tf_op jit(solution)/shard_map/ppermute | solution.py:178
  31.5 1.6 %shard_map.67 = bf16[256,3584]{1,0:T(8,128)(2,1)} custom-call(f32[192,512]{1,0:T(8,128)S(1)} %shard_map.65.keep_ref, bf16[192,512]{1,0:T(8,128)(2,1)S(1)} %collective-permute-done.10.refs_0_, bf16[24,3584]{1,0:T(8,128)(2,1)S(1)} %maximum_maximum_fusion.1.refs_1_, bf16[24,3584]{1,0:T(8,128)(2,1)S(1)} %collective-permute-done.14.refs_2_, ...), custom_call_target="tpu_custom_call" | custom-call | tf_op jit(solution)/shard_map/pallas_call | solution.py:148
  (30 shorter events, 0.2 us)
Async XLA Ops:
  0.0 18.8 %copy-start = (bf16[1792,512]{1,0:T(8,128)(2,1)S(1)}, bf16[1792,512]{1,0:T(8,128)(2,1)}, u32[]{:S(2)}) copy-start(bf16[1792,512]{1,0:T(8,128)(2,1)} %refs_0_.1) | copy-start | bytes 5505028
  2.1 9.6 %collective-permute-start.2 = (bf16[24,896]{1,0:T(8,128)(2,1)S(1)}, bf16[24,896]{1,0:T(8,128)(2,1)S(1)}, u32[]{:S(2)}, u32[]{:S(2)}) collective-permute-start(bf16[24,896]{1,0:T(8,128)(2,1)S(1)} %get-tuple-element.19), channel_id=1, source_target_pairs={{0,12},{1,13},{2,14},{3,15},{4,8},{5,9},{6,10},{7,11},{8,4},{9,5},... | collective-permute-start | bytes 129032 | tf_op jit(solution)/shard_map/ppermute | solution.py:178
  7.2 5.4 %collective-permute-start.1 = (bf16[24,896]{1,0:T(8,128)(2,1)S(1)}, bf16[24,896]{1,0:T(8,128)(2,1)S(1)}, u32[]{:S(2)}, u32[]{:S(2)}) collective-permute-start(bf16[24,896]{1,0:T(8,128)(2,1)S(1)} %get-tuple-element.18), channel_id=1, source_target_pairs={{0,8},{1,9},{2,10},{3,11},{4,12},{5,13},{6,14},{7,15},{8,0},{9,1},... | collective-permute-start | bytes 129032 | tf_op jit(solution)/shard_map/ppermute | solution.py:178
  7.2 5.4 %collective-permute-start = (bf16[24,896]{1,0:T(8,128)(2,1)S(1)}, bf16[24,896]{1,0:T(8,128)(2,1)S(1)}, u32[]{:S(2)}, u32[]{:S(2)}) collective-permute-start(bf16[24,896]{1,0:T(8,128)(2,1)S(1)} %get-tuple-element.17), channel_id=1, source_target_pairs={{0,4},{1,5},{2,6},{3,7},{4,0},{5,1},{6,2},{7,3},{8,12},{9,13},{10,... | collective-permute-start | bytes 129032 | tf_op jit(solution)/shard_map/ppermute | solution.py:178
  7.8 8.0 %collective-permute-start.13 = (bf16[24,896]{1,0:T(8,128)(2,1)S(1)}, bf16[24,896]{1,0:T(8,128)(2,1)S(1)}, u32[]{:S(2)}, u32[]{:S(2)}) collective-permute-start(bf16[24,896]{1,0:T(8,128)(2,1)S(1)} %get-tuple-element.25), channel_id=1, source_target_pairs={{0,12},{1,13},{2,14},{3,15},{4,8},{5,9},{6,10},{7,11},{8,4},{9,5},... | collective-permute-start | bytes 129032 | tf_op jit(solution)/shard_map/ppermute | solution.py:178
  11.6 4.9 %collective-permute-start.12 = (bf16[24,896]{1,0:T(8,128)(2,1)S(1)}, bf16[24,896]{1,0:T(8,128)(2,1)S(1)}, u32[]{:S(2)}, u32[]{:S(2)}) collective-permute-start(bf16[24,896]{1,0:T(8,128)(2,1)S(1)} %get-tuple-element.24), channel_id=1, source_target_pairs={{0,8},{1,9},{2,10},{3,11},{4,12},{5,13},{6,14},{7,15},{8,0},{9,1},... | collective-permute-start | bytes 129032 | tf_op jit(solution)/shard_map/ppermute | solution.py:178
  11.7 7.2 %copy-start.1 = (bf16[1792,512]{1,0:T(8,128)(2,1)S(1)}, bf16[1792,512]{1,0:T(8,128)(2,1)}, u32[]{:S(2)}) copy-start(bf16[1792,512]{1,0:T(8,128)(2,1)} %refs_1_.1) | copy-start | bytes 5505028
  11.7 4.9 %collective-permute-start.11 = (bf16[24,896]{1,0:T(8,128)(2,1)S(1)}, bf16[24,896]{1,0:T(8,128)(2,1)S(1)}, u32[]{:S(2)}, u32[]{:S(2)}) collective-permute-start(bf16[24,896]{1,0:T(8,128)(2,1)S(1)} %get-tuple-element.23), channel_id=1, source_target_pairs={{0,4},{1,5},{2,6},{3,7},{4,0},{5,1},{6,2},{7,3},{8,12},{9,13},{10,... | collective-permute-start | bytes 129032 | tf_op jit(solution)/shard_map/ppermute | solution.py:178
  12.8 4.9 %collective-permute-start.4 = (bf16[24,1792]{1,0:T(8,128)(2,1)S(1)}, bf16[24,1792]{1,0:T(8,128)(2,1)S(1)}, u32[]{:S(2)}, u32[]{:S(2)}) collective-permute-start(bf16[24,1792]{1,0:T(8,128)(2,1)S(1)} %get-tuple-element.27), channel_id=1, source_target_pairs={{0,16},{1,17},{2,18},{3,19},{4,20},{5,21},{6,22},{7,23},{8,24},{9,... | collective-permute-start | bytes 258056 | tf_op jit(solution)/shard_map/ppermute | solution.py:178
  14.3 6.3 %collective-permute-start.5 = (bf16[24,1792]{1,0:T(8,128)(2,1)S(1)}, bf16[24,1792]{1,0:T(8,128)(2,1)S(1)}, u32[]{:S(2)}, u32[]{:S(2)}) collective-permute-start(bf16[24,1792]{1,0:T(8,128)(2,1)S(1)} %get-tuple-element.27), channel_id=1, source_target_pairs={{0,18},{1,19},{2,16},{3,17},{4,22},{5,23},{6,20},{7,21},{8,26},{9,... | collective-permute-start | bytes 258056 | tf_op jit(solution)/shard_map/ppermute | solution.py:178
  15.8 4.8 %collective-permute-start.3 = (bf16[24,1792]{1,0:T(8,128)(2,1)S(1)}, bf16[24,1792]{1,0:T(8,128)(2,1)S(1)}, u32[]{:S(2)}, u32[]{:S(2)}) collective-permute-start(bf16[24,1792]{1,0:T(8,128)(2,1)S(1)} %get-tuple-element.28.refs_2_.refs_3_), channel_id=1, source_target_pairs={{0,2},{1,3},{2,0},{3,1},{4,6},{5,7},{6,4},{7,5},{8,10},{9,11},{10,... | collective-permute-start | bytes 258056 | tf_op jit(solution)/shard_map/ppermute | solution.py:178
  16.5 4.6 %collective-permute-start.6 = (bf16[24,1792]{1,0:T(8,128)(2,1)S(1)}, bf16[24,1792]{1,0:T(8,128)(2,1)S(1)}, u32[]{:S(2)}, u32[]{:S(2)}) collective-permute-start(bf16[24,1792]{1,0:T(8,128)(2,1)S(1)} %get-tuple-element.28.refs_2_.refs_3_), channel_id=1, source_target_pairs={{0,1},{1,0},{2,3},{3,2},{4,5},{5,4},{6,7},{7,6},{8,9},{9,8},{10,11... | collective-permute-start | bytes 258056 | tf_op jit(solution)/shard_map/ppermute | solution.py:178
  17.7 5.8 %collective-permute-start.15 = (bf16[24,3584]{1,0:T(8,128)(2,1)S(1)}, bf16[24,3584]{1,0:T(8,128)(2,1)S(1)}, u32[]{:S(2)}, u32[]{:S(2)}) collective-permute-start(bf16[24,3584]{1,0:T(8,128)(2,1)S(1)} %maximum_maximum_fusion.1.refs_1_), channel_id=1, source_target_pairs={{0,16},{1,17},{2,18},{3,19},{4,20},{5,21},{6,22},{7,23},{8,24},{9,... | collective-permute-start | bytes 516104 | tf_op jit(solution)/shard_map/ppermute | solution.py:178
  18.9 8.9 %collective-permute-start.14 = (bf16[24,3584]{1,0:T(8,128)(2,1)S(1)}, bf16[24,3584]{1,0:T(8,128)(2,1)S(1)}, u32[]{:S(2)}, u32[]{:S(2)}) collective-permute-start(bf16[24,3584]{1,0:T(8,128)(2,1)S(1)} %maximum_maximum_fusion.1.refs_1_), channel_id=1, source_target_pairs={{0,2},{1,3},{2,0},{3,1},{4,6},{5,7},{6,4},{7,5},{8,10},{9,11},{10,... | collective-permute-start | bytes 516104 | tf_op jit(solution)/shard_map/ppermute | solution.py:178
  20.6 4.6 %collective-permute-start.8 = (bf16[24,1792]{1,0:T(8,128)(2,1)S(1)}, bf16[24,1792]{1,0:T(8,128)(2,1)S(1)}, u32[]{:S(2)}, u32[]{:S(2)}) collective-permute-start(bf16[24,1792]{1,0:T(8,128)(2,1)S(1)} %collective-permute-done.4.refs_4_.refs_1_), channel_id=1, source_target_pairs={{0,1},{1,0},{2,3},{3,2},{4,5},{5,4},{6,7},{7,6},{8,9},{9,8},{10,11... | collective-permute-start | bytes 258056 | tf_op jit(solution)/shard_map/ppermute | solution.py:178
  20.6 4.6 %collective-permute-start.7 = (bf16[24,1792]{1,0:T(8,128)(2,1)S(1)}, bf16[24,1792]{1,0:T(8,128)(2,1)S(1)}, u32[]{:S(2)}, u32[]{:S(2)}) collective-permute-start(bf16[24,1792]{1,0:T(8,128)(2,1)S(1)} %collective-permute-done.3.refs_3_.refs_4_), channel_id=1, source_target_pairs={{0,1},{1,0},{2,3},{3,2},{4,5},{5,4},{6,7},{7,6},{8,9},{9,8},{10,11... | collective-permute-start | bytes 258056 | tf_op jit(solution)/shard_map/ppermute | solution.py:178
  21.1 4.1 %collective-permute-start.9 = (bf16[24,1792]{1,0:T(8,128)(2,1)S(1)}, bf16[24,1792]{1,0:T(8,128)(2,1)S(1)}, u32[]{:S(2)}, u32[]{:S(2)}) collective-permute-start(bf16[24,1792]{1,0:T(8,128)(2,1)S(1)} %collective-permute-done.5.refs_5_.refs_2_), channel_id=1, source_target_pairs={{0,1},{1,0},{2,3},{3,2},{4,5},{5,4},{6,7},{7,6},{8,9},{9,8},{10,11... | collective-permute-start | bytes 258056 | tf_op jit(solution)/shard_map/ppermute | solution.py:178
  23.5 5.4 %collective-permute-start.16 = (bf16[24,3584]{1,0:T(8,128)(2,1)S(1)}, bf16[24,3584]{1,0:T(8,128)(2,1)S(1)}, u32[]{:S(2)}, u32[]{:S(2)}) collective-permute-start(bf16[24,3584]{1,0:T(8,128)(2,1)S(1)} %collective-permute-done.15.refs_3_), channel_id=1, source_target_pairs={{0,2},{1,3},{2,0},{3,1},{4,6},{5,7},{6,4},{7,5},{8,10},{9,11},{10,... | collective-permute-start | bytes 516104 | tf_op jit(solution)/shard_map/ppermute | solution.py:178
  25.8 5.7 %collective-permute-start.10 = (bf16[192,512]{1,0:T(8,128)(2,1)S(1)}, bf16[192,512]{1,0:T(8,128)(2,1)S(1)}, u32[]{:S(2)}, u32[]{:S(2)}) collective-permute-start(bf16[192,512]{1,0:T(8,128)(2,1)S(1)} %shard_map.66), channel_id=1, source_target_pairs={{0,16},{1,17},{2,18},{3,19},{4,20},{5,21},{6,22},{7,23},{8,24},{9,... | collective-permute-start | bytes 589832 | tf_op jit(solution)/shard_map/ppermute | solution.py:178
  27.3 2.2 %collective-permute-start.17 = (bf16[24,3584]{1,0:T(8,128)(2,1)S(1)}, bf16[24,3584]{1,0:T(8,128)(2,1)S(1)}, u32[]{:S(2)}, u32[]{:S(2)}) collective-permute-start(bf16[24,3584]{1,0:T(8,128)(2,1)S(1)} %maximum_maximum_fusion.1.refs_1_), channel_id=1, source_target_pairs={{0,1},{1,0},{2,3},{3,2},{4,5},{5,4},{6,7},{7,6},{8,9},{9,8},{10,11... | collective-permute-start | bytes 516104 | tf_op jit(solution)/shard_map/ppermute | solution.py:178
  27.3 4.2 %collective-permute-start.19 = (bf16[24,3584]{1,0:T(8,128)(2,1)S(1)}, bf16[24,3584]{1,0:T(8,128)(2,1)S(1)}, u32[]{:S(2)}, u32[]{:S(2)}) collective-permute-start(bf16[24,3584]{1,0:T(8,128)(2,1)S(1)} %collective-permute-done.15.refs_3_), channel_id=1, source_target_pairs={{0,1},{1,0},{2,3},{3,2},{4,5},{5,4},{6,7},{7,6},{8,9},{9,8},{10,11... | collective-permute-start | bytes 516104 | tf_op jit(solution)/shard_map/ppermute | solution.py:178
  27.8 3.7 %collective-permute-start.18 = (bf16[24,3584]{1,0:T(8,128)(2,1)S(1)}, bf16[24,3584]{1,0:T(8,128)(2,1)S(1)}, u32[]{:S(2)}, u32[]{:S(2)}) collective-permute-start(bf16[24,3584]{1,0:T(8,128)(2,1)S(1)} %collective-permute-done.14.refs_2_), channel_id=1, source_target_pairs={{0,1},{1,0},{2,3},{3,2},{4,5},{5,4},{6,7},{7,6},{8,9},{9,8},{10,11... | collective-permute-start | bytes 516104 | tf_op jit(solution)/shard_map/ppermute | solution.py:178
  28.9 2.6 %collective-permute-start.20 = (bf16[24,3584]{1,0:T(8,128)(2,1)S(1)}, bf16[24,3584]{1,0:T(8,128)(2,1)S(1)}, u32[]{:S(2)}, u32[]{:S(2)}) collective-permute-start(bf16[24,3584]{1,0:T(8,128)(2,1)S(1)} %collective-permute-done.16.refs_4_), channel_id=1, source_target_pairs={{0,1},{1,0},{2,3},{3,2},{4,5},{5,4},{6,7},{7,6},{8,9},{9,8},{10,11... | collective-permute-start | bytes 516104 | tf_op jit(solution)/shard_map/ppermute | solution.py:178

commit v6 on v4

--- a/solution.py
+++ b/solution.py
@@ -224,6 +224,9 @@
         own = [blocks[by_d, by_q] for by_d in range(n_dp) for by_q in (0, 2)]
         return [own, [send(block, 0, 0, 1) for block in own]]
 
+    for by_d in range(1, n_dp):
+        for by_q in (0, 2):
+            x_blocks[by_d, by_q] = after(x_blocks[by_d, by_q], x_blocks[0, 2])
     x_lists, dy_lists = both_cores(x_blocks), both_cores(dy_blocks)
 
     def x_rows(by_d):

time: 33.2 us -> 33.2 us (level)
  no operation moved by 1% of the time
where the time goes in v6:
time: 33.2 us; the launch traced here: 33 us
  starting transfers between devices  20.6 us (62%)
  waiting for transfers between devices  7.02 us (21%)
  Pallas kernels  4.64 us (14%)
    ppermute x21, starting transfers between devices, send(): return lax.ppermute(value, AXES, pairs)  20.6 us
    ppermute x21, waiting for transfers between devices, send(): return lax.ppermute(value, AXES, pairs)  7.02 us
    pallas_call x1, Pallas kernels, pack(): pl.pallas_call(functools.partial(pack_kernel, cap, experts), out_shape=[m...  1.99 us
    pallas_call x1, Pallas kernels, finish(): pl.pallas_call(functools.partial(finish_kernel, len(arrived), len(dy_bloc...  1.61 us
    pallas_call x2, Pallas kernels, project(): pl.pallas_call(functools.partial(project_kernel, len(weights)), out_shape...  1.04 us
  transfers between devices with their start and end apart: 21, of which 7 were waited for; matrix products, arithmetic and copies ran while one was open for 2% of the time, Pallas kernels for 3%

profile of v6, /device:TPU:0, one launch (start us, length us, event | category | flops | bytes accessed | tf_op | source)
XLA Modules:
  0.0 33.0 jit_solution(16026505401318669242)
XLA Ops:
  0.0 2.0 %shard_map.64 = (bf16[24,896]{1,0:T(8,128)(2,1)S(1)}, bf16[24,896]{1,0:T(8,128)(2,1)S(1)}, bf16[24,896]{1,0:T(8,128)(2,1)S(1)}, bf16[24,896]{1,0:T(8,128)(2,1)S(...) custom-call(s32[1]{0:T(128)} %bitcast.1.me_ref, ...), custom_call_target="tpu_custom_call" | custom-call | tf_op jit(solution)/shard_map/pallas_call | solution.py:75
  2.0 5.1 %collective-permute-start.2 = (bf16[24,896]{1,0:T(8,128)(2,1)S(1)}, bf16[24,896]{1,0:T(8,128)(2,1)S(1)}, u32[]{:S(2)}, u32[]{:S(2)}) collective-permute-start(bf16[24,896]{1,0:T(8,128)(2,1)S(1)} %get-tuple-element.21), channel_id=1, source_target_pairs={{0,12},{1,13},{2,14},{3,15},{4,8},{5,9},{6,10},{7,11},{8,4},{9,5},... | collective-permute-start | bytes 129032 | tf_op jit(solution)/shard_map/ppermute | solution.py:176
  7.1 0.6 %collective-permute-start = (bf16[24,896]{1,0:T(8,128)(2,1)S(1)}, bf16[24,896]{1,0:T(8,128)(2,1)S(1)}, u32[]{:S(2)}, u32[]{:S(2)}) collective-permute-start(bf16[24,896]{1,0:T(8,128)(2,1)S(1)} %get-tuple-element.19), channel_id=1, source_target_pairs={{0,4},{1,5},{2,6},{3,7},{4,0},{5,1},{6,2},{7,3},{8,12},{9,13},{10,... | collective-permute-start | bytes 129032 | tf_op jit(solution)/shard_map/ppermute | solution.py:176
  7.8 3.7 %collective-permute-start.13 = (bf16[24,896]{1,0:T(8,128)(2,1)S(1)}, bf16[24,896]{1,0:T(8,128)(2,1)S(1)}, u32[]{:S(2)}, u32[]{:S(2)}) collective-permute-start(bf16[24,896]{1,0:T(8,128)(2,1)S(1)} %get-tuple-element.29), channel_id=1, source_target_pairs={{0,12},{1,13},{2,14},{3,15},{4,8},{5,9},{6,10},{7,11},{8,4},{9,5},... | collective-permute-start | bytes 129032 | tf_op jit(solution)/shard_map/ppermute | solution.py:176
  11.5 0.0 collective-permute-start.12
  11.6 0.0 copy-start.1
  11.6 0.7 %collective-permute-start.11 = (bf16[24,896]{1,0:T(8,128)(2,1)S(1)}, bf16[24,896]{1,0:T(8,128)(2,1)S(1)}, u32[]{:S(2)}, u32[]{:S(2)}) collective-permute-start(bf16[24,896]{1,0:T(8,128)(2,1)S(1)} %get-tuple-element.27), channel_id=1, source_target_pairs={{0,4},{1,5},{2,6},{3,7},{4,0},{5,1},{6,2},{7,3},{8,12},{9,13},{10,... | collective-permute-start | bytes 129032 | tf_op jit(solution)/shard_map/ppermute | solution.py:176
  12.3 0.2 collective-permute-done.1
  12.6 0.1 maximum_maximum_fusion
  12.7 1.6 %collective-permute-start.4 = (bf16[24,1792]{1,0:T(8,128)(2,1)S(1)}, bf16[24,1792]{1,0:T(8,128)(2,1)S(1)}, u32[]{:S(2)}, u32[]{:S(2)}) collective-permute-start(bf16[24,1792]{1,0:T(8,128)(2,1)S(1)} %get-tuple-element.31), channel_id=1, source_target_pairs={{0,16},{1,17},{2,18},{3,19},{4,20},{5,21},{6,22},{7,23},{8,24},{9,... | collective-permute-start | bytes 258056 | tf_op jit(solution)/shard_map/ppermute | solution.py:176
  14.2 1.5 %collective-permute-start.5 = (bf16[24,1792]{1,0:T(8,128)(2,1)S(1)}, bf16[24,1792]{1,0:T(8,128)(2,1)S(1)}, u32[]{:S(2)}, u32[]{:S(2)}) collective-permute-start(bf16[24,1792]{1,0:T(8,128)(2,1)S(1)} %get-tuple-element.31), channel_id=1, source_target_pairs={{0,18},{1,19},{2,16},{3,17},{4,22},{5,23},{6,20},{7,21},{8,26},{9,... | collective-permute-start | bytes 258056 | tf_op jit(solution)/shard_map/ppermute | solution.py:176
  15.7 0.5 %collective-permute-start.3 = (bf16[24,1792]{1,0:T(8,128)(2,1)S(1)}, bf16[24,1792]{1,0:T(8,128)(2,1)S(1)}, u32[]{:S(2)}, u32[]{:S(2)}) collective-permute-start(bf16[24,1792]{1,0:T(8,128)(2,1)S(1)} %get-tuple-element.32.refs_2_.refs_3_), channel_id=1, source_target_pairs={{0,2},{1,3},{2,0},{3,1},{4,6},{5,7},{6,4},{7,5},{8,10},{9,11},{10,... | collective-permute-start | bytes 258056 | tf_op jit(solution)/shard_map/ppermute | solution.py:176
  16.3 0.2 collective-permute-done.12
  16.5 0.1 maximum_maximum_fusion.1.refs_1_
  16.6 1.0 %collective-permute-done.4.refs_4_.refs_1_ = bf16[24,1792]{1,0:T(8,128)(2,1)S(1)} collective-permute-done((bf16[24,1792]{1,0:T(8,128)(2,1)S(1)}, bf16[24,1792]{1,0:T(8,128)(2,1)S(1)}, u32[]{:S(2)}, u32[]{:S(2)}) %collective-permute-start.4) | collective-permute-done | bytes 86048 | tf_op jit(solution)/shard_map/ppermute | solution.py:176
  17.6 1.1 %collective-permute-start.15 = (bf16[24,3584]{1,0:T(8,128)(2,1)S(1)}, bf16[24,3584]{1,0:T(8,128)(2,1)S(1)}, u32[]{:S(2)}, u32[]{:S(2)}) collective-permute-start(bf16[24,3584]{1,0:T(8,128)(2,1)S(1)} %maximum_maximum_fusion.1.refs_1_), channel_id=1, source_target_pairs={{0,16},{1,17},{2,18},{3,19},{4,20},{5,21},{6,22},{7,23},{8,24},{9,... | collective-permute-start | bytes 516104 | tf_op jit(solution)/shard_map/ppermute | solution.py:176
  18.7 0.1 constant_dynamic-slice_fusion
  18.8 1.6 %collective-permute-start.14 = (bf16[24,3584]{1,0:T(8,128)(2,1)S(1)}, bf16[24,3584]{1,0:T(8,128)(2,1)S(1)}, u32[]{:S(2)}, u32[]{:S(2)}) collective-permute-start(bf16[24,3584]{1,0:T(8,128)(2,1)S(1)} %maximum_maximum_fusion.1.refs_1_), channel_id=1, source_target_pairs={{0,2},{1,3},{2,0},{3,1},{4,6},{5,7},{6,4},{7,5},{8,10},{9,11},{10,... | collective-permute-start | bytes 516104 | tf_op jit(solution)/shard_map/ppermute | solution.py:176
  20.4 0.1 collective-permute-done.3.refs_3_.refs_4_
  20.5 0.5 %collective-permute-start.9 = (bf16[24,1792]{1,0:T(8,128)(2,1)S(1)}, bf16[24,1792]{1,0:T(8,128)(2,1)S(1)}, u32[]{:S(2)}, u32[]{:S(2)}) collective-permute-start(bf16[24,1792]{1,0:T(8,128)(2,1)S(1)} %collective-permute-done.5.refs_5_.refs_2_), channel_id=1, source_target_pairs={{0,1},{1,0},{2,3},{3,2},{4,5},{5,4},{6,7},{7,6},{8,9},{9,8},{10,11... | collective-permute-start | bytes 258056 | tf_op jit(solution)/shard_map/ppermute | solution.py:176
  21.1 0.0 collective-permute-start.7
  21.1 2.4 %collective-permute-done.15.refs_3_ = bf16[24,3584]{1,0:T(8,128)(2,1)S(1)} collective-permute-done((bf16[24,3584]{1,0:T(8,128)(2,1)S(1)}, bf16[24,3584]{1,0:T(8,128)(2,1)S(1)}, u32[]{:S(2)}, u32[]{:S(2)}) %collective-permute-start.15) | collective-permute-done | bytes 172064 | tf_op jit(solution)/shard_map/ppermute | solution.py:176
  23.4 1.5 %collective-permute-start.16 = (bf16[24,3584]{1,0:T(8,128)(2,1)S(1)}, bf16[24,3584]{1,0:T(8,128)(2,1)S(1)}, u32[]{:S(2)}, u32[]{:S(2)}) collective-permute-start(bf16[24,3584]{1,0:T(8,128)(2,1)S(1)} %collective-permute-done.15.refs_3_), channel_id=1, source_target_pairs={{0,2},{1,3},{2,0},{3,1},{4,6},{5,7},{6,4},{7,5},{8,10},{9,11},{10,... | collective-permute-start | bytes 516104 | tf_op jit(solution)/shard_map/ppermute | solution.py:176
  25.0 0.1 pad_maximum_fusion.refs_0_
  25.1 0.5 %shard_map.66 = bf16[192,512]{1,0:T(8,128)(2,1)S(1)} custom-call(s32[1]{0:T(128)} %bitcast.at_ref, bf16[1792,512]{1,0:T(8,128)(2,1)S(1)} %pad_maximum_fusion.refs_0_, bf16[24,1792]{1,0:T(8,128)(2,1)S(1)} %collective-permute-done.4.refs_4_.refs_1_, bf16[24,1792]{1,0:T(8,128)(2,1)S(1)} %collective-permute-done.5.refs_5_.refs_2_, ...), custom_call_target="tpu_custom_call" | custom-call | flops 352321536 | bytes 2523136 | tf_op jit(solution)/shard_map/pallas_call | solution.py:105
  25.7 1.6 %collective-permute-start.10 = (bf16[192,512]{1,0:T(8,128)(2,1)S(1)}, bf16[192,512]{1,0:T(8,128)(2,1)S(1)}, u32[]{:S(2)}, u32[]{:S(2)}) collective-permute-start(bf16[192,512]{1,0:T(8,128)(2,1)S(1)} %shard_map.66), channel_id=1, source_target_pairs={{0,16},{1,17},{2,18},{3,19},{4,20},{5,21},{6,22},{7,23},{8,24},{9,... | collective-permute-start | bytes 589832 | tf_op jit(solution)/shard_map/ppermute | solution.py:176
  27.2 0.5 %collective-permute-start.19 = (bf16[24,3584]{1,0:T(8,128)(2,1)S(1)}, bf16[24,3584]{1,0:T(8,128)(2,1)S(1)}, u32[]{:S(2)}, u32[]{:S(2)}) collective-permute-start(bf16[24,3584]{1,0:T(8,128)(2,1)S(1)} %collective-permute-done.15.refs_3_), channel_id=1, source_target_pairs={{0,1},{1,0},{2,3},{3,2},{4,5},{5,4},{6,7},{7,6},{8,9},{9,8},{10,11... | collective-permute-start | bytes 516104 | tf_op jit(solution)/shard_map/ppermute | solution.py:176
  27.7 0.0 collective-permute-start.18
  27.7 1.1 %collective-permute-done.16.refs_4_ = bf16[24,3584]{1,0:T(8,128)(2,1)S(1)} collective-permute-done((bf16[24,3584]{1,0:T(8,128)(2,1)S(1)}, bf16[24,3584]{1,0:T(8,128)(2,1)S(1)}, u32[]{:S(2)}, u32[]{:S(2)}) %collective-permute-start.16) | collective-permute-done | bytes 172064 | tf_op jit(solution)/shard_map/ppermute | solution.py:176
  28.9 0.5 %shard_map.65.keep_ref = f32[192,512]{1,0:T(8,128)S(1)} custom-call(s32[1]{0:T(128)} %bitcast.at_ref, bf16[1792,512]{1,0:T(8,128)(2,1)S(1)} %copy-done, bf16[1792,512]{1,0:T(8,128)(2,1)S(1)} %copy-done.1, bf16[24,1792]{1,0:T(8,128)(2,1)S(1)} %get-tuple-element.32.refs_2_.refs_3_, bf16[24,1792]{1,0:T(8,128)(2,1)S(1)} %collective-permute-done.3.refs_3_.refs_4_, ...), custom_call_target="tpu_custom_call" | custom-call | flops 352321536 | bytes 2523136 | tf_op jit(solution)/shard_map/pallas_call | solution.py:105
  29.4 2.0 %collective-permute-done.10.refs_0_ = bf16[192,512]{1,0:T(8,128)(2,1)S(1)} collective-permute-done((bf16[192,512]{1,0:T(8,128)(2,1)S(1)}, bf16[192,512]{1,0:T(8,128)(2,1)S(1)}, u32[]{:S(2)}, u32[]{:S(2)}) %collective-permute-start.10) | collective-permute-done | bytes 196640 | tf_op jit(solution)/shard_map/ppermute | solution.py:176
  31.4 1.6 %shard_map.67 = bf16[256,3584]{1,0:T(8,128)(2,1)} custom-call(f32[192,512]{1,0:T(8,128)S(1)} %shard_map.65.keep_ref, bf16[192,512]{1,0:T(8,128)(2,1)S(1)} %collective-permute-done.10.refs_0_, bf16[24,3584]{1,0:T(8,128)(2,1)S(1)} %maximum_maximum_fusion.1.refs_1_, bf16[24,3584]{1,0:T(8,128)(2,1)S(1)} %collective-permute-done.14.refs_2_, ...), custom_call_target="tpu_custom_call" | custom-call | tf_op jit(solution)/shard_map/pallas_call | solution.py:146
  (30 shorter events, 0.2 us)
Async XLA Ops:
  0.0 18.7 %copy-start = (bf16[1792,512]{1,0:T(8,128)(2,1)S(1)}, bf16[1792,512]{1,0:T(8,128)(2,1)}, u32[]{:S(2)}) copy-start(bf16[1792,512]{1,0:T(8,128)(2,1)} %refs_0_.1) | copy-start | bytes 5505028
  2.0 9.6 %collective-permute-start.2 = (bf16[24,896]{1,0:T(8,128)(2,1)S(1)}, bf16[24,896]{1,0:T(8,128)(2,1)S(1)}, u32[]{:S(2)}, u32[]{:S(2)}) collective-permute-start(bf16[24,896]{1,0:T(8,128)(2,1)S(1)} %get-tuple-element.21), channel_id=1, source_target_pairs={{0,12},{1,13},{2,14},{3,15},{4,8},{5,9},{6,10},{7,11},{8,4},{9,5},... | collective-permute-start | bytes 129032 | tf_op jit(solution)/shard_map/ppermute | solution.py:176
  7.1 5.4 %collective-permute-start.1 = (bf16[24,896]{1,0:T(8,128)(2,1)S(1)}, bf16[24,896]{1,0:T(8,128)(2,1)S(1)}, u32[]{:S(2)}, u32[]{:S(2)}) collective-permute-start(bf16[24,896]{1,0:T(8,128)(2,1)S(1)} %get-tuple-element.20), channel_id=1, source_target_pairs={{0,8},{1,9},{2,10},{3,11},{4,12},{5,13},{6,14},{7,15},{8,0},{9,1},... | collective-permute-start | bytes 129032 | tf_op jit(solution)/shard_map/ppermute | solution.py:176
  7.1 5.4 %collective-permute-start = (bf16[24,896]{1,0:T(8,128)(2,1)S(1)}, bf16[24,896]{1,0:T(8,128)(2,1)S(1)}, u32[]{:S(2)}, u32[]{:S(2)}) collective-permute-start(bf16[24,896]{1,0:T(8,128)(2,1)S(1)} %get-tuple-element.19), channel_id=1, source_target_pairs={{0,4},{1,5},{2,6},{3,7},{4,0},{5,1},{6,2},{7,3},{8,12},{9,13},{10,... | collective-permute-start | bytes 129032 | tf_op jit(solution)/shard_map/ppermute | solution.py:176
  7.8 8.0 %collective-permute-start.13 = (bf16[24,896]{1,0:T(8,128)(2,1)S(1)}, bf16[24,896]{1,0:T(8,128)(2,1)S(1)}, u32[]{:S(2)}, u32[]{:S(2)}) collective-permute-start(bf16[24,896]{1,0:T(8,128)(2,1)S(1)} %get-tuple-element.29), channel_id=1, source_target_pairs={{0,12},{1,13},{2,14},{3,15},{4,8},{5,9},{6,10},{7,11},{8,4},{9,5},... | collective-permute-start | bytes 129032 | tf_op jit(solution)/shard_map/ppermute | solution.py:176
  11.5 4.9 %collective-permute-start.12 = (bf16[24,896]{1,0:T(8,128)(2,1)S(1)}, bf16[24,896]{1,0:T(8,128)(2,1)S(1)}, u32[]{:S(2)}, u32[]{:S(2)}) collective-permute-start(bf16[24,896]{1,0:T(8,128)(2,1)S(1)} %get-tuple-element.28), channel_id=1, source_target_pairs={{0,8},{1,9},{2,10},{3,11},{4,12},{5,13},{6,14},{7,15},{8,0},{9,1},... | collective-permute-start | bytes 129032 | tf_op jit(solution)/shard_map/ppermute | solution.py:176
  11.6 7.2 %copy-start.1 = (bf16[1792,512]{1,0:T(8,128)(2,1)S(1)}, bf16[1792,512]{1,0:T(8,128)(2,1)}, u32[]{:S(2)}) copy-start(bf16[1792,512]{1,0:T(8,128)(2,1)} %refs_1_.1) | copy-start | bytes 5505028
  11.6 4.9 %collective-permute-start.11 = (bf16[24,896]{1,0:T(8,128)(2,1)S(1)}, bf16[24,896]{1,0:T(8,128)(2,1)S(1)}, u32[]{:S(2)}, u32[]{:S(2)}) collective-permute-start(bf16[24,896]{1,0:T(8,128)(2,1)S(1)} %get-tuple-element.27), channel_id=1, source_target_pairs={{0,4},{1,5},{2,6},{3,7},{4,0},{5,1},{6,2},{7,3},{8,12},{9,13},{10,... | collective-permute-start | bytes 129032 | tf_op jit(solution)/shard_map/ppermute | solution.py:176
  12.7 4.9 %collective-permute-start.4 = (bf16[24,1792]{1,0:T(8,128)(2,1)S(1)}, bf16[24,1792]{1,0:T(8,128)(2,1)S(1)}, u32[]{:S(2)}, u32[]{:S(2)}) collective-permute-start(bf16[24,1792]{1,0:T(8,128)(2,1)S(1)} %get-tuple-element.31), channel_id=1, source_target_pairs={{0,16},{1,17},{2,18},{3,19},{4,20},{5,21},{6,22},{7,23},{8,24},{9,... | collective-permute-start | bytes 258056 | tf_op jit(solution)/shard_map/ppermute | solution.py:176
  14.2 6.3 %collective-permute-start.5 = (bf16[24,1792]{1,0:T(8,128)(2,1)S(1)}, bf16[24,1792]{1,0:T(8,128)(2,1)S(1)}, u32[]{:S(2)}, u32[]{:S(2)}) collective-permute-start(bf16[24,1792]{1,0:T(8,128)(2,1)S(1)} %get-tuple-element.31), channel_id=1, source_target_pairs={{0,18},{1,19},{2,16},{3,17},{4,22},{5,23},{6,20},{7,21},{8,26},{9,... | collective-permute-start | bytes 258056 | tf_op jit(solution)/shard_map/ppermute | solution.py:176
  15.7 4.8 %collective-permute-start.3 = (bf16[24,1792]{1,0:T(8,128)(2,1)S(1)}, bf16[24,1792]{1,0:T(8,128)(2,1)S(1)}, u32[]{:S(2)}, u32[]{:S(2)}) collective-permute-start(bf16[24,1792]{1,0:T(8,128)(2,1)S(1)} %get-tuple-element.32.refs_2_.refs_3_), channel_id=1, source_target_pairs={{0,2},{1,3},{2,0},{3,1},{4,6},{5,7},{6,4},{7,5},{8,10},{9,11},{10,... | collective-permute-start | bytes 258056 | tf_op jit(solution)/shard_map/ppermute | solution.py:176
  16.4 4.6 %collective-permute-start.6 = (bf16[24,1792]{1,0:T(8,128)(2,1)S(1)}, bf16[24,1792]{1,0:T(8,128)(2,1)S(1)}, u32[]{:S(2)}, u32[]{:S(2)}) collective-permute-start(bf16[24,1792]{1,0:T(8,128)(2,1)S(1)} %get-tuple-element.32.refs_2_.refs_3_), channel_id=1, source_target_pairs={{0,1},{1,0},{2,3},{3,2},{4,5},{5,4},{6,7},{7,6},{8,9},{9,8},{10,11... | collective-permute-start | bytes 258056 | tf_op jit(solution)/shard_map/ppermute | solution.py:176
  17.6 5.8 %collective-permute-start.15 = (bf16[24,3584]{1,0:T(8,128)(2,1)S(1)}, bf16[24,3584]{1,0:T(8,128)(2,1)S(1)}, u32[]{:S(2)}, u32[]{:S(2)}) collective-permute-start(bf16[24,3584]{1,0:T(8,128)(2,1)S(1)} %maximum_maximum_fusion.1.refs_1_), channel_id=1, source_target_pairs={{0,16},{1,17},{2,18},{3,19},{4,20},{5,21},{6,22},{7,23},{8,24},{9,... | collective-permute-start | bytes 516104 | tf_op jit(solution)/shard_map/ppermute | solution.py:176
  18.8 8.9 %collective-permute-start.14 = (bf16[24,3584]{1,0:T(8,128)(2,1)S(1)}, bf16[24,3584]{1,0:T(8,128)(2,1)S(1)}, u32[]{:S(2)}, u32[]{:S(2)}) collective-permute-start(bf16[24,3584]{1,0:T(8,128)(2,1)S(1)} %maximum_maximum_fusion.1.refs_1_), channel_id=1, source_target_pairs={{0,2},{1,3},{2,0},{3,1},{4,6},{5,7},{6,4},{7,5},{8,10},{9,11},{10,... | collective-permute-start | bytes 516104 | tf_op jit(solution)/shard_map/ppermute | solution.py:176
  20.5 4.6 %collective-permute-start.8 = (bf16[24,1792]{1,0:T(8,128)(2,1)S(1)}, bf16[24,1792]{1,0:T(8,128)(2,1)S(1)}, u32[]{:S(2)}, u32[]{:S(2)}) collective-permute-start(bf16[24,1792]{1,0:T(8,128)(2,1)S(1)} %collective-permute-done.4.refs_4_.refs_1_), channel_id=1, source_target_pairs={{0,1},{1,0},{2,3},{3,2},{4,5},{5,4},{6,7},{7,6},{8,9},{9,8},{10,11... | collective-permute-start | bytes 258056 | tf_op jit(solution)/shard_map/ppermute | solution.py:176
  20.5 4.6 %collective-permute-start.9 = (bf16[24,1792]{1,0:T(8,128)(2,1)S(1)}, bf16[24,1792]{1,0:T(8,128)(2,1)S(1)}, u32[]{:S(2)}, u32[]{:S(2)}) collective-permute-start(bf16[24,1792]{1,0:T(8,128)(2,1)S(1)} %collective-permute-done.5.refs_5_.refs_2_), channel_id=1, source_target_pairs={{0,1},{1,0},{2,3},{3,2},{4,5},{5,4},{6,7},{7,6},{8,9},{9,8},{10,11... | collective-permute-start | bytes 258056 | tf_op jit(solution)/shard_map/ppermute | solution.py:176
  21.1 4.1 %collective-permute-start.7 = (bf16[24,1792]{1,0:T(8,128)(2,1)S(1)}, bf16[24,1792]{1,0:T(8,128)(2,1)S(1)}, u32[]{:S(2)}, u32[]{:S(2)}) collective-permute-start(bf16[24,1792]{1,0:T(8,128)(2,1)S(1)} %collective-permute-done.3.refs_3_.refs_4_), channel_id=1, source_target_pairs={{0,1},{1,0},{2,3},{3,2},{4,5},{5,4},{6,7},{7,6},{8,9},{9,8},{10,11... | collective-permute-start | bytes 258056 | tf_op jit(solution)/shard_map/ppermute | solution.py:176
  23.4 5.4 %collective-permute-start.16 = (bf16[24,3584]{1,0:T(8,128)(2,1)S(1)}, bf16[24,3584]{1,0:T(8,128)(2,1)S(1)}, u32[]{:S(2)}, u32[]{:S(2)}) collective-permute-start(bf16[24,3584]{1,0:T(8,128)(2,1)S(1)} %collective-permute-done.15.refs_3_), channel_id=1, source_target_pairs={{0,2},{1,3},{2,0},{3,1},{4,6},{5,7},{6,4},{7,5},{8,10},{9,11},{10,... | collective-permute-start | bytes 516104 | tf_op jit(solution)/shard_map/ppermute | solution.py:176
  25.7 5.7 %collective-permute-start.10 = (bf16[192,512]{1,0:T(8,128)(2,1)S(1)}, bf16[192,512]{1,0:T(8,128)(2,1)S(1)}, u32[]{:S(2)}, u32[]{:S(2)}) collective-permute-start(bf16[192,512]{1,0:T(8,128)(2,1)S(1)} %shard_map.66), channel_id=1, source_target_pairs={{0,16},{1,17},{2,18},{3,19},{4,20},{5,21},{6,22},{7,23},{8,24},{9,... | collective-permute-start | bytes 589832 | tf_op jit(solution)/shard_map/ppermute | solution.py:176
  27.2 2.2 %collective-permute-start.17 = (bf16[24,3584]{1,0:T(8,128)(2,1)S(1)}, bf16[24,3584]{1,0:T(8,128)(2,1)S(1)}, u32[]{:S(2)}, u32[]{:S(2)}) collective-permute-start(bf16[24,3584]{1,0:T(8,128)(2,1)S(1)} %maximum_maximum_fusion.1.refs_1_), channel_id=1, source_target_pairs={{0,1},{1,0},{2,3},{3,2},{4,5},{5,4},{6,7},{7,6},{8,9},{9,8},{10,11... | collective-permute-start | bytes 516104 | tf_op jit(solution)/shard_map/ppermute | solution.py:176
  27.2 4.2 %collective-permute-start.19 = (bf16[24,3584]{1,0:T(8,128)(2,1)S(1)}, bf16[24,3584]{1,0:T(8,128)(2,1)S(1)}, u32[]{:S(2)}, u32[]{:S(2)}) collective-permute-start(bf16[24,3584]{1,0:T(8,128)(2,1)S(1)} %collective-permute-done.15.refs_3_), channel_id=1, source_target_pairs={{0,1},{1,0},{2,3},{3,2},{4,5},{5,4},{6,7},{7,6},{8,9},{9,8},{10,11... | collective-permute-start | bytes 516104 | tf_op jit(solution)/shard_map/ppermute | solution.py:176
  27.7 3.7 %collective-permute-start.18 = (bf16[24,3584]{1,0:T(8,128)(2,1)S(1)}, bf16[24,3584]{1,0:T(8,128)(2,1)S(1)}, u32[]{:S(2)}, u32[]{:S(2)}) collective-permute-start(bf16[24,3584]{1,0:T(8,128)(2,1)S(1)} %collective-permute-done.14.refs_2_), channel_id=1, source_target_pairs={{0,1},{1,0},{2,3},{3,2},{4,5},{5,4},{6,7},{7,6},{8,9},{9,8},{10,11... | collective-permute-start | bytes 516104 | tf_op jit(solution)/shard_map/ppermute | solution.py:176
  28.9 2.6 %collective-permute-start.20 = (bf16[24,3584]{1,0:T(8,128)(2,1)S(1)}, bf16[24,3584]{1,0:T(8,128)(2,1)S(1)}, u32[]{:S(2)}, u32[]{:S(2)}) collective-permute-start(bf16[24,3584]{1,0:T(8,128)(2,1)S(1)} %collective-permute-done.16.refs_4_), channel_id=1, source_target_pairs={{0,1},{1,0},{2,3},{3,2},{4,5},{5,4},{6,7},{7,6},{8,9},{9,8},{10,11... | collective-permute-start | bytes 516104 | tf_op jit(solution)/shard_map/ppermute | solution.py:176
